TPU v7x, 256 devices: a whole 4x4x8 slice. The times are simulated.
256 devices in a mesh: seq: 32 (over z, y), chan: 8 (over x, core).
Axes of the slice: x: 4, y: 4, z: 8, core: 2. Of those that a mesh axis runs over, the one named last changes fastest.
Arguments:
- query: bfloat16 [16384, 4096], P('seq', 'chan'), may hold values from -6 to 6
- key_stream: bfloat16 [16384, 4096], P('seq', 'chan'), may hold values from -6 to 6
- value: bfloat16 [16384, 4096], P('seq', 'chan'), may hold values from -6 to 6
- long_filter: float32 [16384, 4096], P('seq', 'chan'), may hold values from -0.046875 to 0.046875
- w_out: bfloat16 [4096, 4096], P('chan'), may hold values from -0.125 to 0.125
Outputs:
- mixed: bfloat16 [16384, 4096], P('seq', 'chan')
All inputs are finite; a program needn't handle non-finite values.
Results may differ from a plain program's by a relative error of at most 0.005.
Values sent between devices are 32-bit elements; how exact they have to be, the bound alone decides.
No kernel may reach another device: no remote copies, remote signals or barrier semaphores. Data moves between devices by JAX's collectives and lax.ppermute only.
A program may use at most 128 MiB of HBM per device.

v0:
```python
import math

import jax
import jax.numpy as jnp
from jax import lax
from jax.sharding import PartitionSpec as P

highest = lax.Precision.HIGHEST


def phase_table(rows, cols, modulus):
    product = rows[:, None] * cols[None, :] % modulus
    angle = product.astype(jnp.float32) * (2.0 * math.pi / modulus)
    return (jnp.cos(angle), jnp.sin(angle))


def contract(spec, cosine, sine, real_part, imag_part, sign):
    out_real = jnp.einsum(spec, cosine, real_part, precision=highest)
    out_imag = sign * jnp.einsum(spec, sine, real_part, precision=highest)
    if imag_part is not None:
        out_real = out_real - sign * jnp.einsum(spec, sine, imag_part, precision=highest)
        out_imag = out_imag + jnp.einsum(spec, cosine, imag_part, precision=highest)
    return (out_real, out_imag)


def rotate(real_part, imag_part, cosine, sine, sign):
    return (
        real_part * cosine - sign * imag_part * sine,
        imag_part * cosine + sign * real_part * sine,
    )


def split_sequence(signal, taps):
    spread = lax.axis_size("seq")
    own_index = lax.axis_index("seq")
    rows_dev, channels = signal.shape
    per_peer = rows_dev // spread
    padded = 2 * spread * rows_dev
    moved = (
        lax.all_to_all(signal, "seq", split_axis=0, concat_axis=0, tiled=True),
        lax.all_to_all(taps, "seq", split_axis=0, concat_axis=0, tiled=True),
    )
    kfirst = jnp.arange(2 * spread, dtype=jnp.int32)
    blocks_idx = jnp.arange(spread, dtype=jnp.int32)
    offsets = own_index * per_peer + jnp.arange(per_peer, dtype=jnp.int32)
    cos_outer, sin_outer = phase_table(kfirst, blocks_idx, 2 * spread)
    cos_twist, sin_twist = phase_table(kfirst, offsets, padded)
    partial_spectra = []
    for stream in moved:
        stacked = stream.reshape(spread, per_peer, channels)
        real_part, imag_part = contract("kp,ptc->ktc", cos_outer, sin_outer, stacked, None, -1.0)
        real_part, imag_part = rotate(
            real_part, imag_part, cos_twist[:, :, None], sin_twist[:, :, None], -1.0
        )
        partial_spectra.extend([real_part, imag_part])
    back = lax.all_to_all(tuple(partial_spectra), "seq", split_axis=0, concat_axis=1, tiled=True)
    all_rows = jnp.arange(rows_dev, dtype=jnp.int32)
    cos_inner, sin_inner = phase_table(all_rows, all_rows, rows_dev)
    sig_real, sig_imag = contract("st,etc->esc", cos_inner, sin_inner, back[0], back[1], -1.0)
    fil_real, fil_imag = contract("st,etc->esc", cos_inner, sin_inner, back[2], back[3], -1.0)
    prod_real = sig_real * fil_real - sig_imag * fil_imag
    prod_imag = sig_real * fil_imag + sig_imag * fil_real
    inv_real, inv_imag = contract("ts,esc->etc", cos_inner, sin_inner, prod_real, prod_imag, 1.0)
    kmine = 2 * own_index + jnp.arange(2, dtype=jnp.int32)
    cos_mine, sin_mine = phase_table(kmine, all_rows, padded)
    inv_real, inv_imag = rotate(inv_real, inv_imag, cos_mine[:, :, None], sin_mine[:, :, None], 1.0)
    turned = (
        lax.all_to_all(inv_real, "seq", split_axis=1, concat_axis=0, tiled=True),
        lax.all_to_all(inv_imag, "seq", split_axis=1, concat_axis=0, tiled=True),
    )
    cos_last, sin_last = phase_table(blocks_idx, kfirst, 2 * spread)
    result = jnp.einsum("pk,ktc->ptc", cos_last, turned[0], precision=highest)
    result = (result - jnp.einsum("pk,ktc->ptc", sin_last, turned[1], precision=highest)) / padded
    home = lax.all_to_all(result, "seq", split_axis=0, concat_axis=1, tiled=True)
    return home.reshape(rows_dev, channels)


def shards(query, key_stream, value, long_filter, w_out):
    signal = key_stream.astype(jnp.float32) * value.astype(jnp.float32)
    conv = split_sequence(signal, long_filter)
    gated = (query.astype(jnp.float32) * conv).astype(jnp.bfloat16)
    partial_sums = jnp.dot(gated, w_out, preferred_element_type=jnp.float32)
    return lax.psum_scatter(partial_sums, "chan", scatter_dimension=1, tiled=True).astype(
        jnp.bfloat16
    )


def solution(mesh):
    in_specs = (
        P("seq", "chan"),
        P("seq", "chan"),
        P("seq", "chan"),
        P("seq", "chan"),
        P("chan", None),
    )
    out_specs = P("seq", "chan")
    return jax.shard_map(shards, mesh=mesh, in_specs=in_specs, out_specs=out_specs, check_vma=False)
```

profile of v0, /device:TPU:8, one launch (start us, length us, event | category | flops | bytes accessed | tf_op | source)
XLA Modules:
  0.0 613.0 jit_solution(2524472311364982516)
XLA Ops:
  6.5 11.8 %all-to-all-start.3 = ((f32[32,16,512]{2,1,0:T(8,128)}), f32[32,16,512]{2,1,0:T(8,128)S(1)}, u32[]{:S(2)}, u32[]{:S(2)}) async-start(f32[32,16,512]{2,1,0:T(8,128)} %bitcast.123), calls=%async_computation.3 | async-start | bytes 2097152 | tf_op jit(solution)/shard_map/all_to_all | solution.py:41
  19.5 26.9 %all-to-all-done.3 = f32[32,16,512]{2,1,0:T(8,128)S(1)} async-done(((f32[32,16,512]{2,1,0:T(8,128)}), f32[32,16,512]{2,1,0:T(8,128)S(1)}, u32[]{:S(2)}, u32[]{:S(2)}) %all-to-all-start.3) | async-done | bytes 1048608 | tf_op jit(solution)/shard_map/all_to_all | solution.py:41
  46.4 5.6 all-to-all-start
  59.7 19.3 %all-to-all-done = f32[32,16,512]{2,1,0:T(8,128)S(1)} async-done(((f32[32,16,512]{2,1,0:T(8,128)}), f32[32,16,512]{2,1,0:T(8,128)S(1)}, u32[]{:S(2)}, u32[]{:S(2)}) %all-to-all-start) | async-done | bytes 1048608 | tf_op jit(solution)/shard_map/all_to_all | solution.py:40
  81.4 5.8 multiply_add_fusion.4
  89.8 6.2 %all-to-all-start.4 = ((f32[64,16,512]{2,1,0:T(8,128)}), f32[64,16,512]{2,1,0:T(8,128)}, u32[]{:S(2)}, u32[]{:S(2)}) async-start(f32[64,16,512]{2,1,0:T(8,128)} %copy.64), calls=%async_computation.4 | async-start | bytes 4194304 | tf_op jit(solution)/shard_map/all_to_all | solution.py:56
  98.5 46.3 %all-to-all-done.4 = f32[64,16,512]{2,1,0:T(8,128)} async-done(((f32[64,16,512]{2,1,0:T(8,128)}), f32[64,16,512]{2,1,0:T(8,128)}, u32[]{:S(2)}, u32[]{:S(2)}) %all-to-all-start.4) | async-done | bytes 2097184 | tf_op jit(solution)/shard_map/all_to_all | solution.py:56
  144.8 5.6 all-to-all-start.5
  153.0 44.8 %all-to-all-done.5 = f32[64,16,512]{2,1,0:T(8,128)} async-done(((f32[64,16,512]{2,1,0:T(8,128)}), f32[64,16,512]{2,1,0:T(8,128)}, u32[]{:S(2)}, u32[]{:S(2)}) %all-to-all-start.5) | async-done | bytes 2097184 | tf_op jit(solution)/shard_map/all_to_all | solution.py:56
  197.8 6.3 %all-to-all-start.1 = ((f32[64,16,512]{2,1,0:T(8,128)}), f32[64,16,512]{2,1,0:T(8,128)}, u32[]{:S(2)}, u32[]{:S(2)}) async-start(f32[64,16,512]{2,1,0:T(8,128)} %copy.56), calls=%async_computation.1 | async-start | bytes 4194304 | tf_op jit(solution)/shard_map/all_to_all | solution.py:56
  206.7 44.5 %all-to-all-done.1 = f32[64,16,512]{2,1,0:T(8,128)} async-done(((f32[64,16,512]{2,1,0:T(8,128)}), f32[64,16,512]{2,1,0:T(8,128)}, u32[]{:S(2)}, u32[]{:S(2)}) %all-to-all-start.1) | async-done | bytes 2097184 | tf_op jit(solution)/shard_map/all_to_all | solution.py:56
  251.2 6.3 %all-to-all-start.2 = ((f32[64,16,512]{2,1,0:T(8,128)}), f32[64,16,512]{2,1,0:T(8,128)S(1)}, u32[]{:S(2)}, u32[]{:S(2)}) async-start(f32[64,16,512]{2,1,0:T(8,128)} %copy.59), calls=%async_computation.2 | async-start | bytes 4194304 | tf_op jit(solution)/shard_map/all_to_all | solution.py:56
  264.6 11.5 %fusion.31 = f32[2,512,512]{2,1,0:T(8,128)} fusion(f32[2,512,512]{2,1,0:T(8,128)S(1)} %bitcast.119), kind=kOutput, calls=%fused_computation.44 | convolution fusion | flops 3224895488 | bytes 4194304 | tf_op jit(solution)/shard_map/st,etc->esc/dot_general | solution.py:18
  276.2 11.5 %fusion.21 = f32[2,512,512]{2,1,0:T(8,128)} fusion(f32[2,512,512]{2,1,0:T(8,128)S(1)} %bitcast.120), kind=kOutput, calls=%fused_computation.34 | convolution fusion | flops 3224895488 | bytes 4194304 | tf_op jit(solution)/shard_map/st,etc->esc/dot_general | solution.py:19
  287.7 11.8 %fusion.33 = f32[2,512,512]{2,1,0:T(8,128)} fusion(f32[2,512,512]{2,1,0:T(8,128)S(1)} %bitcast.121), kind=kOutput, calls=%fused_computation.46 | convolution fusion | flops 3224895488 | bytes 4194304 | tf_op jit(solution)/shard_map/st,etc->esc/dot_general | solution.py:18
  299.5 11.5 %fusion.23 = f32[2,512,512]{2,1,0:T(8,128)} fusion(f32[2,512,512]{2,1,0:T(8,128)S(1)} %bitcast.122), kind=kOutput, calls=%fused_computation.36 | convolution fusion | flops 3224895488 | bytes 4194304 | tf_op jit(solution)/shard_map/st,etc->esc/dot_general | solution.py:19
  313.2 11.4 %multiply_subtract_fusion.1 = f32[2,512,512]{2,1,0:T(8,128)S(1)} fusion(f32[2,512,512]{2,1,0:T(8,128)S(1)} %copy-done.11, f32[2,512,512]{2,1,0:T(8,128)S(1)} %bitcast.117), kind=kOutput, calls=%fused_computation.14 | convolution fusion | flops 3225944064 | bytes 6291456 | tf_op jit(solution)/shard_map/st,etc->esc/dot_general | solution.py:21
  324.7 11.2 %multiply_add_fusion.1 = f32[2,512,512]{2,1,0:T(8,128)S(1)} fusion(f32[2,512,512]{2,1,0:T(8,128)S(1)} %copy-done.9, f32[2,512,512]{2,1,0:T(8,128)S(1)} %bitcast.118), kind=kOutput, calls=%fused_computation.12 | convolution fusion | flops 3225944064 | bytes 6291456 | tf_op jit(solution)/shard_map/st,etc->esc/dot_general | solution.py:22
  335.9 11.6 %multiply_subtract_fusion.3 = f32[2,512,512]{2,1,0:T(8,128)S(1)} fusion(f32[2,512,512]{2,1,0:T(8,128)S(1)} %copy-done.10, f32[2,512,512]{2,1,0:T(8,128)S(1)} %bitcast.112), kind=kOutput, calls=%fused_computation.17 | convolution fusion | flops 3225944064 | bytes 6291456 | tf_op jit(solution)/shard_map/st,etc->esc/dot_general | solution.py:21
  347.5 11.6 %multiply_subtract_fusion = (f32[2,512,512]{2,1,0:T(8,128)S(1)}, f32[2,512,512]{2,1,0:T(8,128)S(1)}) fusion(f32[2,512,512]{2,1,0:T(8,128)S(1)} %multiply_add_fusion.1, f32[2,512,512]{2,1,0:T(8,128)S(1)} %multiply_subtract_fusion.3, f32[2,512,512]{2,1,0:T(8,128)S(1)} %multiply_subtract_fusion.1, f32[2,512,512]{2,1,0:T(8,128)S(1)} %bitcast.113, ...), kind=kOutput, calls=%fused_computation.11 | convolution fusion | flops 3229089792 | bytes 14680064 | tf_op jit(solution)/shard_map/st,etc->esc/dot_general | solution.py:22
  359.1 8.6 %fusion.2 = f32[2,512,512]{2,1,0:T(8,128)S(1)} fusion(f32[2,512,512]{2,1,0:T(8,128)S(1)} %get-tuple-element.6), kind=kOutput, calls=%fused_computation.2 | convolution fusion | flops 3224895488 | bytes 4194304 | tf_op jit(solution)/shard_map/ts,esc->etc/dot_general | solution.py:21
  367.7 8.4 %fusion = f32[2,512,512]{2,1,0:T(8,128)S(1)} fusion(f32[2,512,512]{2,1,0:T(8,128)S(1)} %get-tuple-element.6), kind=kOutput, calls=%fused_computation | convolution fusion | flops 3224895488 | bytes 4194304 | tf_op jit(solution)/shard_map/ts,esc->etc/dot_general | solution.py:22
  376.1 8.7 %fusion.8 = f32[2,512,512]{2,1,0:T(8,128)S(1)} fusion(f32[2,512,512]{2,1,0:T(8,128)S(1)} %fusion.2, f32[2,512,512]{2,1,0:T(8,128)S(1)} %get-tuple-element.5), kind=kOutput, calls=%fused_computation.20 | convolution fusion | flops 3225419776 | bytes 6291456 | tf_op jit(solution)/shard_map/ts,esc->etc/dot_general | solution.py:18
  384.8 8.8 %add_bitcast_fusion = (f32[2,512,512]{1,2,0:T(8,128)}, f32[2,512,512]{1,2,0:T(8,128)S(1)}) fusion(f32[2,512,512]{2,1,0:T(8,128)S(1)} %fusion.8, f32[2,512]{1,0:T(2,128)S(1)} %get-tuple-element.16, f32[2,512]{1,0:T(2,128)S(1)} %get-tuple-element.15, f32[2,512,512]{2,1,0:T(8,128)S(1)} %fusion, f32[2,512,512]{2,1,0:T(8,128)S(1)} %get-tuple-element.5), kind=kOutput, calls=%fused_computation.8 | convolution fusion | flops 3228565504 | bytes 10493952 | tf_op jit(solution)/shard_map/ts,esc->etc/dot_general | solution.py:19
  396.0 9.8 %all-to-all-start.6 = ((f32[2,512,512]{2,0,1:T(2,128)}), f32[2,512,512]{2,0,1:T(2,128)S(1)}, u32[]{:S(2)}, u32[]{:S(2)}) async-start(f32[2,512,512]{2,0,1:T(2,128)} %copy.74), calls=%async_computation.6 | async-start | bytes 4194304 | tf_op jit(solution)/shard_map/all_to_all | solution.py:68
  405.8 4.1 copy.77
  409.9 43.1 %all-to-all-done.6 = f32[2,512,512]{2,0,1:T(2,128)S(1)} async-done(((f32[2,512,512]{2,0,1:T(2,128)}), f32[2,512,512]{2,0,1:T(2,128)S(1)}, u32[]{:S(2)}, u32[]{:S(2)}) %all-to-all-start.6) | async-done | bytes 2097184 | tf_op jit(solution)/shard_map/all_to_all | solution.py:68
  453.0 5.6 all-to-all-start.7
  466.2 39.8 %all-to-all-done.7 = f32[2,512,512]{2,0,1:T(2,128)} async-done(((f32[2,512,512]{2,0,1:T(2,128)}), f32[2,512,512]{2,0,1:T(2,128)}, u32[]{:S(2)}, u32[]{:S(2)}) %all-to-all-start.7) | async-done | bytes 2097184 | tf_op jit(solution)/shard_map/all_to_all | solution.py:69
  515.6 30.4 %all_to_all.135 = f32[32,16,512]{2,1,0:T(8,128)S(1)} all-to-all(f32[32,16,512]{2,1,0:T(8,128)S(1)} %copy.80), channel_id=1, replica_groups=mesh['seq'=32,'chan'=8] {'seq'}, dimensions={0} | all-to-all | bytes 2097152 | tf_op jit(solution)/shard_map/all_to_all | solution.py:74
  546.2 5.6 fusion.178
  551.8 51.9 %reduce-scatter.2.cloned.1.call-done = f32[512,512]{1,0:T(8,128)} async-done(((f32[512,4096]{1,0:T(8,128)}), f32[512,512]{1,0:T(8,128)}) %reduce-scatter.2.cloned.1.call-update) | async-done | bytes 1048592 | tf_op jit(solution)/shard_map/reduce_scatter | solution.py:83
  (55 shorter events, 52.6 us)
Async XLA Ops:
  6.5 11.8 %copy-start.7 = (bf16[512,512]{1,0:T(8,128)(2,1)S(1)}, bf16[512,512]{1,0:T(8,128)(2,1)}, u32[]{:S(2)}) copy-start(bf16[512,512]{1,0:T(8,128)(2,1)} %param.6) | copy-start | bytes 1572868
  6.5 11.9 %copy-start.6 = (bf16[512,512]{1,0:T(8,128)(2,1)S(1)}, bf16[512,512]{1,0:T(8,128)(2,1)}, u32[]{:S(2)}) copy-start(bf16[512,512]{1,0:T(8,128)(2,1)} %param.7) | copy-start | bytes 1572868
  6.5 39.9 %all-to-all-start.3 = ((f32[32,16,512]{2,1,0:T(8,128)}), f32[32,16,512]{2,1,0:T(8,128)S(1)}, u32[]{:S(2)}, u32[]{:S(2)}) async-start(f32[32,16,512]{2,1,0:T(8,128)} %bitcast.123), calls=%async_computation.3 | async-start | bytes 2097152 | tf_op jit(solution)/shard_map/all_to_all | solution.py:41
  46.4 32.6 %all-to-all-start = ((f32[32,16,512]{2,1,0:T(8,128)}), f32[32,16,512]{2,1,0:T(8,128)S(1)}, u32[]{:S(2)}, u32[]{:S(2)}) async-start(f32[32,16,512]{2,1,0:T(8,128)} %bitcast.2), calls=%async_computation | async-start | bytes 2097152 | tf_op jit(solution)/shard_map/all_to_all | solution.py:40
  79.0 2.4 copy-start.2
  89.8 55.0 %all-to-all-start.4 = ((f32[64,16,512]{2,1,0:T(8,128)}), f32[64,16,512]{2,1,0:T(8,128)}, u32[]{:S(2)}, u32[]{:S(2)}) async-start(f32[64,16,512]{2,1,0:T(8,128)} %copy.64), calls=%async_computation.4 | async-start | bytes 4194304 | tf_op jit(solution)/shard_map/all_to_all | solution.py:56
  98.5 51.9 %copy-start.1 = (f32[64,16,512]{2,0,1:T(8,128)S(1)}, f32[64,16,512]{2,0,1:T(8,128)}, u32[]{:S(2)}) copy-start(f32[64,16,512]{2,0,1:T(8,128)} %get-tuple-element.12) | copy-start | bytes 6291460
  144.8 53.0 %all-to-all-start.5 = ((f32[64,16,512]{2,1,0:T(8,128)}), f32[64,16,512]{2,1,0:T(8,128)}, u32[]{:S(2)}, u32[]{:S(2)}) async-start(f32[64,16,512]{2,1,0:T(8,128)} %copy.67), calls=%async_computation.5 | async-start | bytes 4194304 | tf_op jit(solution)/shard_map/all_to_all | solution.py:56
  153.0 51.1 %copy-start = (f32[64,16,512]{2,0,1:T(8,128)S(1)}, f32[64,16,512]{2,0,1:T(8,128)}, u32[]{:S(2)}) copy-start(f32[64,16,512]{2,0,1:T(8,128)} %get-tuple-element.11) | copy-start | bytes 6291460
  197.8 53.5 %all-to-all-start.1 = ((f32[64,16,512]{2,1,0:T(8,128)}), f32[64,16,512]{2,1,0:T(8,128)}, u32[]{:S(2)}, u32[]{:S(2)}) async-start(f32[64,16,512]{2,1,0:T(8,128)} %copy.56), calls=%async_computation.1 | async-start | bytes 4194304 | tf_op jit(solution)/shard_map/all_to_all | solution.py:56
  251.2 59.8 %all-to-all-start.2 = ((f32[64,16,512]{2,1,0:T(8,128)}), f32[64,16,512]{2,1,0:T(8,128)S(1)}, u32[]{:S(2)}, u32[]{:S(2)}) async-start(f32[64,16,512]{2,1,0:T(8,128)} %copy.59), calls=%async_computation.2 | async-start | bytes 4194304 | tf_op jit(solution)/shard_map/all_to_all | solution.py:56
  311.0 1.6 copy-start.5
  311.0 2.2 copy-start.11
  313.2 11.4 %copy-start.9 = (f32[2,512,512]{2,1,0:T(8,128)S(1)}, f32[2,512,512]{2,1,0:T(8,128)}, u32[]{:S(2)}) copy-start(f32[2,512,512]{2,1,0:T(8,128)} %fusion.21) | copy-start | bytes 6291460
  324.7 11.2 %copy-start.10 = (f32[2,512,512]{2,1,0:T(8,128)S(1)}, f32[2,512,512]{2,1,0:T(8,128)}, u32[]{:S(2)}) copy-start(f32[2,512,512]{2,1,0:T(8,128)} %fusion.33) | copy-start | bytes 6291460
  335.9 11.6 %copy-start.4 = (f32[2,512,512]{2,1,0:T(8,128)S(1)}, f32[2,512,512]{2,1,0:T(8,128)}, u32[]{:S(2)}) copy-start(f32[2,512,512]{2,1,0:T(8,128)} %fusion.23) | copy-start | bytes 6291460
  396.0 57.0 %all-to-all-start.6 = ((f32[2,512,512]{2,0,1:T(2,128)}), f32[2,512,512]{2,0,1:T(2,128)S(1)}, u32[]{:S(2)}, u32[]{:S(2)}) async-start(f32[2,512,512]{2,0,1:T(2,128)} %copy.74), calls=%async_computation.6 | async-start | bytes 4194304 | tf_op jit(solution)/shard_map/all_to_all | solution.py:68
  453.0 53.1 %all-to-all-start.7 = ((f32[2,512,512]{2,0,1:T(2,128)}), f32[2,512,512]{2,0,1:T(2,128)}, u32[]{:S(2)}, u32[]{:S(2)}) async-start(f32[2,512,512]{2,0,1:T(2,128)} %copy.77), calls=%async_computation.7 | async-start | bytes 4194304 | tf_op jit(solution)/shard_map/all_to_all | solution.py:69
  458.6 145.0 %reduce-scatter.2.cloned.1.call-start = ((), (), s32[]{:S(2)}) async-start(), calls=%async_computation.10 | async-start | bytes 9437184 | tf_op jit(solution)/shard_map/reduce_scatter | solution.py:83
  513.7 32.2 %copy-start.8 = (bf16[512,512]{1,0:T(8,128)(2,1)S(1)}, bf16[512,512]{1,0:T(8,128)(2,1)}, u32[]{:S(2)}) copy-start(bf16[512,512]{1,0:T(8,128)(2,1)} %param.5) | copy-start | bytes 1572868
  515.0 31.2 %copy-start.3 = (bf16[512,4096]{1,0:T(8,128)(2,1)S(1)}, bf16[512,4096]{1,0:T(8,128)(2,1)}, u32[]{:S(2)}) copy-start(bf16[512,4096]{1,0:T(8,128)(2,1)} %param.9) | copy-start | bytes 12582916
Sparse Core Ops, SparseCore 0:
  551.9 51.6 reduce-scatter.1
where the time goes:
time: 623 us; the launch traced here: 613 us
  waiting for transfers between devices  317 us (51%)
  matrix products  152 us (24%)
  starting transfers between devices  57.2 us (9%)
  local copies, waits for them, and re-layouts  39.1 us (6%)
  blocking collectives  30.4 us (5%)
  between operations  14.2 us (2%)
    all_to_all x4, waiting for transfers between devices, split_sequence(): lax.all_to_all(tuple(partial_spectra), 'seq', split_axis=0, concat_axis=1...  136 us
    reduce_scatter x1, waiting for transfers between devices, shards(): lax.psum_scatter(partial_sums, 'chan', scatter_dimension=1, tiled=True)  51.9 us
    all_to_all x1, waiting for transfers between devices, split_sequence(): lax.all_to_all(inv_real, 'seq', split_axis=1, concat_axis=0, tiled=True)  43.1 us
    dot_general x5, matrix products, contract(): out_real = jnp.einsum(spec, cosine, real_part, precision=highest)  41.5 us
    all_to_all x1, waiting for transfers between devices, split_sequence(): lax.all_to_all(inv_imag, 'seq', split_axis=1, concat_axis=0, tiled=True)  39.8 us
    dot_general x5, matrix products, contract(): out_imag = sign * jnp.einsum(spec, sine, real_part, precision=highest)  38 us
    dot_general x3, matrix products, contract(): jnp.einsum(spec, sine, imag_part, precision=highest)  31.6 us
    dot_general x3, matrix products, contract(): out_imag = out_imag + jnp.einsum(spec, cosine, imag_part, precision=highest)  31.1 us
  transfers between devices with their start and end apart: 9, of which 8 were waited for; matrix products, arithmetic and copies ran while one was open for 13% of the time, Pallas kernels for 0%

commit v1 on v0

v1 whole, which is shorter than its diff:
```python
import functools

import jax
import jax.numpy as jnp
import numpy as np
from jax import lax
from jax.experimental import pallas as pl
from jax.experimental.pallas import tpu as pltpu
from jax.sharding import PartitionSpec as P

LANES = 128
COARSE = 128
TOTAL = 2 * COARSE * LANES
PEERS = 32
OWN = 16
SUB = 4


def split_bf16(x):
    high = x.astype(jnp.bfloat16)
    low = (x - high.astype(jnp.float32)).astype(jnp.bfloat16)
    return high, low


def np_split(x):
    x = np.asarray(x, np.float32)
    high = x.astype(jnp.bfloat16)
    low = (x - high.astype(np.float32)).astype(jnp.bfloat16)
    return high, low


def tables():
    k = np.arange(COARSE)
    q = np.arange(COARSE)
    r = np.arange(LANES)
    coarse = 2.0 * np.pi * ((k[:, None] * q[None, :]) % (2 * COARSE)) / (2 * COARSE)
    first = np.concatenate([np.cos(coarse), -np.sin(coarse)], 0)
    fine = 2.0 * np.pi * ((r[:, None] * r[None, :]) % LANES) / LANES
    cos_f, sin_f = np.cos(fine), np.sin(fine)
    second = np.block([[cos_f, -sin_f], [sin_f, cos_f]])
    second_inv = np.block([[cos_f, sin_f], [-sin_f, cos_f]])
    weight = np.where(k == 0, 1.0, 2.0)[None, :] / TOTAL
    last = np.concatenate([weight * np.cos(coarse.T), -weight * np.sin(coarse.T)], 1)
    twist = 2.0 * np.pi * ((k[:, None] * r[None, :]) % TOTAL) / TOTAL
    middle = 2.0 * np.pi * (COARSE * r) / TOTAL
    edge = np.stack([np.cos(middle), np.sin(middle)], 0)
    sign = np.broadcast_to(np.where(q % 2 == 0, 1.0, -1.0)[:, None] / TOTAL, (COARSE, LANES))
    first_h, first_l = np_split(first)
    out = [np.concatenate([first_h, first_h], 1), first_l]
    for matrix in (second, second_inv, last):
        out.extend(np_split(matrix))
    f32 = lambda x: np.ascontiguousarray(x).astype(np.float32)
    out.extend([f32(np.cos(twist)), f32(np.sin(twist)), f32(edge), f32(sign)])
    return out


def prepare_kernel(key_ref, value_ref, taps_ref, out_ref):
    signal = key_ref[...].astype(jnp.float32) * value_ref[...].astype(jnp.float32)
    taps = taps_ref[...]
    groups = LANES // OWN
    for e in range(SUB):
        rows = slice(e * LANES, (e + 1) * LANES)
        for s, stream in enumerate((signal, taps)):
            at = (2 * e + s) * OWN
            out_ref[:, at:at + OWN, :] = stream[rows, :].T.reshape(groups, OWN, LANES)


def prepare(key_stream, value, taps):
    rows, channels = key_stream.shape
    block = pl.BlockSpec((rows, LANES), lambda i: (0, i))
    return pl.pallas_call(
        prepare_kernel,
        grid=(channels // LANES,),
        in_specs=[block, block, block],
        out_specs=pl.BlockSpec((LANES // OWN, 2 * SUB * OWN, LANES), lambda i: (i, 0, 0)),
        out_shape=jax.ShapeDtypeStruct((PEERS, 2 * SUB * OWN, LANES), jnp.float32),
        compiler_params=pltpu.CompilerParams(vmem_limit_bytes=32 * 1024 * 1024),
        cost_estimate=pl.CostEstimate(flops=0, bytes_accessed=4 << 20, transcendentals=0),
    )(key_stream, value, taps)


def dot(a, b):
    return jnp.dot(a, b, preferred_element_type=jnp.float32)


def dot3(a, b_high, b_low):
    a_high, a_low = split_bf16(a)
    return dot(a_high, b_high) + dot(a_low, b_high) + dot(a_high, b_low)


def convolve_kernel(
    x_ref, first2, first_l, second_h, second_l, inverse_h, inverse_l, last_h, last_l,
    cos_ref, sin_ref, edge_ref, sign_ref, out_ref, edge_out,
):
    def add_pair(i, total):
        at = pl.multiple_of(i * (4 * OWN), 4 * OWN)
        return total + (x_ref[pl.ds(at, 2 * OWN), :] - x_ref[pl.ds(at + 2 * OWN, 2 * OWN), :])

    half = lax.fori_loop(
        0, COARSE // 2, add_pair, jnp.zeros((2 * OWN, LANES), jnp.float32), unroll=8
    )
    edge_cos, edge_sin = edge_ref[0:1, :], edge_ref[1:2, :]
    spun = jnp.concatenate([half * edge_cos, -half * edge_sin], 1)
    spectrum = dot3(spun, second_h[...], second_l[...])
    sig, fil = spectrum[:OWN], spectrum[OWN:]
    sr, si, fr, fi = sig[:, :LANES], sig[:, LANES:], fil[:, :LANES], fil[:, LANES:]
    product = jnp.concatenate([sr * fr - si * fi, sr * fi + si * fr], 1)
    back = dot3(product, inverse_h[...], inverse_l[...])
    edge_out[...] = back[:, :LANES] * edge_cos - back[:, LANES:] * edge_sin

    def pair(i, carry):
        c0 = 2 * i
        streams = [
            x_ref[pl.ds(s * OWN + c0 + j, COARSE, stride=2 * OWN), :]
            for j in range(2) for s in range(2)
        ]
        x = jnp.concatenate(streams, 1)
        x_h, x_l = split_bf16(x)
        y = dot(first2[...], jnp.concatenate([x_h, x_l], 0)) + dot(first_l[...], x_h)
        cos, sin = cos_ref[...], sin_ref[...]
        turned = []
        for j in range(4):
            yr = y[:COARSE, j * LANES:(j + 1) * LANES]
            yi = y[COARSE:, j * LANES:(j + 1) * LANES]
            turned.append(jnp.concatenate([yr * cos + yi * sin, yi * cos - yr * sin], 1))
        z = dot3(jnp.concatenate(turned, 0), second_h[...], second_l[...])
        products = []
        for j in range(2):
            sig = z[2 * j * COARSE:(2 * j + 1) * COARSE]
            fil = z[(2 * j + 1) * COARSE:(2 * j + 2) * COARSE]
            sr, si, fr, fi = sig[:, :LANES], sig[:, LANES:], fil[:, :LANES], fil[:, LANES:]
            products.append(jnp.concatenate([sr * fr - si * fi, sr * fi + si * fr], 1))
        u = dot3(jnp.concatenate(products, 0), inverse_h[...], inverse_l[...])
        columns = []
        for j in range(2):
            ur = u[j * COARSE:(j + 1) * COARSE, :LANES]
            ui = u[j * COARSE:(j + 1) * COARSE, LANES:]
            columns.append(jnp.concatenate([ur * cos - ui * sin, ur * sin + ui * cos], 0))
        v_h, v_l = split_bf16(jnp.concatenate(columns, 1))
        result = dot(last_h[...], v_h) + dot(last_h[...], v_l) + dot(last_l[...], v_h)
        for j in range(2):
            extra = sign_ref[...] * edge_out[pl.ds(c0 + j, 1), :]
            out_ref[pl.ds(c0 + j, COARSE, stride=OWN), :] = (
                result[:, j * LANES:(j + 1) * LANES] + extra
            )
        return carry

    lax.fori_loop(0, OWN // 2, pair, 0)


def convolve(x):
    consts = [jnp.asarray(t) for t in tables()]
    return pl.pallas_call(
        convolve_kernel,
        out_shape=jax.ShapeDtypeStruct((COARSE * OWN, LANES), jnp.float32),
        scratch_shapes=[pltpu.VMEM((OWN, LANES), jnp.float32)],
        compiler_params=pltpu.CompilerParams(vmem_limit_bytes=32 * 1024 * 1024),
        cost_estimate=pl.CostEstimate(flops=4 << 30, bytes_accessed=4 << 20, transcendentals=0),
    )(x, *consts)


def project_kernel(conv_ref, query_ref, w_ref, out_ref):
    conv = conv_ref[...].reshape(PEERS * OWN, LANES).T
    gated = (query_ref[...].astype(jnp.float32) * conv).astype(jnp.bfloat16)
    out_ref[...] = dot(gated, w_ref[...])


def project(conv, query, w_out):
    channels, width = w_out.shape
    return pl.pallas_call(
        project_kernel,
        grid=(SUB,),
        in_specs=[
            pl.BlockSpec((PEERS, OWN, LANES), lambda e: (0, e, 0)),
            pl.BlockSpec((LANES, channels), lambda e: (e, 0)),
            pl.BlockSpec((channels, width), lambda e: (0, 0)),
        ],
        out_specs=pl.BlockSpec((LANES, width), lambda e: (e, 0)),
        out_shape=jax.ShapeDtypeStruct((SUB * LANES, width), jnp.float32),
        compiler_params=pltpu.CompilerParams(vmem_limit_bytes=40 * 1024 * 1024),
        cost_estimate=pl.CostEstimate(flops=2 << 30, bytes_accessed=14 << 20, transcendentals=0),
    )(conv, query, w_out)


def shards(query, key_stream, value, long_filter, w_out):
    sent = prepare(key_stream, value, long_filter)
    moved = lax.all_to_all(sent, "seq", split_axis=0, concat_axis=0, tiled=True)
    conv = convolve(moved.reshape(PEERS * 2 * SUB * OWN, LANES))
    home = lax.all_to_all(
        conv.reshape(PEERS, SUB * OWN, LANES), "seq", split_axis=0, concat_axis=0, tiled=True
    )
    partial_sums = project(home, query, w_out)
    return lax.psum_scatter(partial_sums, "chan", scatter_dimension=1, tiled=True).astype(
        jnp.bfloat16
    )


def solution(mesh):
    in_specs = (
        P("seq", "chan"),
        P("seq", "chan"),
        P("seq", "chan"),
        P("seq", "chan"),
        P("chan", None),
    )
    out_specs = P("seq", "chan")
    return jax.shard_map(shards, mesh=mesh, in_specs=in_specs, out_specs=out_specs, check_vma=False)
```

time: 623 us -> 186 us (0.30); the launches traced: 613 us -> 185 us
  waiting for transfers between devices: 317 us -> 51.9 us
  matrix products: 152 us -> 0 us
  blocking collectives: 30.4 us -> 94.4 us
  starting transfers between devices: 57.2 us -> 0.01 us
  local copies, waits for them, and re-layouts: 39.1 us -> 6.63 us
  Pallas kernels: 0 us -> 16.4 us
    all_to_all x8 -> x0, waiting for transfers between devices: 265 us -> none  [the longest x4 136 us: split_sequence(): lax.all_to_all(tuple(partial_spectra), 'seq', split_axis=0, concat_axis=1...]
    dot_general x19 -> x0, matrix products: 152 us -> none  [the longest x5 41.5 us: contract(): out_real = jnp.einsum(spec, cosine, real_part, precision=highest)]
    all_to_all x1 -> x2, blocking collectives: 30.4 us -> 94.4 us  [the longest x1 62 us: shards(): moved = lax.all_to_all(sent, 'seq', split_axis=0, concat_axis=0, tiled=True)]
    all_to_all x8 -> x0, starting transfers between devices: 57.1 us -> none  [the longest x4 24.3 us: split_sequence(): lax.all_to_all(tuple(partial_spectra), 'seq', split_axis=0, concat_axis=1...]
    all_to_all x10 -> x0, local copies, waits for them, and re-layouts: 19.7 us -> none  [the longest x3 7.66 us: split_sequence(): lax.all_to_all(inv_imag, 'seq', split_axis=1, concat_axis=0, tiled=True)]
    pallas_call x0 -> x3, Pallas kernels: none -> 16.4 us  [the longest x1 12 us: convolve(): pl.pallas_call(convolve_kernel, out_shape=jax.ShapeDtypeStruct((COARSE *...]
    add x3 -> x0, local copies, waits for them, and re-layouts: 9.32 us -> none  [rotate(): imag_part * cosine + sign * real_part * sine]
    sub x3 -> x0, local copies, waits for them, and re-layouts: 7.55 us -> none  [rotate(): real_part * cosine - sign * imag_part * sine]
  transfers between devices with their start and end apart: 9 -> 1, of which waited for: 8 -> 1; matrix products, arithmetic and copies ran while one was open for 13% -> 0% of each run, Pallas kernels for 0% -> 0%
where the time goes in v1:
time: 186 us; the launch traced here: 185 us
  blocking collectives  94.4 us (51%)
  waiting for transfers between devices  51.9 us (28%)
  Pallas kernels  16.4 us (9%)
  between operations  13.6 us (7%)
  local copies, waits for them, and re-layouts  6.63 us (4%)
  other arithmetic  2.08 us (1%)
    all_to_all x1, blocking collectives, shards(): moved = lax.all_to_all(sent, 'seq', split_axis=0, concat_axis=0, tiled=True)  62 us
    reduce_scatter x1, waiting for transfers between devices, shards(): lax.psum_scatter(partial_sums, 'chan', scatter_dimension=1, tiled=True)  51.9 us
    all_to_all x1, blocking collectives, shards(): lax.all_to_all(conv.reshape(PEERS, SUB * OWN, LANES), 'seq', split_axis=0...  32.4 us
    pallas_call x1, Pallas kernels, convolve(): pl.pallas_call(convolve_kernel, out_shape=jax.ShapeDtypeStruct((COARSE *...  12 us
    unnamed x36, local copies, waits for them, and re-layouts  6.63 us
  transfers between devices with their start and end apart: 1, of which 1 were waited for; matrix products, arithmetic and copies ran while one was open for 0% of the time, Pallas kernels for 0%

profile of v1, /device:TPU:8, one launch (start us, length us, event | category | flops | bytes accessed | tf_op | source)
XLA Modules:
  0.0 184.9 jit_solution(15131028361641095394)
XLA Ops:
  6.5 0.0 reduce-scatter.2.cloned.1.call-start
  6.5 1.2 copy-done.2
  7.8 1.0 copy-done.4
  8.8 1.0 copy-done.5
  9.9 0.0 copy-start.10
  9.9 0.0 copy-start.11
  9.9 0.0 copy-start.12
  9.9 0.0 copy-start.13
  9.9 0.0 copy-start.14
  9.9 0.0 copy-start.15
  9.9 0.0 copy-start.16
  10.0 1.2 shard_map.163
  11.2 62.0 %all_to_all.10 = f32[32,128,128]{2,1,0:T(8,128)S(1)} all-to-all(f32[32,128,128]{2,1,0:T(8,128)S(1)} %shard_map.163), channel_id=1, replica_groups=mesh['seq'=32,'chan'=8] {'seq'}, dimensions={0} | all-to-all | bytes 4194304 | tf_op jit(solution)/shard_map/all_to_all | solution.py:187
  73.2 0.0 copy-done.17
  73.2 0.0 copy-done.6
  73.2 0.0 copy-done.7
  73.2 0.0 copy-done.8
  73.2 0.0 copy-done.9
  73.3 0.0 copy-done.10
  73.3 0.0 copy-done.11
  73.3 0.0 copy-done.12
  73.3 0.0 copy-done.13
  73.3 0.0 copy-start.1
  73.3 0.0 copy-start.3
  73.3 12.0 %shard_map.164 = f32[2048,128]{1,0:T(8,128)S(1)} custom-call(f32[4096,128]{1,0:T(8,128)S(1)} %bitcast.2, bf16[256,256]{1,0:T(8,128)(2,1)S(1)} %copy-done.10, bf16[256,128]{1,0:T(8,128)(2,1)S(1)} %copy-done.16, bf16[256,256]{1,0:T(8,128)(2,1)S(1)} %copy-done.9, bf16[256,256]{1,0:T(8,128)(2,1)S(1)} %copy-done.8, bf16[256,256]{1,0:T(8,128)(2,1)S(1)} %copy-done.7, ...), custom_call_target="tpu_custom_call" | custom-call | flops 4294967296 | bytes 4194304 | tf_op jit(solution)/shard_map/pallas_call | solution.py:153
  85.3 32.4 %all_to_all.11.conv_ref = f32[32,64,128]{2,1,0:T(8,128)S(1)} all-to-all(f32[32,64,128]{2,1,0:T(8,128)S(1)} %bitcast.3), channel_id=1, replica_groups=mesh['seq'=32,'chan'=8] {'seq'}, dimensions={0} | all-to-all | bytes 2097152 | tf_op jit(solution)/shard_map/all_to_all | solution.py:189
  117.7 0.0 copy-done.1
  117.7 3.2 %shard_map.165 = f32[512,4096]{1,0:T(8,128)S(1)} custom-call(f32[32,64,128]{2,1,0:T(8,128)S(1)} %all_to_all.11.conv_ref, bf16[512,512]{1,0:T(8,128)(2,1)S(1)} %copy-done.3, bf16[512,4096]{1,0:T(8,128)(2,1)S(1)} %copy-done.1), custom_call_target="tpu_custom_call" | custom-call | flops 2147483648 | bytes 14680064 | tf_op jit(solution)/shard_map/pallas_call | solution.py:170
  120.9 3.2 %copy-done = f32[512,4096]{1,0:T(8,128)} copy-done((f32[512,4096]{1,0:T(8,128)}, f32[512,4096]{1,0:T(8,128)S(1)}, u32[]{:S(2)}) %copy-start) | copy-done | bytes 8388632
  124.1 0.0 reduce-scatter.2.cloned.1.call-update
  124.2 51.9 %reduce-scatter.2.cloned.1.call-done = f32[512,512]{1,0:T(8,128)} async-done(((f32[512,4096]{1,0:T(8,128)}), f32[512,512]{1,0:T(8,128)}) %reduce-scatter.2.cloned.1.call-update) | async-done | bytes 1048592 | tf_op jit(solution)/shard_map/reduce_scatter | solution.py:193
  176.0 2.1 %convert_element_type.3 = bf16[512,512]{1,0:T(8,128)(2,1)} convert(f32[512,512]{1,0:T(8,128)} %reduce-scatter.2.cloned.1.call-done) | non-fusion elementwise | flops 262144 | bytes 1572864 | tf_op jit(solution)/shard_map/convert_element_type | solution.py:193
  (13 shorter events, 0.0 us)
Async XLA Ops:
  6.5 66.7 %copy-start.17 = (f32[2,128]{1,0:T(2,128)S(1)}, f32[2,128]{1,0:T(2,128)}, u32[]{:S(2)}) copy-start(f32[2,128]{1,0:T(2,128)} %constant.34.clone.edge_ref) | copy-start | bytes 3076
  6.5 169.5 %reduce-scatter.2.cloned.1.call-start = ((), (), s32[]{:S(2)}) async-start(), calls=%async_computation.3 | async-start | bytes 9437184 | tf_op jit(solution)/shard_map/reduce_scatter | solution.py:193
  6.5 1.2 copy-start.2
  7.8 1.0 copy-start.4
  8.8 1.0 copy-start.5
  9.9 63.4 %copy-start.6 = (bf16[256,256]{1,0:T(8,128)(2,1)S(1)}, bf16[256,256]{1,0:T(8,128)(2,1)}, u32[]{:S(2)}) copy-start(bf16[256,256]{1,0:T(8,128)(2,1)} %constant.29.clone.inverse_l) | copy-start | bytes 393220
  9.9 63.4 %copy-start.7 = (bf16[256,256]{1,0:T(8,128)(2,1)S(1)}, bf16[256,256]{1,0:T(8,128)(2,1)}, u32[]{:S(2)}) copy-start(bf16[256,256]{1,0:T(8,128)(2,1)} %constant.28.clone.inverse_h) | copy-start | bytes 393220
  9.9 63.4 %copy-start.8 = (bf16[256,256]{1,0:T(8,128)(2,1)S(1)}, bf16[256,256]{1,0:T(8,128)(2,1)}, u32[]{:S(2)}) copy-start(bf16[256,256]{1,0:T(8,128)(2,1)} %constant.27.clone.second_l) | copy-start | bytes 393220
  9.9 63.4 %copy-start.9 = (bf16[256,256]{1,0:T(8,128)(2,1)S(1)}, bf16[256,256]{1,0:T(8,128)(2,1)}, u32[]{:S(2)}) copy-start(bf16[256,256]{1,0:T(8,128)(2,1)} %constant.26.clone.second_h) | copy-start | bytes 393220
  9.9 63.4 %copy-start.10 = (bf16[256,256]{1,0:T(8,128)(2,1)S(1)}, bf16[256,256]{1,0:T(8,128)(2,1)}, u32[]{:S(2)}) copy-start(bf16[256,256]{1,0:T(8,128)(2,1)} %constant.24.clone.first2) | copy-start | bytes 393220
  9.9 63.4 %copy-start.11 = (f32[128,128]{1,0:T(8,128)S(1)}, f32[128,128]{1,0:T(8,128)}, u32[]{:S(2)}) copy-start(f32[128,128]{1,0:T(8,128)} %constant.35.clone.sign_ref) | copy-start | bytes 196612
  9.9 63.4 %copy-start.12 = (f32[128,128]{1,0:T(8,128)S(1)}, f32[128,128]{1,0:T(8,128)}, u32[]{:S(2)}) copy-start(f32[128,128]{1,0:T(8,128)} %constant.33.clone.sin_ref) | copy-start | bytes 196612
  9.9 63.4 %copy-start.13 = (f32[128,128]{1,0:T(8,128)S(1)}, f32[128,128]{1,0:T(8,128)}, u32[]{:S(2)}) copy-start(f32[128,128]{1,0:T(8,128)} %constant.32.clone.cos_ref) | copy-start | bytes 196612
  9.9 63.4 %copy-start.14 = (bf16[128,256]{1,0:T(8,128)(2,1)S(1)}, bf16[128,256]{1,0:T(8,128)(2,1)}, u32[]{:S(2)}) copy-start(bf16[128,256]{1,0:T(8,128)(2,1)} %constant.31.clone.last_l) | copy-start | bytes 196612
  9.9 63.4 %copy-start.15 = (bf16[128,256]{1,0:T(8,128)(2,1)S(1)}, bf16[128,256]{1,0:T(8,128)(2,1)}, u32[]{:S(2)}) copy-start(bf16[128,256]{1,0:T(8,128)(2,1)} %constant.30.clone.last_h) | copy-start | bytes 196612
  9.9 63.4 %copy-start.16 = (bf16[256,128]{1,0:T(8,128)(2,1)S(1)}, bf16[256,128]{1,0:T(8,128)(2,1)}, u32[]{:S(2)}) copy-start(bf16[256,128]{1,0:T(8,128)(2,1)} %constant.25.clone.first_l) | copy-start | bytes 196612
  73.3 44.4 %copy-start.1 = (bf16[512,4096]{1,0:T(8,128)(2,1)S(1)}, bf16[512,4096]{1,0:T(8,128)(2,1)}, u32[]{:S(2)}) copy-start(bf16[512,4096]{1,0:T(8,128)(2,1)} %w_ref.1) | copy-start | bytes 12582916
  73.3 44.4 %copy-start.3 = (bf16[512,512]{1,0:T(8,128)(2,1)S(1)}, bf16[512,512]{1,0:T(8,128)(2,1)}, u32[]{:S(2)}) copy-start(bf16[512,512]{1,0:T(8,128)(2,1)} %query_ref.1) | copy-start | bytes 1572868
  120.9 3.2 %copy-start = (f32[512,4096]{1,0:T(8,128)}, f32[512,4096]{1,0:T(8,128)S(1)}, u32[]{:S(2)}) copy-start(f32[512,4096]{1,0:T(8,128)S(1)} %shard_map.165) | copy-start | bytes 25165828
Sparse Core Ops, SparseCore 0:
  124.3 51.6 reduce-scatter.1

commit v2 on v1

v2 whole, which is shorter than its diff:
```python
import jax
import jax.numpy as jnp
import numpy as np
from jax import lax
from jax.experimental import pallas as pl
from jax.experimental.pallas import tpu as pltpu
from jax.sharding import PartitionSpec as P

LANES = 128
COARSE = 128
TOTAL = 2 * COARSE * LANES
PEERS = 32
OWN = 16
SUB = 4
CHIPS = 4
BLOCK = 512
GROUP = 8
BIG = 56 * 1024 * 1024
SMALL = 24 * 1024 * 1024


def split_bf16(x):
    high = x.astype(jnp.bfloat16)
    low = (x - high.astype(jnp.float32)).astype(jnp.bfloat16)
    return high, low


def tables():
    k = np.arange(COARSE)
    q = np.arange(COARSE)
    r = np.arange(LANES)
    coarse = 2.0 * np.pi * ((k[:, None] * q[None, :]) % (2 * COARSE)) / (2 * COARSE)
    first = np.concatenate([np.cos(coarse), -np.sin(coarse)], 0)
    fine = 2.0 * np.pi * ((r[:, None] * r[None, :]) % LANES) / LANES
    cos_f, sin_f = np.cos(fine), np.sin(fine)
    second = np.block([[cos_f, -sin_f], [sin_f, cos_f]])
    second_inv = np.block([[cos_f, sin_f], [-sin_f, cos_f]])
    weight = np.where(k == 0, 1.0, 2.0)[None, :] / TOTAL
    last = np.concatenate([weight * np.cos(coarse.T), -weight * np.sin(coarse.T)], 1)
    twist = 2.0 * np.pi * ((k[:, None] * r[None, :]) % TOTAL) / TOTAL
    middle = 2.0 * np.pi * (COARSE * r) / TOTAL
    edge = np.stack([np.cos(middle), np.sin(middle)], 0)
    sign = np.broadcast_to(np.where(q % 2 == 0, 1.0, -1.0)[:, None] / TOTAL, (COARSE, LANES))
    f32 = lambda x: np.ascontiguousarray(x).astype(np.float32)
    return [f32(t) for t in (first, second, second_inv, last, np.cos(twist), np.sin(twist), edge, sign)]


def prepare_kernel(key_ref, value_ref, taps_ref, out_ref):
    signal = key_ref[...].astype(jnp.float32) * value_ref[...].astype(jnp.float32)
    taps = taps_ref[...]
    for e in range(signal.shape[0] // LANES):
        rows = slice(e * LANES, (e + 1) * LANES)
        for s, stream in enumerate((signal, taps)):
            at = (2 * e + s) * OWN
            out_ref[:, at:at + OWN, :] = stream[rows, :].T.reshape(PEERS, OWN, LANES)


def prepare(key_stream, value, taps):
    rows, channels = key_stream.shape
    steps = 2
    block = pl.BlockSpec((rows // steps, channels), lambda i: (i, 0))
    sent = 2 * SUB * OWN
    return pl.pallas_call(
        prepare_kernel,
        grid=(steps,),
        in_specs=[block, block, block],
        out_specs=pl.BlockSpec((PEERS, sent // steps, LANES), lambda i: (0, i, 0)),
        out_shape=jax.ShapeDtypeStruct((PEERS, sent, LANES), jnp.float32),
        compiler_params=pltpu.CompilerParams(vmem_limit_bytes=BIG),
        cost_estimate=pl.CostEstimate(flops=0, bytes_accessed=4 << 20, transcendentals=0),
    )(key_stream, value, taps)


def dot(a, b):
    return jnp.dot(a, b, preferred_element_type=jnp.float32)


def rows_by(a, stacked):
    high, low = split_bf16(a)
    return dot(jnp.concatenate([high, low, high], 1), stacked)


def by_columns(stacked, a):
    high, low = split_bf16(a)
    return dot(stacked, jnp.concatenate([high, low, high], 0))


def multiply(a, b):
    ar, ai, br, bi = a[:, :LANES], a[:, LANES:], b[:, :LANES], b[:, LANES:]
    return jnp.concatenate([ar * br - ai * bi, ar * bi + ai * br], 1)


def convolve_kernel(
    x_ref, first_ref, second_ref, inverse_ref, last_ref, cos_ref, sin_ref, edge_ref, sign_ref,
    out_ref, edge_out, first, second, inverse, last,
):
    for ref, table, axis in (
        (first_ref, first, 1), (second_ref, second, 0), (inverse_ref, inverse, 0), (last_ref, last, 1)
    ):
        high, low = split_bf16(ref[...])
        table[...] = jnp.concatenate([high, high, low], axis)

    def add_pair(i, total):
        at = pl.multiple_of(i * (4 * OWN), 4 * OWN)
        return total + (x_ref[pl.ds(at, 2 * OWN), :] - x_ref[pl.ds(at + 2 * OWN, 2 * OWN), :])

    half = lax.fori_loop(
        0, COARSE // 2, add_pair, jnp.zeros((2 * OWN, LANES), jnp.float32), unroll=8
    )
    edge_cos, edge_sin = edge_ref[0:1, :], edge_ref[1:2, :]
    spectrum = rows_by(jnp.concatenate([half * edge_cos, -half * edge_sin], 1), second[...])
    back = rows_by(multiply(spectrum[:OWN], spectrum[OWN:]), inverse[...])
    edge_out[...] = back[:, :LANES] * edge_cos - back[:, LANES:] * edge_sin

    def some_channels(i, carry):
        c0 = GROUP * i
        streams = [
            x_ref[pl.ds(s * OWN + c0 + j, COARSE, stride=2 * OWN), :]
            for j in range(GROUP) for s in range(2)
        ]
        y = by_columns(first[...], jnp.concatenate(streams, 1))
        cos, sin = cos_ref[...], sin_ref[...]
        turned = []
        for j in range(2 * GROUP):
            yr = y[:COARSE, j * LANES:(j + 1) * LANES]
            yi = y[COARSE:, j * LANES:(j + 1) * LANES]
            turned.append(jnp.concatenate([yr * cos + yi * sin, yi * cos - yr * sin], 1))
        z = rows_by(jnp.concatenate(turned, 0), second[...])
        products = [
            multiply(
                z[2 * j * COARSE:(2 * j + 1) * COARSE], z[(2 * j + 1) * COARSE:(2 * j + 2) * COARSE]
            )
            for j in range(GROUP)
        ]
        u = rows_by(jnp.concatenate(products, 0), inverse[...])
        columns = []
        for j in range(GROUP):
            ur = u[j * COARSE:(j + 1) * COARSE, :LANES]
            ui = u[j * COARSE:(j + 1) * COARSE, LANES:]
            columns.append(jnp.concatenate([ur * cos - ui * sin, ur * sin + ui * cos], 0))
        result = by_columns(last[...], jnp.concatenate(columns, 1))
        for j in range(GROUP):
            extra = sign_ref[...] * edge_out[pl.ds(c0 + j, 1), :]
            out_ref[pl.ds(c0 + j, COARSE, stride=OWN), :] = (
                result[:, j * LANES:(j + 1) * LANES] + extra
            )
        return carry

    lax.fori_loop(0, OWN // GROUP, some_channels, 0)


def convolve(x):
    consts = [jnp.asarray(t) for t in tables()]
    return pl.pallas_call(
        convolve_kernel,
        out_shape=jax.ShapeDtypeStruct((COARSE * OWN, LANES), jnp.float32),
        scratch_shapes=[
            pltpu.VMEM((OWN, LANES), jnp.float32),
            pltpu.VMEM((2 * COARSE, 3 * COARSE), jnp.bfloat16),
            pltpu.VMEM((6 * LANES, 2 * LANES), jnp.bfloat16),
            pltpu.VMEM((6 * LANES, 2 * LANES), jnp.bfloat16),
            pltpu.VMEM((COARSE, 6 * COARSE), jnp.bfloat16),
        ],
        compiler_params=pltpu.CompilerParams(vmem_limit_bytes=SMALL),
        cost_estimate=pl.CostEstimate(flops=4 << 30, bytes_accessed=4 << 20, transcendentals=0),
    )(x, *consts)


def widen_kernel(where_ref, both_ref, first_ref, second_ref, one_ref, two_ref):
    both = both_ref[...].astype(jnp.float32)
    one_ref[0], one_ref[1] = both, first_ref[...].astype(jnp.float32)
    two_ref[0], two_ref[1] = both, second_ref[...].astype(jnp.float32)


def widen(w_out, where):
    channels, width = w_out.shape
    quarter = width // CHIPS
    steps = 2
    rows = channels // steps
    column = lambda n: pl.BlockSpec((rows, quarter), lambda i, where: (i, where[n]))
    out = pl.BlockSpec((2, rows, quarter), lambda i, where: (0, i, 0))
    shape = jax.ShapeDtypeStruct((2, channels, quarter), jnp.float32)
    return pl.pallas_call(
        widen_kernel,
        grid_spec=pltpu.PrefetchScalarGridSpec(
            num_scalar_prefetch=1,
            grid=(steps,),
            in_specs=[column(0), column(1), column(2)],
            out_specs=(out, out),
        ),
        out_shape=(shape, shape),
        compiler_params=pltpu.CompilerParams(vmem_limit_bytes=BIG),
        cost_estimate=pl.CostEstimate(flops=0, bytes_accessed=11 << 20, transcendentals=0),
    )(where, w_out, w_out, w_out)


def gate_kernel(conv_ref, query_ref, top_ref, bottom_ref):
    for e in range(SUB):
        rows = slice(e * LANES, (e + 1) * LANES)
        conv = conv_ref[:, e * OWN:(e + 1) * OWN, :].reshape(PEERS * OWN, LANES).T
        gated = query_ref[rows, :].astype(jnp.float32) * conv
        out_ref = top_ref if e < SUB // 2 else bottom_ref
        at = (e % (SUB // 2)) * LANES
        out_ref[at:at + LANES, :] = gated.astype(jnp.bfloat16).astype(jnp.float32)


def gate(conv, query):
    rows, channels = query.shape
    half = jax.ShapeDtypeStruct((rows // 2, channels), jnp.float32)
    return pl.pallas_call(
        gate_kernel,
        out_shape=(half, half),
        compiler_params=pltpu.CompilerParams(vmem_limit_bytes=SMALL),
        cost_estimate=pl.CostEstimate(flops=0, bytes_accessed=3 << 20, transcendentals=0),
    )(conv, query)


def own_kernel(where_ref, top_ref, bottom_ref, w_ref, out_ref):
    gated = jnp.where(pl.program_id(0) % 2 == 0, top_ref[...], bottom_ref[...])
    out_ref[...] = dot(gated.astype(jnp.bfloat16), w_ref[...])


def own_part(top, bottom, w_out, where):
    rows, channels = top.shape
    quarter = w_out.shape[1] // CHIPS
    whole = pl.BlockSpec((rows, channels), lambda i, where: (0, 0))
    return pl.pallas_call(
        own_kernel,
        grid_spec=pltpu.PrefetchScalarGridSpec(
            num_scalar_prefetch=1,
            grid=(4,),
            in_specs=[whole, whole, pl.BlockSpec((channels, quarter), lambda i, where: (0, where[i]))],
            out_specs=pl.BlockSpec((None, None, rows, quarter), lambda i, where: (i // 2, i % 2, 0, 0)),
        ),
        out_shape=jax.ShapeDtypeStruct((2, 2, rows, quarter), jnp.float32),
        compiler_params=pltpu.CompilerParams(vmem_limit_bytes=SMALL),
        cost_estimate=pl.CostEstimate(flops=1 << 30, bytes_accessed=8 << 20, transcendentals=0),
    )(where, top, bottom, w_out)


def add_kernel(core_ref, acc_ref, top_ref, bottom_ref, w_top_ref, w_bottom_ref, out_ref):
    for i, (gated, w) in enumerate(((top_ref, w_top_ref), (bottom_ref, w_bottom_ref))):
        out_ref[i] = acc_ref[i] + dot(
            gated[...].astype(jnp.bfloat16), w[...].astype(jnp.bfloat16)
        )


def add_partner(acc, top, bottom, w_top, w_bottom, which, parity):
    rows, channels = top.shape
    steps = 2
    columns = BLOCK // steps
    at = lambda n, parity: parity[0] * steps + n
    whole = pl.BlockSpec((rows, channels), lambda n, parity: (0, 0))
    weights = pl.BlockSpec((None, channels, columns), lambda n, parity: (which, 0, at(n, parity)))
    return pl.pallas_call(
        add_kernel,
        grid_spec=pltpu.PrefetchScalarGridSpec(
            num_scalar_prefetch=1,
            grid=(steps,),
            in_specs=[
                pl.BlockSpec(
                    (None, 2, rows, columns), lambda n, parity: (which, 0, 0, at(n, parity))
                ),
                whole,
                whole,
                weights,
                weights,
            ],
            out_specs=pl.BlockSpec((2, rows, columns), lambda n, parity: (0, 0, n)),
        ),
        out_shape=jax.ShapeDtypeStruct((2, rows, BLOCK), jnp.float32),
        compiler_params=pltpu.CompilerParams(vmem_limit_bytes=SMALL),
        cost_estimate=pl.CostEstimate(flops=1 << 28, bytes_accessed=5 << 20, transcendentals=0),
    )(parity, acc, top, bottom, w_top, w_bottom)


def sum_kernel(a_ref, b_ref, top_ref, bottom_ref):
    top_ref[...] = a_ref[0] + b_ref[0]
    bottom_ref[...] = a_ref[1] + b_ref[1]


def sum_cores(a, b):
    half = jax.ShapeDtypeStruct(a.shape[1:], jnp.float32)
    return pl.pallas_call(
        sum_kernel,
        out_shape=(half, half),
        compiler_params=pltpu.CompilerParams(vmem_limit_bytes=SMALL),
        cost_estimate=pl.CostEstimate(flops=1 << 18, bytes_accessed=3 << 20, transcendentals=0),
    )(a, b)


def last_kernel(a_ref, b_ref, top_ref, bottom_ref, out_ref):
    rows = top_ref.shape[0]
    for i, far in enumerate((top_ref, bottom_ref)):
        total = a_ref[i] + b_ref[i] + far[...]
        out_ref[i * rows:(i + 1) * rows, :] = total.astype(out_ref.dtype)


def last_sum(a, b, top, bottom):
    rows, columns = top.shape
    return pl.pallas_call(
        last_kernel,
        out_shape=jax.ShapeDtypeStruct((2 * rows, columns), jnp.bfloat16),
        compiler_params=pltpu.CompilerParams(vmem_limit_bytes=SMALL),
        cost_estimate=pl.CostEstimate(flops=1 << 19, bytes_accessed=4 << 20, transcendentals=0),
    )(a, b, top, bottom)


def shards(query, key_stream, value, long_filter, w_out):
    index = lax.axis_index("chan")
    chip, core = index // 2, index % 2
    step = 1 - 2 * (chip % 2)
    one, two, opposite = (chip + step) % CHIPS, (chip - step) % CHIPS, (chip + 2) % CHIPS
    size = 2 * CHIPS
    send_one = lambda x: lax.ppermute(x, "chan", [(i, i ^ 2) for i in range(size)])
    send_two = lambda x: lax.ppermute(
        x, "chan", [(i, (i - 2 if i // 2 % 2 == 0 else i + 2) % size) for i in range(size)]
    )
    send_core = lambda x: lax.ppermute(x, "chan", [(i, i ^ 1) for i in range(size)])

    sent = prepare(key_stream, value, long_filter)
    wide_one, wide_two = widen(w_out, jnp.stack([opposite, one, two]))
    w_one, w_two = send_one(wide_one), send_two(wide_two)
    moved = lax.all_to_all(sent, "seq", split_axis=0, concat_axis=0, tiled=True)
    conv = convolve(moved.reshape(PEERS * 2 * SUB * OWN, LANES))
    home = lax.all_to_all(
        conv.reshape(PEERS, SUB * OWN, LANES), "seq", split_axis=0, concat_axis=0, tiled=True
    )
    top, bottom = gate(home, query)
    top_one, bottom_two = send_one(top), send_two(bottom)
    acc = own_part(top, bottom, w_out, jnp.stack([two, one, chip, chip]))
    mine, theirs = core.reshape(1), (1 - core).reshape(1)
    add = lambda which, parity: add_partner(
        acc, top_one, bottom_two, w_one, w_two, which, parity
    )
    away_top, away_bottom = sum_cores(add(0, mine), send_core(add(0, theirs)))
    from_two, from_one = send_two(away_top), send_one(away_bottom)
    return last_sum(add(1, mine), send_core(add(1, theirs)), from_two, from_one)


def solution(mesh):
    in_specs = (
        P("seq", "chan"),
        P("seq", "chan"),
        P("seq", "chan"),
        P("seq", "chan"),
        P("chan", None),
    )
    out_specs = P("seq", "chan")
    return jax.shard_map(shards, mesh=mesh, in_specs=in_specs, out_specs=out_specs, check_vma=False)
```

time: 186 us -> 151 us (0.81)
  blocking collectives: 94.4 us -> 33.7 us
  starting transfers between devices: 0.01 us -> 21.8 us
  between operations: 13.6 us -> 0.27 us
  Pallas kernels: 16.4 us -> 28.7 us
  waiting for transfers between devices: 51.9 us -> 62.9 us
  local copies, waits for them, and re-layouts: 6.63 us -> 2.24 us
    all_to_all x1 -> x0, blocking collectives: 62 us -> none  [shards(): moved = lax.all_to_all(sent, 'seq', split_axis=0, concat_axis=0, tiled=True)]
    reduce_scatter x1 -> x0, waiting for transfers between devices: 51.9 us -> none  [shards(): lax.psum_scatter(partial_sums, 'chan', scatter_dimension=1, tiled=True)]
    all_to_all x0 -> x1, waiting for transfers between devices: none -> 39.2 us  [shards(): moved = lax.all_to_all(sent, 'seq', split_axis=0, concat_axis=0, tiled=True)]
    ppermute x0 -> x8, waiting for transfers between devices: none -> 23.7 us  [the longest x3 16.1 us: shards(): lax.ppermute(x, 'chan', [(i, (i - 2 if i // 2 % 2 == 0 else i + 2) % size...]
    pallas_call x2 -> x10, Pallas kernels: 4.38 us -> 20.6 us  [the longest x4 7.99 us: add_partner(): pl.pallas_call(add_kernel, grid_spec=pltpu.PrefetchScalarGridSpec(num_sca...]
    all_to_all x0 -> x1, starting transfers between devices: none -> 11.7 us  [shards(): moved = lax.all_to_all(sent, 'seq', split_axis=0, concat_axis=0, tiled=True)]
    ppermute x0 -> x8, starting transfers between devices: none -> 10.1 us  [the longest x3 6.38 us: shards(): lax.ppermute(x, 'chan', [(i, (i - 2 if i // 2 % 2 == 0 else i + 2) % size...]
    unnamed x36 -> x20, local copies, waits for them, and re-layouts: 6.63 us -> 2.24 us
  transfers between devices with their start and end apart: 1 -> 9, of which waited for: 1 -> 7; matrix products, arithmetic and copies ran while one was open for 0% -> 0% of each run, Pallas kernels for 0% -> 15%
where the time goes in v2:
time: 151 us; the launch traced here: 150 us
  waiting for transfers between devices  62.9 us (42%)
  blocking collectives  33.7 us (22%)
  Pallas kernels  28.7 us (19%)
  starting transfers between devices  21.8 us (14%)
  local copies, waits for them, and re-layouts  2.24 us (1%)
    all_to_all x1, waiting for transfers between devices, shards(): moved = lax.all_to_all(sent, 'seq', split_axis=0, concat_axis=0, tiled=True)  39.2 us
    all_to_all x1, blocking collectives, shards(): lax.all_to_all(conv.reshape(PEERS, SUB * OWN, LANES), 'seq', split_axis=0...  33.7 us
    ppermute x3, waiting for transfers between devices, shards(): lax.ppermute(x, 'chan', [(i, (i - 2 if i // 2 % 2 == 0 else i + 2) % size...  16.1 us
    all_to_all x1, starting transfers between devices, shards(): moved = lax.all_to_all(sent, 'seq', split_axis=0, concat_axis=0, tiled=True)  11.7 us
    pallas_call x1, Pallas kernels, convolve(): pl.pallas_call(convolve_kernel, out_shape=jax.ShapeDtypeStruct((COARSE *...  8.04 us
    pallas_call x4, Pallas kernels, add_partner(): pl.pallas_call(add_kernel, grid_spec=pltpu.PrefetchScalarGridSpec(num_sca...  7.99 us
    ppermute x3, waiting for transfers between devices, shards(): lax.ppermute(x, 'chan', [(i, i ^ 2) for i in range(size)])  7.59 us
    ppermute x3, starting transfers between devices, shards(): lax.ppermute(x, 'chan', [(i, (i - 2 if i // 2 % 2 == 0 else i + 2) % size...  6.38 us
  transfers between devices with their start and end apart: 9, of which 7 were waited for; matrix products, arithmetic and copies ran while one was open for 0% of the time, Pallas kernels for 15%

profile of v2, /device:TPU:8, one launch (start us, length us, event | category | flops | bytes accessed | tf_op | source)
XLA Modules:
  0.0 150.3 jit_solution(15422777025245920605)
XLA Ops:
  0.0 3.0 %shard_map.127 = f32[32,128,128]{2,1,0:T(8,128)} custom-call(bf16[512,512]{1,0:T(8,128)(2,1)} %key_ref.1, bf16[512,512]{1,0:T(8,128)(2,1)} %value_ref.1, f32[512,512]{1,0:T(8,128)} %taps_ref.1), custom_call_target="tpu_custom_call" | custom-call | bytes 4194304 | tf_op jit(solution)/shard_map/pallas_call | solution.py:63
  3.0 11.7 %all-to-all-start = ((f32[32,128,128]{2,1,0:T(8,128)}), f32[32,128,128]{2,1,0:T(8,128)S(1)}, u32[]{:S(2)}, u32[]{:S(2)}) async-start(f32[32,128,128]{2,1,0:T(8,128)} %shard_map.127), calls=%async_computation | async-start | bytes 4194304 | tf_op jit(solution)/shard_map/all_to_all | solution.py:324
  14.7 0.6 pad_add_fusion.1.where_ref
  15.3 0.0 copy-start.6
  15.4 0.0 copy-start.7
  15.4 5.7 %shard_map.131 = (f32[2,512,1024]{2,1,0:T(8,128)}, f32[2,512,1024]{2,1,0:T(8,128)}) custom-call(s32[3]{0:T(128)} %pad_add_fusion.1.where_ref, bf16[512,4096]{1,0:T(8,128)(2,1)} %second_ref.2, bf16[512,4096]{1,0:T(8,128)(2,1)} %second_ref.2, bf16[512,4096]{1,0:T(8,128)(2,1)} %second_ref.2), custom_call_target="tpu_custom_call" | custom-call | bytes 11534336 | tf_op jit(solution)/shard_map/pallas_call | solution.py:183
  21.1 1.5 collective-permute-start.2
  22.6 2.1 %collective-permute-start.3 = (f32[2,512,1024]{2,1,0:T(8,128)}, f32[2,512,1024]{2,1,0:T(8,128)}, u32[]{:S(2)}, u32[]{:S(2)}) collective-permute-start(f32[2,512,1024]{2,1,0:T(8,128)} %get-tuple-element.14), channel_id=1, source_target_pairs={{0,6},{1,7},{2,4},{3,5},{4,2},{5,3},{6,0},{7,1},{8,14},{9,15},{10,... | collective-permute-start | bytes 12582920 | tf_op jit(solution)/shard_map/ppermute | solution.py:316
  24.7 39.2 %all-to-all-done = f32[32,128,128]{2,1,0:T(8,128)S(1)} async-done(((f32[32,128,128]{2,1,0:T(8,128)}), f32[32,128,128]{2,1,0:T(8,128)S(1)}, u32[]{:S(2)}, u32[]{:S(2)}) %all-to-all-start) | async-done | bytes 2097184 | tf_op jit(solution)/shard_map/all_to_all | solution.py:324
  64.0 8.0 %shard_map.128 = f32[2048,128]{1,0:T(8,128)S(1)} custom-call(f32[4096,128]{1,0:T(8,128)S(1)} %bitcast.8, f32[256,128]{1,0:T(8,128)S(1)} %copy-done.4, f32[256,256]{1,0:T(8,128)S(1)} %copy-done.2, f32[256,256]{1,0:T(8,128)S(1)} %copy-done.3, f32[128,256]{1,0:T(8,128)S(1)} %copy-done.5, f32[128,128]{1,0:T(8,128)S(1)} %copy-done.6, f32[128,128]{1,0:T(8,128)S(1)} %copy-done.7, ...), custom_call_target="tpu_custom_call" | custom-call | flops 4294967296 | bytes 4194304 | tf_op jit(solution)/shard_map/pallas_call | solution.py:154
  72.0 33.7 %all_to_all.10.conv_ref = f32[32,64,128]{2,1,0:T(8,128)S(1)} all-to-all(f32[32,64,128]{2,1,0:T(8,128)S(1)} %bitcast.9), channel_id=1, replica_groups=mesh['seq'=32,'chan'=8] {'seq'}, dimensions={0} | all-to-all | bytes 2097152 | tf_op jit(solution)/shard_map/all_to_all | solution.py:326
  105.8 0.3 shard_map.129
  106.1 1.6 %collective-permute-start = (f32[256,512]{1,0:T(8,128)S(1)}, f32[256,512]{1,0:T(8,128)S(1)}, u32[]{:S(2)}, u32[]{:S(2)}) collective-permute-start(f32[256,512]{1,0:T(8,128)S(1)} %get-tuple-element.11.top_ref), channel_id=1, source_target_pairs={{0,2},{1,3},{2,0},{3,1},{4,6},{5,7},{6,4},{7,5},{8,10},{9,11},{10,... | collective-permute-start | bytes 1572872 | tf_op jit(solution)/shard_map/ppermute | solution.py:315
  107.7 2.1 %collective-permute-start.1 = (f32[256,512]{1,0:T(8,128)S(1)}, f32[256,512]{1,0:T(8,128)S(1)}, u32[]{:S(2)}, u32[]{:S(2)}) collective-permute-start(f32[256,512]{1,0:T(8,128)S(1)} %get-tuple-element.12.bottom_ref), channel_id=1, source_target_pairs={{0,6},{1,7},{2,4},{3,5},{4,2},{5,3},{6,0},{7,1},{8,14},{9,15},{10,... | collective-permute-start | bytes 1572872 | tf_op jit(solution)/shard_map/ppermute | solution.py:316
  109.8 0.1 pad_add_fusion.where_ref
  109.9 2.2 %copy-done = bf16[512,4096]{1,0:T(8,128)(2,1)S(1)} copy-done((bf16[512,4096]{1,0:T(8,128)(2,1)S(1)}, bf16[512,4096]{1,0:T(8,128)(2,1)}, u32[]{:S(2)}) %copy-start) | copy-done | bytes 4194328
  112.0 2.6 %shard_map.130.acc_ref = f32[2,2,256,1024]{3,2,1,0:T(8,128)S(1)} custom-call(s32[4]{0:T(128)S(1)} %pad_add_fusion.where_ref, f32[256,512]{1,0:T(8,128)S(1)} %get-tuple-element.11.top_ref, f32[256,512]{1,0:T(8,128)S(1)} %get-tuple-element.12.bottom_ref, bf16[512,4096]{1,0:T(8,128)(2,1)S(1)} %copy-done), custom_call_target="tpu_custom_call" | custom-call | flops 1073741824 | bytes 8388608 | tf_op jit(solution)/shard_map/pallas_call | solution.py:227
  114.6 0.3 collective-permute-done.2.w_top_ref
  115.0 2.7 %collective-permute-done.3.w_bottom_ref = f32[2,512,1024]{2,1,0:T(8,128)} collective-permute-done((f32[2,512,1024]{2,1,0:T(8,128)}, f32[2,512,1024]{2,1,0:T(8,128)}, u32[]{:S(2)}, u32[]{:S(2)}) %collective-permute-start.3) | collective-permute-done | bytes 4194336 | tf_op jit(solution)/shard_map/ppermute | solution.py:316
  117.7 6.7 %collective-permute-done.top_ref = f32[256,512]{1,0:T(8,128)S(1)} collective-permute-done((f32[256,512]{1,0:T(8,128)S(1)}, f32[256,512]{1,0:T(8,128)S(1)}, u32[]{:S(2)}, u32[]{:S(2)}) %collective-permute-start) | collective-permute-done | bytes 524320 | tf_op jit(solution)/shard_map/ppermute | solution.py:315
  124.3 2.4 %collective-permute-done.1.bottom_ref = f32[256,512]{1,0:T(8,128)S(1)} collective-permute-done((f32[256,512]{1,0:T(8,128)S(1)}, f32[256,512]{1,0:T(8,128)S(1)}, u32[]{:S(2)}, u32[]{:S(2)}) %collective-permute-start.1) | collective-permute-done | bytes 524320 | tf_op jit(solution)/shard_map/ppermute | solution.py:316
  126.7 2.0 %shard_map.135 = f32[2,256,512]{2,1,0:T(8,128)S(1)} custom-call(s32[1]{0:T(128)} %bitcast.7.core_ref, f32[2,2,256,1024]{3,2,1,0:T(8,128)S(1)} %shard_map.130.acc_ref, f32[256,512]{1,0:T(8,128)S(1)} %collective-permute-done.top_ref, f32[256,512]{1,0:T(8,128)S(1)} %collective-permute-done.1.bottom_ref, f32[2,512,1024]{2,1,0:T(8,128)} %collective-permute-done.2.w_top_ref, ...), custom_call_target="tpu_custom_call" | custom-call | flops 268435456 | bytes 5242880 | tf_op jit(solution)/shard_map/pallas_call | solution.py:255
  128.7 0.1 collective-permute-start.5
  128.8 2.0 %shard_map.133 = f32[2,256,512]{2,1,0:T(8,128)S(1)} custom-call(s32[1]{0:T(128)} %bitcast.7.core_ref, f32[2,2,256,1024]{3,2,1,0:T(8,128)S(1)} %shard_map.130.acc_ref, f32[256,512]{1,0:T(8,128)S(1)} %collective-permute-done.top_ref, f32[256,512]{1,0:T(8,128)S(1)} %collective-permute-done.1.bottom_ref, f32[2,512,1024]{2,1,0:T(8,128)} %collective-permute-done.2.w_top_ref, ...), custom_call_target="tpu_custom_call" | custom-call | flops 268435456 | bytes 5242880 | tf_op jit(solution)/shard_map/pallas_call | solution.py:255
  130.9 0.6 collective-permute-start.4
  131.4 2.0 %shard_map.134.a_ref = f32[2,256,512]{2,1,0:T(8,128)S(1)} custom-call(s32[1]{0:T(128)} %bitcast.core_ref, f32[2,2,256,1024]{3,2,1,0:T(8,128)S(1)} %shard_map.130.acc_ref, f32[256,512]{1,0:T(8,128)S(1)} %collective-permute-done.top_ref, f32[256,512]{1,0:T(8,128)S(1)} %collective-permute-done.1.bottom_ref, f32[2,512,1024]{2,1,0:T(8,128)} %collective-permute-done.2.w_top_ref, ...), custom_call_target="tpu_custom_call" | custom-call | flops 268435456 | bytes 5242880 | tf_op jit(solution)/shard_map/pallas_call | solution.py:255
  133.4 0.1 shard_map.136
  133.6 2.2 %collective-permute-start.6 = (f32[256,512]{1,0:T(8,128)S(1)}, f32[256,512]{1,0:T(8,128)S(1)}, u32[]{:S(2)}, u32[]{:S(2)}) collective-permute-start(f32[256,512]{1,0:T(8,128)S(1)} %get-tuple-element.15), channel_id=1, source_target_pairs={{0,6},{1,7},{2,4},{3,5},{4,2},{5,3},{6,0},{7,1},{8,14},{9,15},{10,... | collective-permute-start | bytes 1572872 | tf_op jit(solution)/shard_map/ppermute | solution.py:316
  135.7 2.0 %shard_map.132.a_ref = f32[2,256,512]{2,1,0:T(8,128)S(1)} custom-call(s32[1]{0:T(128)} %bitcast.core_ref, f32[2,2,256,1024]{3,2,1,0:T(8,128)S(1)} %shard_map.130.acc_ref, f32[256,512]{1,0:T(8,128)S(1)} %collective-permute-done.top_ref, f32[256,512]{1,0:T(8,128)S(1)} %collective-permute-done.1.bottom_ref, f32[2,512,1024]{2,1,0:T(8,128)} %collective-permute-done.2.w_top_ref, ...), custom_call_target="tpu_custom_call" | custom-call | flops 268435456 | bytes 5242880 | tf_op jit(solution)/shard_map/pallas_call | solution.py:255
  137.7 11.0 %collective-permute-done.6.top_ref = f32[256,512]{1,0:T(8,128)S(1)} collective-permute-done((f32[256,512]{1,0:T(8,128)S(1)}, f32[256,512]{1,0:T(8,128)S(1)}, u32[]{:S(2)}, u32[]{:S(2)}) %collective-permute-start.6) | collective-permute-done | bytes 524320 | tf_op jit(solution)/shard_map/ppermute | solution.py:316
  148.7 0.6 collective-permute-done.7.bottom_ref
  149.3 0.9 shard_map.137
  (20 shorter events, 0.0 us)
Async XLA Ops:
  3.0 60.9 %all-to-all-start = ((f32[32,128,128]{2,1,0:T(8,128)}), f32[32,128,128]{2,1,0:T(8,128)S(1)}, u32[]{:S(2)}, u32[]{:S(2)}) async-start(f32[32,128,128]{2,1,0:T(8,128)} %shard_map.127), calls=%async_computation | async-start | bytes 4194304 | tf_op jit(solution)/shard_map/all_to_all | solution.py:324
  15.3 48.6 %copy-start.2 = (f32[256,256]{1,0:T(8,128)S(1)}, f32[256,256]{1,0:T(8,128)}, u32[]{:S(2)}) copy-start(f32[256,256]{1,0:T(8,128)} %constant.68.clone.second_ref) | copy-start | bytes 786436
  15.3 48.6 %copy-start.3 = (f32[256,256]{1,0:T(8,128)S(1)}, f32[256,256]{1,0:T(8,128)}, u32[]{:S(2)}) copy-start(f32[256,256]{1,0:T(8,128)} %constant.69.clone.inverse_ref) | copy-start | bytes 786436
  15.3 48.6 %copy-start.4 = (f32[256,128]{1,0:T(8,128)S(1)}, f32[256,128]{1,0:T(8,128)}, u32[]{:S(2)}) copy-start(f32[256,128]{1,0:T(8,128)} %constant.67.clone.first_ref) | copy-start | bytes 393220
  15.3 48.6 %copy-start.5 = (f32[128,256]{1,0:T(8,128)S(1)}, f32[128,256]{1,0:T(8,128)}, u32[]{:S(2)}) copy-start(f32[128,256]{1,0:T(8,128)} %constant.70.clone.last_ref) | copy-start | bytes 393220
  15.3 48.6 %copy-start.6 = (f32[128,128]{1,0:T(8,128)S(1)}, f32[128,128]{1,0:T(8,128)}, u32[]{:S(2)}) copy-start(f32[128,128]{1,0:T(8,128)} %constant.71.clone.cos_ref) | copy-start | bytes 196612
  15.4 48.6 %copy-start.7 = (f32[128,128]{1,0:T(8,128)S(1)}, f32[128,128]{1,0:T(8,128)}, u32[]{:S(2)}) copy-start(f32[128,128]{1,0:T(8,128)} %constant.72.clone.sin_ref) | copy-start | bytes 196612
  15.4 48.6 %copy-start.8 = (f32[128,128]{1,0:T(8,128)S(1)}, f32[128,128]{1,0:T(8,128)}, u32[]{:S(2)}) copy-start(f32[128,128]{1,0:T(8,128)} %constant.74.clone.sign_ref) | copy-start | bytes 196612
  15.4 48.6 %copy-start.9 = (f32[2,128]{1,0:T(2,128)S(1)}, f32[2,128]{1,0:T(2,128)}, u32[]{:S(2)}) copy-start(f32[2,128]{1,0:T(2,128)} %constant.73.clone.edge_ref) | copy-start | bytes 3076
  21.1 93.8 %collective-permute-start.2 = (f32[2,512,1024]{2,1,0:T(8,128)}, f32[2,512,1024]{2,1,0:T(8,128)}, u32[]{:S(2)}, u32[]{:S(2)}) collective-permute-start(f32[2,512,1024]{2,1,0:T(8,128)} %get-tuple-element.13), channel_id=1, source_target_pairs={{0,2},{1,3},{2,0},{3,1},{4,6},{5,7},{6,4},{7,5},{8,10},{9,11},{10,... | collective-permute-start | bytes 12582920 | tf_op jit(solution)/shard_map/ppermute | solution.py:315
  22.6 95.0 %collective-permute-start.3 = (f32[2,512,1024]{2,1,0:T(8,128)}, f32[2,512,1024]{2,1,0:T(8,128)}, u32[]{:S(2)}, u32[]{:S(2)}) collective-permute-start(f32[2,512,1024]{2,1,0:T(8,128)} %get-tuple-element.14), channel_id=1, source_target_pairs={{0,6},{1,7},{2,4},{3,5},{4,2},{5,3},{6,0},{7,1},{8,14},{9,15},{10,... | collective-permute-start | bytes 12582920 | tf_op jit(solution)/shard_map/ppermute | solution.py:316
  64.0 41.8 %copy-start.1 = (bf16[512,512]{1,0:T(8,128)(2,1)S(1)}, bf16[512,512]{1,0:T(8,128)(2,1)}, u32[]{:S(2)}) copy-start(bf16[512,512]{1,0:T(8,128)(2,1)} %query_ref.1) | copy-start | bytes 1572868
  106.1 18.2 %collective-permute-start = (f32[256,512]{1,0:T(8,128)S(1)}, f32[256,512]{1,0:T(8,128)S(1)}, u32[]{:S(2)}, u32[]{:S(2)}) collective-permute-start(f32[256,512]{1,0:T(8,128)S(1)} %get-tuple-element.11.top_ref), channel_id=1, source_target_pairs={{0,2},{1,3},{2,0},{3,1},{4,6},{5,7},{6,4},{7,5},{8,10},{9,11},{10,... | collective-permute-start | bytes 1572872 | tf_op jit(solution)/shard_map/ppermute | solution.py:315
  107.7 19.1 %collective-permute-start.1 = (f32[256,512]{1,0:T(8,128)S(1)}, f32[256,512]{1,0:T(8,128)S(1)}, u32[]{:S(2)}, u32[]{:S(2)}) collective-permute-start(f32[256,512]{1,0:T(8,128)S(1)} %get-tuple-element.12.bottom_ref), channel_id=1, source_target_pairs={{0,6},{1,7},{2,4},{3,5},{4,2},{5,3},{6,0},{7,1},{8,14},{9,15},{10,... | collective-permute-start | bytes 1572872 | tf_op jit(solution)/shard_map/ppermute | solution.py:316
  109.9 2.2 %copy-start = (bf16[512,4096]{1,0:T(8,128)(2,1)S(1)}, bf16[512,4096]{1,0:T(8,128)(2,1)}, u32[]{:S(2)}) copy-start(bf16[512,4096]{1,0:T(8,128)(2,1)} %second_ref.2) | copy-start | bytes 12582916
  128.7 4.7 %collective-permute-start.5 = (f32[2,256,512]{2,1,0:T(8,128)S(1)}, f32[2,256,512]{2,1,0:T(8,128)S(1)}, u32[]{:S(2)}, u32[]{:S(2)}) collective-permute-start(f32[2,256,512]{2,1,0:T(8,128)S(1)} %shard_map.135), channel_id=1, source_target_pairs={{0,1},{1,0},{2,3},{3,2},{4,5},{5,4},{6,7},{7,6},{8,9},{9,8},{10,11... | collective-permute-start | bytes 3145736 | tf_op jit(solution)/shard_map/ppermute | solution.py:319
  130.9 6.9 %collective-permute-start.4 = (f32[2,256,512]{2,1,0:T(8,128)S(1)}, f32[2,256,512]{2,1,0:T(8,128)S(1)}, u32[]{:S(2)}, u32[]{:S(2)}) collective-permute-start(f32[2,256,512]{2,1,0:T(8,128)S(1)} %shard_map.133), channel_id=1, source_target_pairs={{0,1},{1,0},{2,3},{3,2},{4,5},{5,4},{6,7},{7,6},{8,9},{9,8},{10,11... | collective-permute-start | bytes 3145736 | tf_op jit(solution)/shard_map/ppermute | solution.py:319
  133.6 15.2 %collective-permute-start.6 = (f32[256,512]{1,0:T(8,128)S(1)}, f32[256,512]{1,0:T(8,128)S(1)}, u32[]{:S(2)}, u32[]{:S(2)}) collective-permute-start(f32[256,512]{1,0:T(8,128)S(1)} %get-tuple-element.15), channel_id=1, source_target_pairs={{0,6},{1,7},{2,4},{3,5},{4,2},{5,3},{6,0},{7,1},{8,14},{9,15},{10,... | collective-permute-start | bytes 1572872 | tf_op jit(solution)/shard_map/ppermute | solution.py:316
  135.7 13.6 %collective-permute-start.7 = (f32[256,512]{1,0:T(8,128)S(1)}, f32[256,512]{1,0:T(8,128)S(1)}, u32[]{:S(2)}, u32[]{:S(2)}) collective-permute-start(f32[256,512]{1,0:T(8,128)S(1)} %get-tuple-element.16), channel_id=1, source_target_pairs={{0,2},{1,3},{2,0},{3,1},{4,6},{5,7},{6,4},{7,5},{8,10},{9,11},{10,... | collective-permute-start | bytes 1572872 | tf_op jit(solution)/shard_map/ppermute | solution.py:315

commit v3 on v2

--- a/solution.py
+++ b/solution.py
@@ -1,3 +1,5 @@
+import functools
+
 import jax
 import jax.numpy as jnp
 import numpy as np
@@ -14,6 +16,8 @@
 SUB = 4
 CHIPS = 4
 BLOCK = 512
+MAIN = 416
+TAIL = 48
 GROUP = 8
 BIG = 56 * 1024 * 1024
 SMALL = 24 * 1024 * 1024
@@ -39,10 +43,12 @@
     last = np.concatenate([weight * np.cos(coarse.T), -weight * np.sin(coarse.T)], 1)
     twist = 2.0 * np.pi * ((k[:, None] * r[None, :]) % TOTAL) / TOTAL
     middle = 2.0 * np.pi * (COARSE * r) / TOTAL
-    edge = np.stack([np.cos(middle), np.sin(middle)], 0)
-    sign = np.broadcast_to(np.where(q % 2 == 0, 1.0, -1.0)[:, None] / TOTAL, (COARSE, LANES))
-    f32 = lambda x: np.ascontiguousarray(x).astype(np.float32)
-    return [f32(t) for t in (first, second, second_inv, last, np.cos(twist), np.sin(twist), edge, sign)]
+    edge = np.tile(np.concatenate([np.cos(middle), np.sin(middle)])[None, :], (8, 1))
+    rows = [
+        np.concatenate([first[:COARSE], first[COARSE:]], 1), second, second_inv, last,
+        np.concatenate([np.cos(twist), np.sin(twist)], 1), edge,
+    ]
+    return np.concatenate(rows, 0).astype(np.float32)
 
 
 def prepare_kernel(key_ref, value_ref, taps_ref, out_ref):
@@ -91,14 +97,24 @@
 
 
 def convolve_kernel(
-    x_ref, first_ref, second_ref, inverse_ref, last_ref, cos_ref, sin_ref, edge_ref, sign_ref,
-    out_ref, edge_out, first, second, inverse, last,
+    x_ref, table_ref, one_ref, two_ref, out_ref, edge_out, first, second, inverse, last,
 ):
-    for ref, table, axis in (
-        (first_ref, first, 1), (second_ref, second, 0), (inverse_ref, inverse, 0), (last_ref, last, 1)
+    ends = np.cumsum([0, COARSE, 2 * LANES, 2 * LANES, COARSE, COARSE, 8])
+    first_at, second_at, inverse_at, last_at, twist_at, edge_at = [
+        slice(int(p), int(q)) for p, q in zip(ends[:-1], ends[1:])
+    ]
+    re_im = table_ref[first_at, :]
+    for values, table, axis in (
+        (jnp.concatenate([re_im[:, :COARSE], re_im[:, COARSE:]], 0), first, 1),
+        (table_ref[second_at, :], second, 0),
+        (table_ref[inverse_at, :], inverse, 0),
+        (table_ref[last_at, :], last, 1),
     ):
-        high, low = split_bf16(ref[...])
+        high, low = split_bf16(values)
         table[...] = jnp.concatenate([high, high, low], axis)
+    odd = lax.broadcasted_iota(jnp.int32, (COARSE, LANES), 0) % 2
+    sign = jnp.where(odd == 0, 1.0 / TOTAL, -1.0 / TOTAL)
+    edge = table_ref[edge_at, :][:1]
 
     def add_pair(i, total):
         at = pl.multiple_of(i * (4 * OWN), 4 * OWN)
@@ -107,7 +123,7 @@
     half = lax.fori_loop(
         0, COARSE // 2, add_pair, jnp.zeros((2 * OWN, LANES), jnp.float32), unroll=8
     )
-    edge_cos, edge_sin = edge_ref[0:1, :], edge_ref[1:2, :]
+    edge_cos, edge_sin = edge[:, :LANES], edge[:, LANES:]
     spectrum = rows_by(jnp.concatenate([half * edge_cos, -half * edge_sin], 1), second[...])
     back = rows_by(multiply(spectrum[:OWN], spectrum[OWN:]), inverse[...])
     edge_out[...] = back[:, :LANES] * edge_cos - back[:, LANES:] * edge_sin
@@ -119,7 +135,7 @@
             for j in range(GROUP) for s in range(2)
         ]
         y = by_columns(first[...], jnp.concatenate(streams, 1))
-        cos, sin = cos_ref[...], sin_ref[...]
+        cos, sin = table_ref[twist_at, :LANES], table_ref[twist_at, LANES:]
         turned = []
         for j in range(2 * GROUP):
             yr = y[:COARSE, j * LANES:(j + 1) * LANES]
@@ -140,7 +156,7 @@
             columns.append(jnp.concatenate([ur * cos - ui * sin, ur * sin + ui * cos], 0))
         result = by_columns(last[...], jnp.concatenate(columns, 1))
         for j in range(GROUP):
-            extra = sign_ref[...] * edge_out[pl.ds(c0 + j, 1), :]
+            extra = sign * edge_out[pl.ds(c0 + j, 1), :]
             out_ref[pl.ds(c0 + j, COARSE, stride=OWN), :] = (
                 result[:, j * LANES:(j + 1) * LANES] + extra
             )
@@ -149,10 +165,10 @@
     lax.fori_loop(0, OWN // GROUP, some_channels, 0)
 
 
-def convolve(x):
-    consts = [jnp.asarray(t) for t in tables()]
+def convolve(x, *before):
     return pl.pallas_call(
         convolve_kernel,
+        in_specs=[pl.BlockSpec()] * 2 + [pl.BlockSpec(memory_space=pltpu.VMEM)] * 2,
         out_shape=jax.ShapeDtypeStruct((COARSE * OWN, LANES), jnp.float32),
         scratch_shapes=[
             pltpu.VMEM((OWN, LANES), jnp.float32),
@@ -163,35 +179,64 @@
         ],
         compiler_params=pltpu.CompilerParams(vmem_limit_bytes=SMALL),
         cost_estimate=pl.CostEstimate(flops=4 << 30, bytes_accessed=4 << 20, transcendentals=0),
-    )(x, *consts)
-
-
-def widen_kernel(where_ref, both_ref, first_ref, second_ref, one_ref, two_ref):
-    both = both_ref[...].astype(jnp.float32)
-    one_ref[0], one_ref[1] = both, first_ref[...].astype(jnp.float32)
-    two_ref[0], two_ref[1] = both, second_ref[...].astype(jnp.float32)
+    )(x, jnp.asarray(tables()), *before)
+
+
+def widen_kernel(where_ref, w_ref, one_tail, two_tail, one_main, two_main):
+    quarter = one_main.shape[2]
+    main = pl.ds(0, MAIN)
+    tail = pl.ds(pl.multiple_of(MAIN + where_ref[3] * TAIL, 16), TAIL)
+    for rows, one_ref, two_ref in ((tail, one_tail, two_tail), (main, one_main, two_main)):
+        for n, refs in enumerate(((one_ref.at[0], two_ref.at[0]), (one_ref.at[1],), (two_ref.at[1],))):
+            at = pl.ds(pl.multiple_of(where_ref[n] * quarter, quarter), quarter)
+            wide = w_ref[rows, at].astype(jnp.float32)
+            for ref in refs:
+                ref[...] = wide
 
 
 def widen(w_out, where):
-    channels, width = w_out.shape
-    quarter = width // CHIPS
-    steps = 2
-    rows = channels // steps
-    column = lambda n: pl.BlockSpec((rows, quarter), lambda i, where: (i, where[n]))
-    out = pl.BlockSpec((2, rows, quarter), lambda i, where: (0, i, 0))
-    shape = jax.ShapeDtypeStruct((2, channels, quarter), jnp.float32)
+    quarter = w_out.shape[1] // CHIPS
+    tail = jax.ShapeDtypeStruct((2, TAIL, quarter), jnp.float32)
+    main = jax.ShapeDtypeStruct((2, MAIN, quarter), jnp.float32)
+    in_vmem = pl.BlockSpec(memory_space=pltpu.VMEM)
     return pl.pallas_call(
         widen_kernel,
+        in_specs=[pl.BlockSpec(memory_space=pltpu.SMEM), in_vmem],
+        out_specs=(in_vmem,) * 4,
+        out_shape=(tail, tail, main, main),
+        compiler_params=pltpu.CompilerParams(vmem_limit_bytes=SMALL),
+        cost_estimate=pl.CostEstimate(flops=0, bytes_accessed=11 << 20, transcendentals=0),
+    )(where, w_out)
+
+
+def narrow_kernel(mine_ref, one_main, two_main, one_tail, two_tail, one_far, two_far, one_out, two_out):
+    mine = pl.ds(pl.multiple_of(MAIN + mine_ref[0] * TAIL, 16), TAIL)
+    theirs = pl.ds(pl.multiple_of(MAIN + (1 - mine_ref[0]) * TAIL, 16), TAIL)
+    for main, tail, far, out in (
+        (one_main, one_tail, one_far, one_out), (two_main, two_tail, two_far, two_out)
+    ):
+        out[:MAIN, :] = main[...].astype(jnp.bfloat16)
+        out[mine, :] = tail[...].astype(jnp.bfloat16)
+        out[theirs, :] = far[...].astype(jnp.bfloat16)
+
+
+def narrow(mine, *parts):
+    quarter = parts[0].shape[2]
+    block = lambda rows: pl.BlockSpec((None, rows, quarter), lambda i, mine: (i, 0, 0))
+    channels = MAIN + 2 * TAIL
+    shape = jax.ShapeDtypeStruct((2, channels, quarter), jnp.bfloat16)
+    return pl.pallas_call(
+        narrow_kernel,
         grid_spec=pltpu.PrefetchScalarGridSpec(
             num_scalar_prefetch=1,
-            grid=(steps,),
-            in_specs=[column(0), column(1), column(2)],
-            out_specs=(out, out),
+            grid=(2,),
+            in_specs=[block(MAIN)] * 2 + [block(TAIL)] * 4,
+            out_specs=(block(channels), block(channels)),
         ),
         out_shape=(shape, shape),
-        compiler_params=pltpu.CompilerParams(vmem_limit_bytes=BIG),
-        cost_estimate=pl.CostEstimate(flops=0, bytes_accessed=11 << 20, transcendentals=0),
-    )(where, w_out, w_out, w_out)
+        compiler_params=pltpu.CompilerParams(vmem_limit_bytes=SMALL),
+        cost_estimate=pl.CostEstimate(flops=0, bytes_accessed=12 << 20, transcendentals=0),
+    )(mine, *parts)
 
 
 def gate_kernel(conv_ref, query_ref, top_ref, bottom_ref):
@@ -238,40 +283,30 @@
     )(where, top, bottom, w_out)
 
 
-def add_kernel(core_ref, acc_ref, top_ref, bottom_ref, w_top_ref, w_bottom_ref, out_ref):
-    for i, (gated, w) in enumerate(((top_ref, w_top_ref), (bottom_ref, w_bottom_ref))):
-        out_ref[i] = acc_ref[i] + dot(
-            gated[...].astype(jnp.bfloat16), w[...].astype(jnp.bfloat16)
-        )
-
-
-def add_partner(acc, top, bottom, w_top, w_bottom, which, parity):
-    rows, channels = top.shape
-    steps = 2
-    columns = BLOCK // steps
-    at = lambda n, parity: parity[0] * steps + n
-    whole = pl.BlockSpec((rows, channels), lambda n, parity: (0, 0))
-    weights = pl.BlockSpec((None, channels, columns), lambda n, parity: (which, 0, at(n, parity)))
-    return pl.pallas_call(
-        add_kernel,
-        grid_spec=pltpu.PrefetchScalarGridSpec(
-            num_scalar_prefetch=1,
-            grid=(steps,),
-            in_specs=[
-                pl.BlockSpec(
-                    (None, 2, rows, columns), lambda n, parity: (which, 0, 0, at(n, parity))
-                ),
-                whole,
-                whole,
-                weights,
-                weights,
-            ],
-            out_specs=pl.BlockSpec((2, rows, columns), lambda n, parity: (0, 0, n)),
+def add_kernel(jobs, core_ref, acc_ref, top_ref, bottom_ref, w_top_ref, w_bottom_ref, *out_refs):
+    for (which, own), out_ref in zip(jobs, out_refs):
+        parity = core_ref[0] if own else 1 - core_ref[0]
+        at = pl.ds(pl.multiple_of(parity * BLOCK, BLOCK), BLOCK)
+        for i, (gated, w) in enumerate(((top_ref, w_top_ref), (bottom_ref, w_bottom_ref))):
+            out_ref[i] = acc_ref[which, i, :, at] + dot(
+                gated[...].astype(jnp.bfloat16), w[which, :, at]
+            )
+
+
+def add_partner(core, acc, top, bottom, w_top, w_bottom, jobs):
+    rows = top.shape[0]
+    shape = jax.ShapeDtypeStruct((2, rows, BLOCK), jnp.float32)
+    return pl.pallas_call(
+        functools.partial(add_kernel, jobs),
+        in_specs=[pl.BlockSpec(memory_space=pltpu.SMEM)]
+        + [pl.BlockSpec(memory_space=pltpu.VMEM)] * 5,
+        out_specs=tuple(pl.BlockSpec(memory_space=pltpu.VMEM) for _ in jobs),
+        out_shape=tuple(shape for _ in jobs),
+        compiler_params=pltpu.CompilerParams(vmem_limit_bytes=SMALL),
+        cost_estimate=pl.CostEstimate(
+            flops=len(jobs) << 28, bytes_accessed=len(jobs) << 22, transcendentals=0
         ),
-        out_shape=jax.ShapeDtypeStruct((2, rows, BLOCK), jnp.float32),
-        compiler_params=pltpu.CompilerParams(vmem_limit_bytes=SMALL),
-        cost_estimate=pl.CostEstimate(flops=1 << 28, bytes_accessed=5 << 20, transcendentals=0),
-    )(parity, acc, top, bottom, w_top, w_bottom)
+    )(core, acc, top, bottom, w_top, w_bottom)
 
 
 def sum_kernel(a_ref, b_ref, top_ref, bottom_ref):
@@ -319,23 +354,33 @@
     send_core = lambda x: lax.ppermute(x, "chan", [(i, i ^ 1) for i in range(size)])
 
     sent = prepare(key_stream, value, long_filter)
-    wide_one, wide_two = widen(w_out, jnp.stack([opposite, one, two]))
-    w_one, w_two = send_one(wide_one), send_two(wide_two)
+    side = lax.axis_index("seq") % 2
+    send_side = lambda x: lax.ppermute(x, "seq", [(i, i ^ 1) for i in range(PEERS)])
+    wide = widen(w_out, jnp.stack([opposite, one, two, side]))
+    near_one, near_two = send_one(wide[0]), send_two(wide[1])
+    main_one, main_two = send_one(wide[2]), send_two(wide[3])
+    far_one, far_two = send_side(near_one), send_side(near_two)
     moved = lax.all_to_all(sent, "seq", split_axis=0, concat_axis=0, tiled=True)
-    conv = convolve(moved.reshape(PEERS * 2 * SUB * OWN, LANES))
+    conv = convolve(moved.reshape(PEERS * 2 * SUB * OWN, LANES), far_one, far_two)
     home = lax.all_to_all(
         conv.reshape(PEERS, SUB * OWN, LANES), "seq", split_axis=0, concat_axis=0, tiled=True
     )
     top, bottom = gate(home, query)
     top_one, bottom_two = send_one(top), send_two(bottom)
     acc = own_part(top, bottom, w_out, jnp.stack([two, one, chip, chip]))
-    mine, theirs = core.reshape(1), (1 - core).reshape(1)
-    add = lambda which, parity: add_partner(
-        acc, top_one, bottom_two, w_one, w_two, which, parity
-    )
-    away_top, away_bottom = sum_cores(add(0, mine), send_core(add(0, theirs)))
+    narrow_one, narrow_two = narrow(
+        side.reshape(1), main_one, main_two, near_one, near_two, far_one, far_two
+    )
+    add = lambda *jobs: add_partner(
+        core.reshape(1), acc, top_one, bottom_two, narrow_one, narrow_two, jobs
+    )
+    other, own = 0, 1
+    (away_sent,) = add((other, False))
+    away_kept, here_sent = add((other, True), (own, False))
+    away_top, away_bottom = sum_cores(away_kept, send_core(away_sent))
     from_two, from_one = send_two(away_top), send_one(away_bottom)
-    return last_sum(add(1, mine), send_core(add(1, theirs)), from_two, from_one)
+    (here_kept,) = add((own, True))
+    return last_sum(here_kept, send_core(here_sent), from_two, from_one)
 
 
 def solution(mesh):

time: 151 us -> 142 us (0.940)
  waiting for transfers between devices: 62.9 us -> 54.4 us
  Pallas kernels: 28.7 us -> 23.7 us
  local copies, waits for them, and re-layouts: 2.24 us -> 6.26 us
  starting transfers between devices: 21.8 us -> 23.6 us
    all_to_all x1, waiting for transfers between devices: 39.2 us -> 2.17 us  [shards(): moved = lax.all_to_all(sent, 'seq', split_axis=0, concat_axis=0, tiled=True)]
    ppermute x0 -> x2, waiting for transfers between devices: none -> 25.2 us  [shards(): lax.ppermute(x, 'seq', [(i, i ^ 1) for i in range(PEERS)])]
    pallas_call x6, Pallas kernels: 21.8 us -> 16.9 us  [the longest x1 8.06 us: convolve(): pl.pallas_call(convolve_kernel, in_specs=[pl.BlockSpec()] * 2 + [pl.Block...]
    unnamed x20 -> x14, local copies, waits for them, and re-layouts: 2.24 us -> 6.26 us
    ppermute x3 -> x4, waiting for transfers between devices: 16.1 us -> 17.5 us  [shards(): lax.ppermute(x, 'chan', [(i, (i - 2 if i // 2 % 2 == 0 else i + 2) % size...]
    ppermute x3 -> x4, starting transfers between devices: 6.38 us -> 6.98 us  [shards(): lax.ppermute(x, 'chan', [(i, (i - 2 if i // 2 % 2 == 0 else i + 2) % size...]
    ppermute x3 -> x4, starting transfers between devices: 3.07 us -> 3.66 us  [shards(): lax.ppermute(x, 'chan', [(i, i ^ 2) for i in range(size)])]
    ppermute x3 -> x4, waiting for transfers between devices: 7.59 us -> 8.13 us  [shards(): lax.ppermute(x, 'chan', [(i, i ^ 2) for i in range(size)])]
  transfers between devices with their start and end apart: 9 -> 13, of which waited for: 7 -> 10; matrix products, arithmetic and copies ran while one was open for 0% -> 0% of each run, Pallas kernels for 15% -> 14%
where the time goes in v3:
time: 142 us
  waiting for transfers between devices  54.4 us (38%)
  blocking collectives  33.7 us (24%)
  Pallas kernels  23.7 us (17%)
  starting transfers between devices  23.6 us (17%)
  local copies, waits for them, and re-layouts  6.26 us (4%)
    all_to_all x1, blocking collectives, shards(): lax.all_to_all(conv.reshape(PEERS, SUB * OWN, LANES), 'seq', split_axis=0...  33.7 us
    ppermute x2, waiting for transfers between devices, shards(): lax.ppermute(x, 'seq', [(i, i ^ 1) for i in range(PEERS)])  25.2 us
    ppermute x4, waiting for transfers between devices, shards(): lax.ppermute(x, 'chan', [(i, (i - 2 if i // 2 % 2 == 0 else i + 2) % size...  17.5 us
    all_to_all x1, starting transfers between devices, shards(): moved = lax.all_to_all(sent, 'seq', split_axis=0, concat_axis=0, tiled=True)  11.7 us
    ppermute x4, waiting for transfers between devices, shards(): lax.ppermute(x, 'chan', [(i, i ^ 2) for i in range(size)])  8.13 us
    pallas_call x1, Pallas kernels, convolve(): pl.pallas_call(convolve_kernel, in_specs=[pl.BlockSpec()] * 2 + [pl.Block...  8.06 us
    ppermute x4, starting transfers between devices, shards(): lax.ppermute(x, 'chan', [(i, (i - 2 if i // 2 % 2 == 0 else i + 2) % size...  6.98 us
    unnamed x14, local copies, waits for them, and re-layouts  6.26 us
  transfers between devices with their start and end apart: 13, of which 10 were waited for; matrix products, arithmetic and copies ran while one was open for 0% of the time, Pallas kernels for 14%

profile of v3, /device:TPU:8, one launch (start us, length us, event | category | flops | bytes accessed | tf_op | source)
XLA Modules:
  0.0 142.1 jit_solution(9576511279786672109)
XLA Ops:
  0.0 2.9 %shard_map.64 = f32[32,128,128]{2,1,0:T(8,128)} custom-call(bf16[512,512]{1,0:T(8,128)(2,1)} %key_ref.1, bf16[512,512]{1,0:T(8,128)(2,1)} %value_ref.1, f32[512,512]{1,0:T(8,128)} %taps_ref.1), custom_call_target="tpu_custom_call" | custom-call | bytes 4194304 | tf_op jit(solution)/shard_map/pallas_call | solution.py:69
  2.9 11.7 %all-to-all-start = ((f32[32,128,128]{2,1,0:T(8,128)}), f32[32,128,128]{2,1,0:T(8,128)S(1)}, u32[]{:S(2)}, u32[]{:S(2)}) async-start(f32[32,128,128]{2,1,0:T(8,128)} %shard_map.64), calls=%async_computation | async-start | bytes 4194304 | tf_op jit(solution)/shard_map/all_to_all | solution.py:363
  14.7 2.2 %copy-done = bf16[512,4096]{1,0:T(8,128)(2,1)S(1)} copy-done((bf16[512,4096]{1,0:T(8,128)(2,1)S(1)}, bf16[512,4096]{1,0:T(8,128)(2,1)}, u32[]{:S(2)}) %copy-start) | copy-done | bytes 4194328
  16.9 3.8 %shard_map.65 = (f32[2,48,1024]{2,1,0:T(8,128)S(1)}, f32[2,48,1024]{2,1,0:T(8,128)S(1)}, f32[2,416,1024]{2,1,0:T(8,128)}, f32[2,416,1024]{2,1,0:T(8,128)}) custom-call(s32[4]{0:T(128)S(1)} %pad_add_fusion.1.where_ref, bf16[512,4096]{1,0:T(8,128)(2,1)S(1)} %copy-done), custom_call_target="tpu_custom_call" | custom-call | bytes 11534336 | tf_op jit(solution)/shard_map/pallas_call | solution.py:202
  20.7 1.5 %collective-permute-start = (f32[2,48,1024]{2,1,0:T(8,128)S(1)}, f32[2,48,1024]{2,1,0:T(8,128)S(1)}, u32[]{:S(2)}, u32[]{:S(2)}) collective-permute-start(f32[2,48,1024]{2,1,0:T(8,128)S(1)} %get-tuple-element.17), channel_id=1, source_target_pairs={{0,2},{1,3},{2,0},{3,1},{4,6},{5,7},{6,4},{7,5},{8,10},{9,11},{10,... | collective-permute-start | bytes 1179656 | tf_op jit(solution)/shard_map/ppermute | solution.py:350
  22.2 2.1 %collective-permute-start.2 = (f32[2,48,1024]{2,1,0:T(8,128)S(1)}, f32[2,48,1024]{2,1,0:T(8,128)S(1)}, u32[]{:S(2)}, u32[]{:S(2)}) collective-permute-start(f32[2,48,1024]{2,1,0:T(8,128)S(1)} %get-tuple-element.18), channel_id=1, source_target_pairs={{0,6},{1,7},{2,4},{3,5},{4,2},{5,3},{6,0},{7,1},{8,14},{9,15},{10,... | collective-permute-start | bytes 1179656 | tf_op jit(solution)/shard_map/ppermute | solution.py:351
  24.3 0.6 collective-permute-start.6
  24.9 0.6 collective-permute-start.7
  25.5 7.3 %collective-permute-done.one_tail = f32[2,48,1024]{2,1,0:T(8,128)S(1)} collective-permute-done((f32[2,48,1024]{2,1,0:T(8,128)S(1)}, f32[2,48,1024]{2,1,0:T(8,128)S(1)}, u32[]{:S(2)}, u32[]{:S(2)}) %collective-permute-start) | collective-permute-done | bytes 393248 | tf_op jit(solution)/shard_map/ppermute | solution.py:350
  33.0 2.5 %collective-permute-done.2.two_tail = f32[2,48,1024]{2,1,0:T(8,128)S(1)} collective-permute-done((f32[2,48,1024]{2,1,0:T(8,128)S(1)}, f32[2,48,1024]{2,1,0:T(8,128)S(1)}, u32[]{:S(2)}, u32[]{:S(2)}) %collective-permute-start.2) | collective-permute-done | bytes 393248 | tf_op jit(solution)/shard_map/ppermute | solution.py:351
  35.7 13.4 %collective-permute-done.1.one_ref.one_far = f32[2,48,1024]{2,1,0:T(8,128)S(1)} collective-permute-done((f32[2,48,1024]{2,1,0:T(8,128)S(1)}, f32[2,48,1024]{2,1,0:T(8,128)S(1)}, u32[]{:S(2)}, u32[]{:S(2)}) %collective-permute-start.1) | collective-permute-done | bytes 393248 | tf_op jit(solution)/shard_map/ppermute | solution.py:358
  49.1 11.8 %collective-permute-done.3.two_ref.two_far = f32[2,48,1024]{2,1,0:T(8,128)S(1)} collective-permute-done((f32[2,48,1024]{2,1,0:T(8,128)S(1)}, f32[2,48,1024]{2,1,0:T(8,128)S(1)}, u32[]{:S(2)}, u32[]{:S(2)}) %collective-permute-start.3) | collective-permute-done | bytes 393248 | tf_op jit(solution)/shard_map/ppermute | solution.py:358
  60.9 0.7 copy-done.3
  61.6 2.2 %all-to-all-done = f32[32,128,128]{2,1,0:T(8,128)S(1)} async-done(((f32[32,128,128]{2,1,0:T(8,128)}), f32[32,128,128]{2,1,0:T(8,128)S(1)}, u32[]{:S(2)}, u32[]{:S(2)}) %all-to-all-start) | async-done | bytes 2097184 | tf_op jit(solution)/shard_map/all_to_all | solution.py:363
  63.8 1.0 copy-done.4
  64.8 1.2 copy-done.6
  66.0 8.1 %shard_map.66 = f32[2048,128]{1,0:T(8,128)S(1)} custom-call(f32[4096,128]{1,0:T(8,128)S(1)} %bitcast.8, f32[904,256]{1,0:T(8,128)S(1)} %copy-done.6, f32[2,48,1024]{2,1,0:T(8,128)S(1)} %collective-permute-done.1.one_ref.one_far, f32[2,48,1024]{2,1,0:T(8,128)S(1)} %copy-done.4), custom_call_target="tpu_custom_call" | custom-call | flops 4294967296 | bytes 4194304 | tf_op jit(solution)/shard_map/pallas_call | solution.py:169
  74.1 33.7 %all_to_all.10.conv_ref = f32[32,64,128]{2,1,0:T(8,128)S(1)} all-to-all(f32[32,64,128]{2,1,0:T(8,128)S(1)} %bitcast.9), channel_id=1, replica_groups=mesh['seq'=32,'chan'=8] {'seq'}, dimensions={0} | all-to-all | bytes 2097152 | tf_op jit(solution)/shard_map/all_to_all | solution.py:365
  108.1 1.6 %collective-permute-start.4 = (f32[256,512]{1,0:T(8,128)S(1)}, f32[256,512]{1,0:T(8,128)S(1)}, u32[]{:S(2)}, u32[]{:S(2)}) collective-permute-start(f32[256,512]{1,0:T(8,128)S(1)} %get-tuple-element.19.top_ref), channel_id=1, source_target_pairs={{0,2},{1,3},{2,0},{3,1},{4,6},{5,7},{6,4},{7,5},{8,10},{9,11},{10,... | collective-permute-start | bytes 1572872 | tf_op jit(solution)/shard_map/ppermute | solution.py:350
  109.7 2.1 %collective-permute-start.5 = (f32[256,512]{1,0:T(8,128)S(1)}, f32[256,512]{1,0:T(8,128)S(1)}, u32[]{:S(2)}, u32[]{:S(2)}) collective-permute-start(f32[256,512]{1,0:T(8,128)S(1)} %get-tuple-element.20.bottom_ref), channel_id=1, source_target_pairs={{0,6},{1,7},{2,4},{3,5},{4,2},{5,3},{6,0},{7,1},{8,14},{9,15},{10,... | collective-permute-start | bytes 1572872 | tf_op jit(solution)/shard_map/ppermute | solution.py:351
  111.9 1.1 copy-done.5
  113.0 3.4 %shard_map.69 = (bf16[2,512,1024]{2,1,0:T(8,128)(2,1)S(1)}, bf16[2,512,1024]{2,1,0:T(8,128)(2,1)S(1)}) custom-call(s32[1]{0:T(128)} %bitcast.6.mine_ref, f32[2,416,1024]{2,1,0:T(8,128)} %collective-permute-done.6.one_main, f32[2,416,1024]{2,1,0:T(8,128)} %collective-permute-done.7.two_main, f32[2,48,1024]{2,1,0:T(8,128)S(1)} %collective-permute-done.one_tail, ...), custom_call_target="tpu_custom_call" | custom-call | bytes 12582912 | tf_op jit(solution)/shard_map/pallas_call | solution.py:228
  116.5 2.6 %shard_map.68.acc_ref = f32[2,2,256,1024]{3,2,1,0:T(8,128)S(1)} custom-call(s32[4]{0:T(128)S(1)} %pad_add_fusion.where_ref, f32[256,512]{1,0:T(8,128)S(1)} %get-tuple-element.19.top_ref, f32[256,512]{1,0:T(8,128)S(1)} %get-tuple-element.20.bottom_ref, bf16[512,4096]{1,0:T(8,128)(2,1)S(1)} %copy-done.1), custom_call_target="tpu_custom_call" | custom-call | flops 1073741824 | bytes 8388608 | tf_op jit(solution)/shard_map/pallas_call | solution.py:272
  119.3 2.4 %collective-permute-done.5.bottom_ref = f32[256,512]{1,0:T(8,128)S(1)} collective-permute-done((f32[256,512]{1,0:T(8,128)S(1)}, f32[256,512]{1,0:T(8,128)S(1)}, u32[]{:S(2)}, u32[]{:S(2)}) %collective-permute-start.5) | collective-permute-done | bytes 524320 | tf_op jit(solution)/shard_map/ppermute | solution.py:351
  121.8 0.4 shard_map.72
  122.5 0.7 shard_map.71
  123.3 0.6 collective-permute-start.8
  123.8 1.3 collective-permute-done.9.b_ref
  125.3 2.2 %collective-permute-start.10 = (f32[256,512]{1,0:T(8,128)S(1)}, f32[256,512]{1,0:T(8,128)S(1)}, u32[]{:S(2)}, u32[]{:S(2)}) collective-permute-start(f32[256,512]{1,0:T(8,128)S(1)} %get-tuple-element.27), channel_id=1, source_target_pairs={{0,6},{1,7},{2,4},{3,5},{4,2},{5,3},{6,0},{7,1},{8,14},{9,15},{10,... | collective-permute-start | bytes 1572872 | tf_op jit(solution)/shard_map/ppermute | solution.py:351
  127.9 12.6 %collective-permute-done.10.top_ref = f32[256,512]{1,0:T(8,128)S(1)} collective-permute-done((f32[256,512]{1,0:T(8,128)S(1)}, f32[256,512]{1,0:T(8,128)S(1)}, u32[]{:S(2)}, u32[]{:S(2)}) %collective-permute-start.10) | collective-permute-done | bytes 524320 | tf_op jit(solution)/shard_map/ppermute | solution.py:351
  140.5 0.6 collective-permute-done.11.bottom_ref
  141.1 0.9 shard_map.74
  (22 shorter events, 2.1 us)
Async XLA Ops:
  2.9 60.9 %all-to-all-start = ((f32[32,128,128]{2,1,0:T(8,128)}), f32[32,128,128]{2,1,0:T(8,128)S(1)}, u32[]{:S(2)}, u32[]{:S(2)}) async-start(f32[32,128,128]{2,1,0:T(8,128)} %shard_map.64), calls=%async_computation | async-start | bytes 4194304 | tf_op jit(solution)/shard_map/all_to_all | solution.py:363
  14.7 2.2 %copy-start = (bf16[512,4096]{1,0:T(8,128)(2,1)S(1)}, bf16[512,4096]{1,0:T(8,128)(2,1)}, u32[]{:S(2)}) copy-start(bf16[512,4096]{1,0:T(8,128)(2,1)} %w_ref.3) | copy-start | bytes 12582916
  20.7 12.1 %collective-permute-start = (f32[2,48,1024]{2,1,0:T(8,128)S(1)}, f32[2,48,1024]{2,1,0:T(8,128)S(1)}, u32[]{:S(2)}, u32[]{:S(2)}) collective-permute-start(f32[2,48,1024]{2,1,0:T(8,128)S(1)} %get-tuple-element.17), channel_id=1, source_target_pairs={{0,2},{1,3},{2,0},{3,1},{4,6},{5,7},{6,4},{7,5},{8,10},{9,11},{10,... | collective-permute-start | bytes 1179656 | tf_op jit(solution)/shard_map/ppermute | solution.py:350
  22.2 13.3 %collective-permute-start.2 = (f32[2,48,1024]{2,1,0:T(8,128)S(1)}, f32[2,48,1024]{2,1,0:T(8,128)S(1)}, u32[]{:S(2)}, u32[]{:S(2)}) collective-permute-start(f32[2,48,1024]{2,1,0:T(8,128)S(1)} %get-tuple-element.18), channel_id=1, source_target_pairs={{0,6},{1,7},{2,4},{3,5},{4,2},{5,3},{6,0},{7,1},{8,14},{9,15},{10,... | collective-permute-start | bytes 1179656 | tf_op jit(solution)/shard_map/ppermute | solution.py:351
  24.3 87.6 %collective-permute-start.6 = (f32[2,416,1024]{2,1,0:T(8,128)}, f32[2,416,1024]{2,1,0:T(8,128)}, u32[]{:S(2)}, u32[]{:S(2)}) collective-permute-start(f32[2,416,1024]{2,1,0:T(8,128)} %get-tuple-element.21), channel_id=1, source_target_pairs={{0,2},{1,3},{2,0},{3,1},{4,6},{5,7},{6,4},{7,5},{8,10},{9,11},{10,... | collective-permute-start | bytes 10223624 | tf_op jit(solution)/shard_map/ppermute | solution.py:350
  24.9 87.0 %collective-permute-start.7 = (f32[2,416,1024]{2,1,0:T(8,128)}, f32[2,416,1024]{2,1,0:T(8,128)}, u32[]{:S(2)}, u32[]{:S(2)}) collective-permute-start(f32[2,416,1024]{2,1,0:T(8,128)} %get-tuple-element.22), channel_id=1, source_target_pairs={{0,6},{1,7},{2,4},{3,5},{4,2},{5,3},{6,0},{7,1},{8,14},{9,15},{10,... | collective-permute-start | bytes 10223624 | tf_op jit(solution)/shard_map/ppermute | solution.py:351
  32.8 16.3 %collective-permute-start.1 = (f32[2,48,1024]{2,1,0:T(8,128)S(1)}, f32[2,48,1024]{2,1,0:T(8,128)S(1)}, u32[]{:S(2)}, u32[]{:S(2)}) collective-permute-start(f32[2,48,1024]{2,1,0:T(8,128)S(1)} %collective-permute-done.one_tail), channel_id=1, source_target_pairs={{0,8},{8,0},{16,24},{24,16},{32,40},{40,32},{48,56},{56,48},{64,72... | collective-permute-start | bytes 1179656 | tf_op jit(solution)/shard_map/ppermute | solution.py:358
  35.5 25.4 %collective-permute-start.3 = (f32[2,48,1024]{2,1,0:T(8,128)S(1)}, f32[2,48,1024]{2,1,0:T(8,128)S(1)}, u32[]{:S(2)}, u32[]{:S(2)}) collective-permute-start(f32[2,48,1024]{2,1,0:T(8,128)S(1)} %collective-permute-done.2.two_tail), channel_id=1, source_target_pairs={{0,8},{8,0},{16,24},{24,16},{32,40},{40,32},{48,56},{56,48},{64,72... | collective-permute-start | bytes 1179656 | tf_op jit(solution)/shard_map/ppermute | solution.py:358
  60.9 0.7 copy-start.3
  63.8 1.0 copy-start.4
  64.8 1.2 copy-start.6
  66.0 41.8 %copy-start.2 = (bf16[512,512]{1,0:T(8,128)(2,1)S(1)}, bf16[512,512]{1,0:T(8,128)(2,1)}, u32[]{:S(2)}) copy-start(bf16[512,512]{1,0:T(8,128)(2,1)} %query_ref.1) | copy-start | bytes 1572868
  108.1 11.2 %collective-permute-start.4 = (f32[256,512]{1,0:T(8,128)S(1)}, f32[256,512]{1,0:T(8,128)S(1)}, u32[]{:S(2)}, u32[]{:S(2)}) collective-permute-start(f32[256,512]{1,0:T(8,128)S(1)} %get-tuple-element.19.top_ref), channel_id=1, source_target_pairs={{0,2},{1,3},{2,0},{3,1},{4,6},{5,7},{6,4},{7,5},{8,10},{9,11},{10,... | collective-permute-start | bytes 1572872 | tf_op jit(solution)/shard_map/ppermute | solution.py:350
  109.7 12.0 %collective-permute-start.5 = (f32[256,512]{1,0:T(8,128)S(1)}, f32[256,512]{1,0:T(8,128)S(1)}, u32[]{:S(2)}, u32[]{:S(2)}) collective-permute-start(f32[256,512]{1,0:T(8,128)S(1)} %get-tuple-element.20.bottom_ref), channel_id=1, source_target_pairs={{0,6},{1,7},{2,4},{3,5},{4,2},{5,3},{6,0},{7,1},{8,14},{9,15},{10,... | collective-permute-start | bytes 1572872 | tf_op jit(solution)/shard_map/ppermute | solution.py:351
  111.9 4.6 %copy-start.1 = (bf16[512,4096]{1,0:T(8,128)(2,1)S(1)}, bf16[512,4096]{1,0:T(8,128)(2,1)}, u32[]{:S(2)}) copy-start(bf16[512,4096]{1,0:T(8,128)(2,1)} %w_ref.3) | copy-start | bytes 12582916
  111.9 1.1 copy-start.5
  122.2 2.9 %collective-permute-start.9 = (f32[2,256,512]{2,1,0:T(8,128)S(1)}, f32[2,256,512]{2,1,0:T(8,128)S(1)}, u32[]{:S(2)}, u32[]{:S(2)}) collective-permute-start(f32[2,256,512]{2,1,0:T(8,128)S(1)} %shard_map.72), channel_id=1, source_target_pairs={{0,1},{1,0},{2,3},{3,2},{4,5},{5,4},{6,7},{7,6},{8,9},{9,8},{10,11... | collective-permute-start | bytes 3145736 | tf_op jit(solution)/shard_map/ppermute | solution.py:354
  123.3 4.6 %collective-permute-start.8 = (f32[2,256,512]{2,1,0:T(8,128)S(1)}, f32[2,256,512]{2,1,0:T(8,128)S(1)}, u32[]{:S(2)}, u32[]{:S(2)}) collective-permute-start(f32[2,256,512]{2,1,0:T(8,128)S(1)} %get-tuple-element.25), channel_id=1, source_target_pairs={{0,1},{1,0},{2,3},{3,2},{4,5},{5,4},{6,7},{7,6},{8,9},{9,8},{10,11... | collective-permute-start | bytes 3145736 | tf_op jit(solution)/shard_map/ppermute | solution.py:354
  125.3 15.3 %collective-permute-start.10 = (f32[256,512]{1,0:T(8,128)S(1)}, f32[256,512]{1,0:T(8,128)S(1)}, u32[]{:S(2)}, u32[]{:S(2)}) collective-permute-start(f32[256,512]{1,0:T(8,128)S(1)} %get-tuple-element.27), channel_id=1, source_target_pairs={{0,6},{1,7},{2,4},{3,5},{4,2},{5,3},{6,0},{7,1},{8,14},{9,15},{10,... | collective-permute-start | bytes 1572872 | tf_op jit(solution)/shard_map/ppermute | solution.py:351
  127.4 13.7 %collective-permute-start.11 = (f32[256,512]{1,0:T(8,128)S(1)}, f32[256,512]{1,0:T(8,128)S(1)}, u32[]{:S(2)}, u32[]{:S(2)}) collective-permute-start(f32[256,512]{1,0:T(8,128)S(1)} %get-tuple-element.28), channel_id=1, source_target_pairs={{0,2},{1,3},{2,0},{3,1},{4,6},{5,7},{6,4},{7,5},{8,10},{9,11},{10,... | collective-permute-start | bytes 1572872 | tf_op jit(solution)/shard_map/ppermute | solution.py:350

commit v4 on v3

--- a/solution.py
+++ b/solution.py
@@ -16,9 +16,9 @@
 SUB = 4
 CHIPS = 4
 BLOCK = 512
-MAIN = 416
-TAIL = 48
-GROUP = 8
+MAIN = 448
+TAIL = 32
+GROUP = 16
 BIG = 56 * 1024 * 1024
 SMALL = 24 * 1024 * 1024
 
@@ -34,19 +34,11 @@
     q = np.arange(COARSE)
     r = np.arange(LANES)
     coarse = 2.0 * np.pi * ((k[:, None] * q[None, :]) % (2 * COARSE)) / (2 * COARSE)
-    first = np.concatenate([np.cos(coarse), -np.sin(coarse)], 0)
     fine = 2.0 * np.pi * ((r[:, None] * r[None, :]) % LANES) / LANES
-    cos_f, sin_f = np.cos(fine), np.sin(fine)
-    second = np.block([[cos_f, -sin_f], [sin_f, cos_f]])
-    second_inv = np.block([[cos_f, sin_f], [-sin_f, cos_f]])
-    weight = np.where(k == 0, 1.0, 2.0)[None, :] / TOTAL
-    last = np.concatenate([weight * np.cos(coarse.T), -weight * np.sin(coarse.T)], 1)
     twist = 2.0 * np.pi * ((k[:, None] * r[None, :]) % TOTAL) / TOTAL
-    middle = 2.0 * np.pi * (COARSE * r) / TOTAL
-    edge = np.tile(np.concatenate([np.cos(middle), np.sin(middle)])[None, :], (8, 1))
+    middle = 2.0 * np.pi * np.tile((COARSE * r)[None, :], (8, 1)) / TOTAL
     rows = [
-        np.concatenate([first[:COARSE], first[COARSE:]], 1), second, second_inv, last,
-        np.concatenate([np.cos(twist), np.sin(twist)], 1), edge,
+        np.concatenate([np.cos(angle), np.sin(angle)], 1) for angle in (coarse, fine, twist, middle)
     ]
     return np.concatenate(rows, 0).astype(np.float32)
 
@@ -99,22 +91,25 @@
 def convolve_kernel(
     x_ref, table_ref, one_ref, two_ref, out_ref, edge_out, first, second, inverse, last,
 ):
-    ends = np.cumsum([0, COARSE, 2 * LANES, 2 * LANES, COARSE, COARSE, 8])
-    first_at, second_at, inverse_at, last_at, twist_at, edge_at = [
-        slice(int(p), int(q)) for p, q in zip(ends[:-1], ends[1:])
-    ]
-    re_im = table_ref[first_at, :]
+    coarse_at, fine_at, twist_at = [slice(i * COARSE, (i + 1) * COARSE) for i in range(3)]
+    edge_at = slice(3 * COARSE, 3 * COARSE + 1)
+    cos, sin = table_ref[coarse_at, :LANES], table_ref[coarse_at, LANES:]
+    lane = lax.broadcasted_iota(jnp.int32, (COARSE, COARSE), 1)
+    weight = jnp.where(lane == 0, 1.0 / TOTAL, 2.0 / TOTAL)
+    beside = lambda *parts: jnp.concatenate(parts, 1)
+    over = lambda *parts: jnp.concatenate(parts, 0)
+    fine_cos, fine_sin = table_ref[fine_at, :LANES], table_ref[fine_at, LANES:]
     for values, table, axis in (
-        (jnp.concatenate([re_im[:, :COARSE], re_im[:, COARSE:]], 0), first, 1),
-        (table_ref[second_at, :], second, 0),
-        (table_ref[inverse_at, :], inverse, 0),
-        (table_ref[last_at, :], last, 1),
+        (over(cos, -sin), first, 1),
+        (over(beside(fine_cos, -fine_sin), beside(fine_sin, fine_cos)), second, 0),
+        (over(beside(fine_cos, fine_sin), beside(-fine_sin, fine_cos)), inverse, 0),
+        (beside(weight * cos, -weight * sin), last, 1),
     ):
         high, low = split_bf16(values)
         table[...] = jnp.concatenate([high, high, low], axis)
     odd = lax.broadcasted_iota(jnp.int32, (COARSE, LANES), 0) % 2
     sign = jnp.where(odd == 0, 1.0 / TOTAL, -1.0 / TOTAL)
-    edge = table_ref[edge_at, :][:1]
+    edge = table_ref[edge_at, :]
 
     def add_pair(i, total):
         at = pl.multiple_of(i * (4 * OWN), 4 * OWN)
@@ -182,31 +177,68 @@
     )(x, jnp.asarray(tables()), *before)
 
 
-def widen_kernel(where_ref, w_ref, one_tail, two_tail, one_main, two_main):
-    quarter = one_main.shape[2]
-    main = pl.ds(0, MAIN)
-    tail = pl.ds(pl.multiple_of(MAIN + where_ref[3] * TAIL, 16), TAIL)
-    for rows, one_ref, two_ref in ((tail, one_tail, two_tail), (main, one_main, two_main)):
-        for n, refs in enumerate(((one_ref.at[0], two_ref.at[0]), (one_ref.at[1],), (two_ref.at[1],))):
-            at = pl.ds(pl.multiple_of(where_ref[n] * quarter, quarter), quarter)
-            wide = w_ref[rows, at].astype(jnp.float32)
-            for ref in refs:
-                ref[...] = wide
-
-
-def widen(w_out, where):
+def place():
+    index = lax.axis_index("chan")
+    chip, core = index // 2, index % 2
+    step = 1 - 2 * (chip % 2)
+    around = lambda n: (chip + CHIPS + n) % CHIPS
+    return chip, core, around(step), around(-step), around(2)
+
+
+def widen_kernel(tail, w_ref, one_ref, two_ref, buffer, arrived):
+    rows, quarter = buffer.shape[1:]
+    _, _, one, two, opposite = place()
+    start = pl.multiple_of(MAIN + lax.axis_index("seq") % 2 * TAIL, 16) if tail else 0
+    copies = []
+    for n, column in enumerate((opposite, one, two)):
+        at = pl.multiple_of(column * quarter, quarter)
+        copies.append(
+            pltpu.make_async_copy(
+                w_ref.at[pl.ds(start, rows), pl.ds(at, quarter)], buffer.at[n], arrived.at[n]
+            )
+        )
+        copies[n].start()
+    for n, refs in enumerate(((one_ref.at[0], two_ref.at[0]), (one_ref.at[1],), (two_ref.at[1],))):
+        copies[n].wait()
+        wide = buffer[n].astype(jnp.float32)
+        for ref in refs:
+            ref[...] = wide
+
+
+def widen(w_out, tail):
+    rows = TAIL if tail else MAIN
     quarter = w_out.shape[1] // CHIPS
-    tail = jax.ShapeDtypeStruct((2, TAIL, quarter), jnp.float32)
-    main = jax.ShapeDtypeStruct((2, MAIN, quarter), jnp.float32)
-    in_vmem = pl.BlockSpec(memory_space=pltpu.VMEM)
-    return pl.pallas_call(
-        widen_kernel,
-        in_specs=[pl.BlockSpec(memory_space=pltpu.SMEM), in_vmem],
-        out_specs=(in_vmem,) * 4,
-        out_shape=(tail, tail, main, main),
-        compiler_params=pltpu.CompilerParams(vmem_limit_bytes=SMALL),
-        cost_estimate=pl.CostEstimate(flops=0, bytes_accessed=11 << 20, transcendentals=0),
-    )(where, w_out)
+    shape = jax.ShapeDtypeStruct((2, rows, quarter), jnp.float32)
+    return pl.pallas_call(
+        functools.partial(widen_kernel, tail),
+        in_specs=[pl.BlockSpec(memory_space=pltpu.HBM)],
+        out_shape=(shape, shape),
+        scratch_shapes=[
+            pltpu.VMEM((3, rows, quarter), jnp.bfloat16),
+            pltpu.SemaphoreType.DMA((3,)),
+        ],
+        compiler_params=pltpu.CompilerParams(vmem_limit_bytes=BIG),
+        cost_estimate=pl.CostEstimate(
+            flops=0, bytes_accessed=rows * quarter * 22, transcendentals=0
+        ),
+    )(w_out)
+
+
+def after_kernel(x_ref, before_ref, out_ref):
+    pass
+
+
+def after(x, before):
+    anywhere = pl.BlockSpec(memory_space=pl.ANY)
+    return pl.pallas_call(
+        after_kernel,
+        in_specs=[anywhere, pl.BlockSpec(memory_space=pltpu.VMEM)],
+        out_specs=anywhere,
+        out_shape=jax.ShapeDtypeStruct(x.shape, x.dtype),
+        input_output_aliases={0: 0},
+        compiler_params=pltpu.CompilerParams(vmem_limit_bytes=SMALL),
+        cost_estimate=pl.CostEstimate(flops=0, bytes_accessed=4096, transcendentals=0),
+    )(x, before[0, :8, :LANES])
 
 
 def narrow_kernel(mine_ref, one_main, two_main, one_tail, two_tail, one_far, two_far, one_out, two_out):
@@ -342,10 +374,7 @@
 
 
 def shards(query, key_stream, value, long_filter, w_out):
-    index = lax.axis_index("chan")
-    chip, core = index // 2, index % 2
-    step = 1 - 2 * (chip % 2)
-    one, two, opposite = (chip + step) % CHIPS, (chip - step) % CHIPS, (chip + 2) % CHIPS
+    chip, core, one, two, opposite = place()
     size = 2 * CHIPS
     send_one = lambda x: lax.ppermute(x, "chan", [(i, i ^ 2) for i in range(size)])
     send_two = lambda x: lax.ppermute(
@@ -356,12 +385,13 @@
     sent = prepare(key_stream, value, long_filter)
     side = lax.axis_index("seq") % 2
     send_side = lambda x: lax.ppermute(x, "seq", [(i, i ^ 1) for i in range(PEERS)])
-    wide = widen(w_out, jnp.stack([opposite, one, two, side]))
-    near_one, near_two = send_one(wide[0]), send_two(wide[1])
-    main_one, main_two = send_one(wide[2]), send_two(wide[3])
+    tail_one, tail_two = widen(w_out, True)
+    near_one, near_two = send_one(tail_one), send_two(tail_two)
+    wide_one, wide_two = widen(w_out, False)
+    main_one, main_two = send_one(after(wide_one, near_one)), send_two(after(wide_two, near_two))
     far_one, far_two = send_side(near_one), send_side(near_two)
     moved = lax.all_to_all(sent, "seq", split_axis=0, concat_axis=0, tiled=True)
-    conv = convolve(moved.reshape(PEERS * 2 * SUB * OWN, LANES), far_one, far_two)
+    conv = convolve(moved.reshape(PEERS * 2 * SUB * OWN, LANES), far_one[0, :8, :LANES], far_two[0, :8, :LANES])
     home = lax.all_to_all(
         conv.reshape(PEERS, SUB * OWN, LANES), "seq", split_axis=0, concat_axis=0, tiled=True
     )

time: 142 us -> 140 us (0.986)
  local copies, waits for them, and re-layouts: 6.26 us -> 0.84 us
  Pallas kernels: 23.7 us -> 26.3 us
  starting transfers between devices: 23.6 us -> 26.2 us
  waiting for transfers between devices: 54.4 us -> 52.1 us
    all_to_all x1, waiting for transfers between devices: 2.17 us -> 16.3 us  [shards(): moved = lax.all_to_all(sent, 'seq', split_axis=0, concat_axis=0, tiled=True)]
    ppermute x2, waiting for transfers between devices: 25.2 us -> 17.2 us  [shards(): lax.ppermute(x, 'seq', [(i, i ^ 1) for i in range(PEERS)])]
    unnamed x14 -> x6, local copies, waits for them, and re-layouts: 6.26 us -> 0.83 us
    ppermute x4, waiting for transfers between devices: 8.13 us -> 3.41 us  [shards(): lax.ppermute(x, 'chan', [(i, i ^ 2) for i in range(size)])]
    ppermute x4, waiting for transfers between devices: 17.5 us -> 13.9 us  [shards(): lax.ppermute(x, 'chan', [(i, (i - 2 if i // 2 % 2 == 0 else i + 2) % size...]
    ppermute x4, starting transfers between devices: 6.98 us -> 9.88 us  [shards(): lax.ppermute(x, 'chan', [(i, (i - 2 if i // 2 % 2 == 0 else i + 2) % size...]
    pallas_call x1 -> x4, Pallas kernels: 3.77 us -> 6.53 us  [the longest x2 6.53 us: widen(): pl.pallas_call(functools.partial(widen_kernel, tail), in_specs=[pl.BlockS...]
    ppermute x4, starting transfers between devices: 3.66 us -> 1.9 us  [shards(): lax.ppermute(x, 'chan', [(i, i ^ 2) for i in range(size)])]
  transfers between devices with their start and end apart: 13 -> 13, of which waited for: 10 -> 10; matrix products, arithmetic and copies ran while one was open for 0% -> 0% of each run, Pallas kernels for 14% -> 16%
where the time goes in v4:
time: 140 us; the launch traced here: 139 us
  waiting for transfers between devices  52.1 us (37%)
  blocking collectives  33.7 us (24%)
  Pallas kernels  26.3 us (19%)
  starting transfers between devices  26.2 us (19%)
    all_to_all x1, blocking collectives, shards(): lax.all_to_all(conv.reshape(PEERS, SUB * OWN, LANES), 'seq', split_axis=0...  33.7 us
    ppermute x2, waiting for transfers between devices, shards(): lax.ppermute(x, 'seq', [(i, i ^ 1) for i in range(PEERS)])  17.2 us
    all_to_all x1, waiting for transfers between devices, shards(): moved = lax.all_to_all(sent, 'seq', split_axis=0, concat_axis=0, tiled=True)  16.3 us
    ppermute x4, waiting for transfers between devices, shards(): lax.ppermute(x, 'chan', [(i, (i - 2 if i // 2 % 2 == 0 else i + 2) % size...  13.9 us
    all_to_all x1, starting transfers between devices, shards(): moved = lax.all_to_all(sent, 'seq', split_axis=0, concat_axis=0, tiled=True)  11.7 us
    ppermute x4, starting transfers between devices, shards(): lax.ppermute(x, 'chan', [(i, (i - 2 if i // 2 % 2 == 0 else i + 2) % size...  9.88 us
    pallas_call x1, Pallas kernels, convolve(): pl.pallas_call(convolve_kernel, in_specs=[pl.BlockSpec()] * 2 + [pl.Block...  7.53 us
    pallas_call x2, Pallas kernels, widen(): pl.pallas_call(functools.partial(widen_kernel, tail), in_specs=[pl.BlockS...  6.53 us
  transfers between devices with their start and end apart: 13, of which 10 were waited for; matrix products, arithmetic and copies ran while one was open for 0% of the time, Pallas kernels for 16%

profile of v4, /device:TPU:8, one launch (start us, length us, event | category | flops | bytes accessed | tf_op | source)
XLA Modules:
  0.0 139.4 jit_solution(13834912808386446788)
XLA Ops:
  0.0 3.0 %shard_map.64 = f32[32,128,128]{2,1,0:T(8,128)} custom-call(bf16[512,512]{1,0:T(8,128)(2,1)} %key_ref.1, bf16[512,512]{1,0:T(8,128)(2,1)} %value_ref.1, f32[512,512]{1,0:T(8,128)} %taps_ref.1), custom_call_target="tpu_custom_call" | custom-call | bytes 4194304 | tf_op jit(solution)/shard_map/pallas_call | solution.py:61
  3.0 11.7 %all-to-all-start = ((f32[32,128,128]{2,1,0:T(8,128)}), f32[32,128,128]{2,1,0:T(8,128)S(1)}, u32[]{:S(2)}, u32[]{:S(2)}) async-start(f32[32,128,128]{2,1,0:T(8,128)} %shard_map.64), calls=%async_computation | async-start | bytes 4194304 | tf_op jit(solution)/shard_map/all_to_all | solution.py:393
  14.7 1.7 %shard_map.65 = (f32[2,32,1024]{2,1,0:T(8,128)}, f32[2,32,1024]{2,1,0:T(8,128)}) custom-call(bf16[512,4096]{1,0:T(8,128)(2,1)} %w_ref.5), custom_call_target="tpu_custom_call" | custom-call | bytes 720896 | tf_op jit(solution)/shard_map/pallas_call | solution.py:212
  16.4 2.8 %collective-permute-start.2 = (f32[2,32,1024]{2,1,0:T(8,128)}, f32[2,32,1024]{2,1,0:T(8,128)S(1)}, u32[]{:S(2)}, u32[]{:S(2)}) collective-permute-start(f32[2,32,1024]{2,1,0:T(8,128)} %get-tuple-element.18), channel_id=1, source_target_pairs={{0,6},{1,7},{2,4},{3,5},{4,2},{5,3},{6,0},{7,1},{8,14},{9,15},{10,... | collective-permute-start | bytes 786440 | tf_op jit(solution)/shard_map/ppermute | solution.py:380
  19.3 0.2 collective-permute-start
  19.5 4.8 %shard_map.69 = (f32[2,448,1024]{2,1,0:T(8,128)}, f32[2,448,1024]{2,1,0:T(8,128)}) custom-call(bf16[512,4096]{1,0:T(8,128)(2,1)} %w_ref.5), custom_call_target="tpu_custom_call" | custom-call | bytes 10092544 | tf_op jit(solution)/shard_map/pallas_call | solution.py:212
  24.3 1.1 collective-permute-done.2.two_tail
  25.4 2.8 %collective-permute-start.7 = (f32[2,448,1024]{2,1,0:T(8,128)}, f32[2,448,1024]{2,1,0:T(8,128)}, u32[]{:S(2)}, u32[]{:S(2)}) collective-permute-start(f32[2,448,1024]{2,1,0:T(8,128)} %shard_map.71), channel_id=1, source_target_pairs={{0,6},{1,7},{2,4},{3,5},{4,2},{5,3},{6,0},{7,1},{8,14},{9,15},{10,... | collective-permute-start | bytes 11010056 | tf_op jit(solution)/shard_map/ppermute | solution.py:380
  28.3 0.6 collective-permute-start.1
  28.9 1.5 %collective-permute-start.3 = (f32[2,32,1024]{2,1,0:T(8,128)S(1)}, f32[2,32,1024]{2,1,0:T(8,128)S(1)}, u32[]{:S(2)}, u32[]{:S(2)}) collective-permute-start(f32[2,32,1024]{2,1,0:T(8,128)S(1)} %collective-permute-done.2.two_tail), channel_id=1, source_target_pairs={{0,8},{8,0},{16,24},{24,16},{32,40},{40,32},{48,56},{56,48},{64,72... | collective-permute-start | bytes 786440 | tf_op jit(solution)/shard_map/ppermute | solution.py:387
  30.4 10.9 %collective-permute-done.1.one_far = f32[2,32,1024]{2,1,0:T(8,128)S(1)} collective-permute-done((f32[2,32,1024]{2,1,0:T(8,128)S(1)}, f32[2,32,1024]{2,1,0:T(8,128)S(1)}, u32[]{:S(2)}, u32[]{:S(2)}) %collective-permute-start.1) | collective-permute-done | bytes 262176 | tf_op jit(solution)/shard_map/ppermute | solution.py:387
  41.3 6.3 %collective-permute-done.3.two_far = f32[2,32,1024]{2,1,0:T(8,128)S(1)} collective-permute-done((f32[2,32,1024]{2,1,0:T(8,128)S(1)}, f32[2,32,1024]{2,1,0:T(8,128)S(1)}, u32[]{:S(2)}, u32[]{:S(2)}) %collective-permute-start.3) | collective-permute-done | bytes 262176 | tf_op jit(solution)/shard_map/ppermute | solution.py:387
  47.6 16.3 %all-to-all-done = f32[32,128,128]{2,1,0:T(8,128)S(1)} async-done(((f32[32,128,128]{2,1,0:T(8,128)}), f32[32,128,128]{2,1,0:T(8,128)S(1)}, u32[]{:S(2)}, u32[]{:S(2)}) %all-to-all-start) | async-done | bytes 2097184 | tf_op jit(solution)/shard_map/all_to_all | solution.py:393
  63.9 7.5 %shard_map.66 = f32[2048,128]{1,0:T(8,128)S(1)} custom-call(f32[4096,128]{1,0:T(8,128)S(1)} %bitcast.15, f32[392,256]{1,0:T(8,128)S(1)} %copy-done.2, f32[8,128]{1,0:T(8,128)S(1)} %slice_bitcast_fusion.3.one_ref, f32[8,128]{1,0:T(8,128)S(1)} %slice_bitcast_fusion.2.two_ref), custom_call_target="tpu_custom_call" | custom-call | flops 4294967296 | bytes 4194304 | tf_op jit(solution)/shard_map/pallas_call | solution.py:164
  71.5 33.7 %all_to_all.10.conv_ref = f32[32,64,128]{2,1,0:T(8,128)S(1)} all-to-all(f32[32,64,128]{2,1,0:T(8,128)S(1)} %bitcast.16), channel_id=1, replica_groups=mesh['seq'=32,'chan'=8] {'seq'}, dimensions={0} | all-to-all | bytes 2097152 | tf_op jit(solution)/shard_map/all_to_all | solution.py:395
  105.2 0.3 shard_map.67
  105.5 1.6 %collective-permute-start.4 = (f32[256,512]{1,0:T(8,128)S(1)}, f32[256,512]{1,0:T(8,128)S(1)}, u32[]{:S(2)}, u32[]{:S(2)}) collective-permute-start(f32[256,512]{1,0:T(8,128)S(1)} %get-tuple-element.19.top_ref), channel_id=1, source_target_pairs={{0,2},{1,3},{2,0},{3,1},{4,6},{5,7},{6,4},{7,5},{8,10},{9,11},{10,... | collective-permute-start | bytes 1572872 | tf_op jit(solution)/shard_map/ppermute | solution.py:379
  107.1 2.1 %collective-permute-start.5 = (f32[256,512]{1,0:T(8,128)S(1)}, f32[256,512]{1,0:T(8,128)S(1)}, u32[]{:S(2)}, u32[]{:S(2)}) collective-permute-start(f32[256,512]{1,0:T(8,128)S(1)} %get-tuple-element.20.bottom_ref), channel_id=1, source_target_pairs={{0,6},{1,7},{2,4},{3,5},{4,2},{5,3},{6,0},{7,1},{8,14},{9,15},{10,... | collective-permute-start | bytes 1572872 | tf_op jit(solution)/shard_map/ppermute | solution.py:380
  109.3 0.8 collective-permute-done.6.one_main
  110.1 3.5 %shard_map.72 = (bf16[2,512,1024]{2,1,0:T(8,128)(2,1)S(1)}, bf16[2,512,1024]{2,1,0:T(8,128)(2,1)S(1)}) custom-call(s32[1]{0:T(128)} %bitcast.8.mine_ref, f32[2,448,1024]{2,1,0:T(8,128)} %collective-permute-done.6.one_main, f32[2,448,1024]{2,1,0:T(8,128)} %collective-permute-done.7.two_main, f32[2,32,1024]{2,1,0:T(8,128)S(1)} %collective-permute-done.one_tail, ...), custom_call_target="tpu_custom_call" | custom-call | bytes 12582912 | tf_op jit(solution)/shard_map/pallas_call | solution.py:260
  113.7 0.8 copy-done
  114.5 2.6 %shard_map.68.acc_ref = f32[2,2,256,1024]{3,2,1,0:T(8,128)S(1)} custom-call(s32[4]{0:T(128)S(1)} %pad_add_fusion.where_ref, f32[256,512]{1,0:T(8,128)S(1)} %get-tuple-element.19.top_ref, f32[256,512]{1,0:T(8,128)S(1)} %get-tuple-element.20.bottom_ref, bf16[512,4096]{1,0:T(8,128)(2,1)S(1)} %copy-done), custom_call_target="tpu_custom_call" | custom-call | flops 1073741824 | bytes 8388608 | tf_op jit(solution)/shard_map/pallas_call | solution.py:304
  117.1 2.0 %collective-permute-done.4.top_ref = f32[256,512]{1,0:T(8,128)S(1)} collective-permute-done((f32[256,512]{1,0:T(8,128)S(1)}, f32[256,512]{1,0:T(8,128)S(1)}, u32[]{:S(2)}, u32[]{:S(2)}) %collective-permute-start.4) | collective-permute-done | bytes 524320 | tf_op jit(solution)/shard_map/ppermute | solution.py:379
  119.2 0.5 shard_map.75
  119.7 0.8 shard_map.74
  120.5 0.6 collective-permute-start.8
  121.0 1.3 collective-permute-done.9.b_ref
  122.5 2.2 %collective-permute-start.10 = (f32[256,512]{1,0:T(8,128)S(1)}, f32[256,512]{1,0:T(8,128)S(1)}, u32[]{:S(2)}, u32[]{:S(2)}) collective-permute-start(f32[256,512]{1,0:T(8,128)S(1)} %get-tuple-element.27), channel_id=1, source_target_pairs={{0,6},{1,7},{2,4},{3,5},{4,2},{5,3},{6,0},{7,1},{8,14},{9,15},{10,... | collective-permute-start | bytes 1572872 | tf_op jit(solution)/shard_map/ppermute | solution.py:380
  124.7 0.4 shard_map.73.a_ref
  125.1 12.6 %collective-permute-done.10.top_ref = f32[256,512]{1,0:T(8,128)S(1)} collective-permute-done((f32[256,512]{1,0:T(8,128)S(1)}, f32[256,512]{1,0:T(8,128)S(1)}, u32[]{:S(2)}, u32[]{:S(2)}) %collective-permute-start.10) | collective-permute-done | bytes 524320 | tf_op jit(solution)/shard_map/ppermute | solution.py:380
  137.7 0.6 collective-permute-done.11.bottom_ref
  138.3 1.1 shard_map.77
  (20 shorter events, 0.5 us)
Async XLA Ops:
  3.0 60.9 %all-to-all-start = ((f32[32,128,128]{2,1,0:T(8,128)}), f32[32,128,128]{2,1,0:T(8,128)S(1)}, u32[]{:S(2)}, u32[]{:S(2)}) async-start(f32[32,128,128]{2,1,0:T(8,128)} %shard_map.64), calls=%async_computation | async-start | bytes 4194304 | tf_op jit(solution)/shard_map/all_to_all | solution.py:393
  16.4 9.0 %collective-permute-start.2 = (f32[2,32,1024]{2,1,0:T(8,128)}, f32[2,32,1024]{2,1,0:T(8,128)S(1)}, u32[]{:S(2)}, u32[]{:S(2)}) collective-permute-start(f32[2,32,1024]{2,1,0:T(8,128)} %get-tuple-element.18), channel_id=1, source_target_pairs={{0,6},{1,7},{2,4},{3,5},{4,2},{5,3},{6,0},{7,1},{8,14},{9,15},{10,... | collective-permute-start | bytes 786440 | tf_op jit(solution)/shard_map/ppermute | solution.py:380
  19.3 8.9 %collective-permute-start = (f32[2,32,1024]{2,1,0:T(8,128)}, f32[2,32,1024]{2,1,0:T(8,128)S(1)}, u32[]{:S(2)}, u32[]{:S(2)}) collective-permute-start(f32[2,32,1024]{2,1,0:T(8,128)} %get-tuple-element.17), channel_id=1, source_target_pairs={{0,2},{1,3},{2,0},{3,1},{4,6},{5,7},{6,4},{7,5},{8,10},{9,11},{10,... | collective-permute-start | bytes 786440 | tf_op jit(solution)/shard_map/ppermute | solution.py:379
  25.4 83.9 %collective-permute-start.7 = (f32[2,448,1024]{2,1,0:T(8,128)}, f32[2,448,1024]{2,1,0:T(8,128)}, u32[]{:S(2)}, u32[]{:S(2)}) collective-permute-start(f32[2,448,1024]{2,1,0:T(8,128)} %shard_map.71), channel_id=1, source_target_pairs={{0,6},{1,7},{2,4},{3,5},{4,2},{5,3},{6,0},{7,1},{8,14},{9,15},{10,... | collective-permute-start | bytes 11010056 | tf_op jit(solution)/shard_map/ppermute | solution.py:380
  28.2 35.7 %copy-start.2 = (f32[392,256]{1,0:T(8,128)S(1)}, f32[392,256]{1,0:T(8,128)}, u32[]{:S(2)}) copy-start(f32[392,256]{1,0:T(8,128)} %constant.58.clone.table_ref) | copy-start | bytes 1204228
  28.2 81.9 %collective-permute-start.6 = (f32[2,448,1024]{2,1,0:T(8,128)}, f32[2,448,1024]{2,1,0:T(8,128)}, u32[]{:S(2)}, u32[]{:S(2)}) collective-permute-start(f32[2,448,1024]{2,1,0:T(8,128)} %shard_map.70), channel_id=1, source_target_pairs={{0,2},{1,3},{2,0},{3,1},{4,6},{5,7},{6,4},{7,5},{8,10},{9,11},{10,... | collective-permute-start | bytes 11010056 | tf_op jit(solution)/shard_map/ppermute | solution.py:379
  28.3 13.0 %collective-permute-start.1 = (f32[2,32,1024]{2,1,0:T(8,128)S(1)}, f32[2,32,1024]{2,1,0:T(8,128)S(1)}, u32[]{:S(2)}, u32[]{:S(2)}) collective-permute-start(f32[2,32,1024]{2,1,0:T(8,128)S(1)} %collective-permute-done.one_tail), channel_id=1, source_target_pairs={{0,8},{8,0},{16,24},{24,16},{32,40},{40,32},{48,56},{56,48},{64,72... | collective-permute-start | bytes 786440 | tf_op jit(solution)/shard_map/ppermute | solution.py:387
  28.9 18.7 %collective-permute-start.3 = (f32[2,32,1024]{2,1,0:T(8,128)S(1)}, f32[2,32,1024]{2,1,0:T(8,128)S(1)}, u32[]{:S(2)}, u32[]{:S(2)}) collective-permute-start(f32[2,32,1024]{2,1,0:T(8,128)S(1)} %collective-permute-done.2.two_tail), channel_id=1, source_target_pairs={{0,8},{8,0},{16,24},{24,16},{32,40},{40,32},{48,56},{56,48},{64,72... | collective-permute-start | bytes 786440 | tf_op jit(solution)/shard_map/ppermute | solution.py:387
  63.9 41.3 %copy-start.1 = (bf16[512,512]{1,0:T(8,128)(2,1)S(1)}, bf16[512,512]{1,0:T(8,128)(2,1)}, u32[]{:S(2)}) copy-start(bf16[512,512]{1,0:T(8,128)(2,1)} %query_ref.1) | copy-start | bytes 1572868
  105.5 13.5 %collective-permute-start.4 = (f32[256,512]{1,0:T(8,128)S(1)}, f32[256,512]{1,0:T(8,128)S(1)}, u32[]{:S(2)}, u32[]{:S(2)}) collective-permute-start(f32[256,512]{1,0:T(8,128)S(1)} %get-tuple-element.19.top_ref), channel_id=1, source_target_pairs={{0,2},{1,3},{2,0},{3,1},{4,6},{5,7},{6,4},{7,5},{8,10},{9,11},{10,... | collective-permute-start | bytes 1572872 | tf_op jit(solution)/shard_map/ppermute | solution.py:379
  107.1 12.0 %collective-permute-start.5 = (f32[256,512]{1,0:T(8,128)S(1)}, f32[256,512]{1,0:T(8,128)S(1)}, u32[]{:S(2)}, u32[]{:S(2)}) collective-permute-start(f32[256,512]{1,0:T(8,128)S(1)} %get-tuple-element.20.bottom_ref), channel_id=1, source_target_pairs={{0,6},{1,7},{2,4},{3,5},{4,2},{5,3},{6,0},{7,1},{8,14},{9,15},{10,... | collective-permute-start | bytes 1572872 | tf_op jit(solution)/shard_map/ppermute | solution.py:380
  110.1 4.4 %copy-start = (bf16[512,4096]{1,0:T(8,128)(2,1)S(1)}, bf16[512,4096]{1,0:T(8,128)(2,1)}, u32[]{:S(2)}) copy-start(bf16[512,4096]{1,0:T(8,128)(2,1)} %w_ref.5) | copy-start | bytes 12582916
  119.6 2.7 %collective-permute-start.9 = (f32[2,256,512]{2,1,0:T(8,128)S(1)}, f32[2,256,512]{2,1,0:T(8,128)S(1)}, u32[]{:S(2)}, u32[]{:S(2)}) collective-permute-start(f32[2,256,512]{2,1,0:T(8,128)S(1)} %shard_map.75), channel_id=1, source_target_pairs={{0,1},{1,0},{2,3},{3,2},{4,5},{5,4},{6,7},{7,6},{8,9},{9,8},{10,11... | collective-permute-start | bytes 3145736 | tf_op jit(solution)/shard_map/ppermute | solution.py:383
  120.5 4.6 %collective-permute-start.8 = (f32[2,256,512]{2,1,0:T(8,128)S(1)}, f32[2,256,512]{2,1,0:T(8,128)S(1)}, u32[]{:S(2)}, u32[]{:S(2)}) collective-permute-start(f32[2,256,512]{2,1,0:T(8,128)S(1)} %get-tuple-element.25), channel_id=1, source_target_pairs={{0,1},{1,0},{2,3},{3,2},{4,5},{5,4},{6,7},{7,6},{8,9},{9,8},{10,11... | collective-permute-start | bytes 3145736 | tf_op jit(solution)/shard_map/ppermute | solution.py:383
  122.5 15.3 %collective-permute-start.10 = (f32[256,512]{1,0:T(8,128)S(1)}, f32[256,512]{1,0:T(8,128)S(1)}, u32[]{:S(2)}, u32[]{:S(2)}) collective-permute-start(f32[256,512]{1,0:T(8,128)S(1)} %get-tuple-element.27), channel_id=1, source_target_pairs={{0,6},{1,7},{2,4},{3,5},{4,2},{5,3},{6,0},{7,1},{8,14},{9,15},{10,... | collective-permute-start | bytes 1572872 | tf_op jit(solution)/shard_map/ppermute | solution.py:380
  124.7 13.7 %collective-permute-start.11 = (f32[256,512]{1,0:T(8,128)S(1)}, f32[256,512]{1,0:T(8,128)S(1)}, u32[]{:S(2)}, u32[]{:S(2)}) collective-permute-start(f32[256,512]{1,0:T(8,128)S(1)} %get-tuple-element.28), channel_id=1, source_target_pairs={{0,2},{1,3},{2,0},{3,1},{4,6},{5,7},{6,4},{7,5},{8,10},{9,11},{10,... | collective-permute-start | bytes 1572872 | tf_op jit(solution)/shard_map/ppermute | solution.py:379

commit v5 on v4

v5 whole, which is shorter than its diff:
```python
import functools

import jax
import jax.numpy as jnp
import numpy as np
from jax import lax
from jax.experimental import pallas as pl
from jax.experimental.pallas import tpu as pltpu
from jax.sharding import PartitionSpec as P

LANES = 128
COARSE = 128
TOTAL = 2 * COARSE * LANES
PEERS = 32
OWN = 16
SUB = 4
CHIPS = 4
BLOCK = 512
MAIN = 448
TAIL = 32
GROUP = 16
BIG = 56 * 1024 * 1024
SMALL = 24 * 1024 * 1024


def split_bf16(x):
    high = x.astype(jnp.bfloat16)
    low = (x - high.astype(jnp.float32)).astype(jnp.bfloat16)
    return high, low


def tables():
    k = np.arange(COARSE)
    q = np.arange(COARSE)
    r = np.arange(LANES)
    coarse = 2.0 * np.pi * ((k[:, None] * q[None, :]) % (2 * COARSE)) / (2 * COARSE)
    fine = 2.0 * np.pi * ((r[:, None] * r[None, :]) % LANES) / LANES
    twist = 2.0 * np.pi * ((k[:, None] * r[None, :]) % TOTAL) / TOTAL
    middle = 2.0 * np.pi * np.tile((COARSE * r)[None, :], (8, 1)) / TOTAL
    rows = [
        np.concatenate([np.cos(angle), np.sin(angle)], 1) for angle in (coarse, fine, twist, middle)
    ]
    return np.concatenate(rows, 0).astype(np.float32)


def place():
    index = lax.axis_index("chan")
    chip, core = index // 2, index % 2
    step = (1 - 2 * (chip % 2)) * (1 - 2 * core)
    around = lambda n: (chip + CHIPS + n) % CHIPS
    return chip, core, around(step), around(-step), around(2)


def prepare_kernel(
    key_ref, value_ref, taps_ref, w_ref, out_ref, token_ref, same_ref, cross_ref, buffer, arrived
):
    rows, quarter = buffer.shape[1:]
    _, _, gather, reduce, opposite = place()
    start = pl.multiple_of(MAIN + lax.axis_index("seq") % 2 * TAIL, 16)
    copies = []
    for n, column in enumerate((opposite, gather, reduce)):
        at = pl.multiple_of(column * quarter, quarter)
        copies.append(
            pltpu.make_async_copy(
                w_ref.at[pl.ds(start, rows), pl.ds(at, quarter)], buffer.at[n], arrived.at[n]
            )
        )

    @pl.when(pl.program_id(0) == 0)
    def _():
        token_ref[...] = jnp.zeros_like(token_ref)
        for copy in copies:
            copy.start()

    signal = key_ref[...].astype(jnp.float32) * value_ref[...].astype(jnp.float32)
    taps = taps_ref[...]
    for e in range(signal.shape[0] // LANES):
        part = slice(e * LANES, (e + 1) * LANES)
        for s, stream in enumerate((signal, taps)):
            at = (2 * e + s) * OWN
            out_ref[:, at:at + OWN, :] = stream[part, :].T.reshape(PEERS, OWN, LANES)

    @pl.when(pl.program_id(0) == pl.num_programs(0) - 1)
    def _():
        for copy in copies:
            copy.wait()
        both = buffer[0].astype(jnp.float32)
        same_ref[0], cross_ref[0] = both, both
        same_ref[1] = buffer[1].astype(jnp.float32)
        cross_ref[1] = buffer[2].astype(jnp.float32)


def prepare(key_stream, value, taps, w_out):
    rows, channels = key_stream.shape
    quarter = w_out.shape[1] // CHIPS
    steps = 2
    block = pl.BlockSpec((rows // steps, channels), lambda i: (i, 0))
    sent = 2 * SUB * OWN
    tail = jax.ShapeDtypeStruct((2, TAIL, quarter), jnp.float32)
    tail_block = pl.BlockSpec((2, TAIL, quarter), lambda i: (0, 0, 0))
    return pl.pallas_call(
        prepare_kernel,
        grid=(steps,),
        in_specs=[block, block, block, pl.BlockSpec(memory_space=pltpu.HBM)],
        out_specs=(
            pl.BlockSpec((PEERS, sent // steps, LANES), lambda i: (0, i, 0)),
            pl.BlockSpec((8, LANES), lambda i: (0, 0)),
            tail_block,
            tail_block,
        ),
        out_shape=(
            jax.ShapeDtypeStruct((PEERS, sent, LANES), jnp.float32),
            jax.ShapeDtypeStruct((8, LANES), jnp.float32),
            tail,
            tail,
        ),
        scratch_shapes=[
            pltpu.VMEM((3, TAIL, quarter), jnp.bfloat16),
            pltpu.SemaphoreType.DMA((3,)),
        ],
        compiler_params=pltpu.CompilerParams(vmem_limit_bytes=BIG),
        cost_estimate=pl.CostEstimate(flops=0, bytes_accessed=5 << 20, transcendentals=0),
    )(key_stream, value, taps, w_out)


def dot(a, b):
    return jnp.dot(a, b, preferred_element_type=jnp.float32)


def rows_by(a, stacked):
    high, low = split_bf16(a)
    return dot(jnp.concatenate([high, low, high], 1), stacked)


def by_columns(stacked, a):
    high, low = split_bf16(a)
    return dot(stacked, jnp.concatenate([high, low, high], 0))


def multiply(a, b):
    ar, ai, br, bi = a[:, :LANES], a[:, LANES:], b[:, :LANES], b[:, LANES:]
    return jnp.concatenate([ar * br - ai * bi, ar * bi + ai * br], 1)


def convolve_kernel(
    x_ref, table_ref, *refs
):
    out_ref, edge_out, first, second, inverse, last = refs[-6:]
    coarse_at, fine_at, twist_at = [slice(i * COARSE, (i + 1) * COARSE) for i in range(3)]
    edge_at = slice(3 * COARSE, 3 * COARSE + 1)
    cos, sin = table_ref[coarse_at, :LANES], table_ref[coarse_at, LANES:]
    lane = lax.broadcasted_iota(jnp.int32, (COARSE, COARSE), 1)
    weight = jnp.where(lane == 0, 1.0 / TOTAL, 2.0 / TOTAL)
    beside = lambda *parts: jnp.concatenate(parts, 1)
    over = lambda *parts: jnp.concatenate(parts, 0)
    fine_cos, fine_sin = table_ref[fine_at, :LANES], table_ref[fine_at, LANES:]
    for values, table, axis in (
        (over(cos, -sin), first, 1),
        (over(beside(fine_cos, -fine_sin), beside(fine_sin, fine_cos)), second, 0),
        (over(beside(fine_cos, fine_sin), beside(-fine_sin, fine_cos)), inverse, 0),
        (beside(weight * cos, -weight * sin), last, 1),
    ):
        high, low = split_bf16(values)
        table[...] = jnp.concatenate([high, high, low], axis)
    odd = lax.broadcasted_iota(jnp.int32, (COARSE, LANES), 0) % 2
    sign = jnp.where(odd == 0, 1.0 / TOTAL, -1.0 / TOTAL)
    edge = table_ref[edge_at, :]

    half = jnp.zeros((2 * OWN, LANES), jnp.float32)
    for at in range(0, COARSE * 2 * OWN, 4 * OWN):
        half += x_ref[at:at + 2 * OWN, :] - x_ref[at + 2 * OWN:at + 4 * OWN, :]
    edge_cos, edge_sin = edge[:, :LANES], edge[:, LANES:]
    spectrum = rows_by(jnp.concatenate([half * edge_cos, -half * edge_sin], 1), second[...])
    back = rows_by(multiply(spectrum[:OWN], spectrum[OWN:]), inverse[...])
    edge_out[...] = back[:, :LANES] * edge_cos - back[:, LANES:] * edge_sin

    def some_channels(i):
        c0 = GROUP * i
        streams = [
            x_ref[pl.ds(s * OWN + c0 + j, COARSE, stride=2 * OWN), :]
            for j in range(GROUP) for s in range(2)
        ]
        y = by_columns(first[...], jnp.concatenate(streams, 1))
        cos, sin = table_ref[twist_at, :LANES], table_ref[twist_at, LANES:]
        turned = []
        for j in range(2 * GROUP):
            yr = y[:COARSE, j * LANES:(j + 1) * LANES]
            yi = y[COARSE:, j * LANES:(j + 1) * LANES]
            turned.append(jnp.concatenate([yr * cos + yi * sin, yi * cos - yr * sin], 1))
        z = rows_by(jnp.concatenate(turned, 0), second[...])
        products = [
            multiply(
                z[2 * j * COARSE:(2 * j + 1) * COARSE], z[(2 * j + 1) * COARSE:(2 * j + 2) * COARSE]
            )
            for j in range(GROUP)
        ]
        u = rows_by(jnp.concatenate(products, 0), inverse[...])
        columns = []
        for j in range(GROUP):
            ur = u[j * COARSE:(j + 1) * COARSE, :LANES]
            ui = u[j * COARSE:(j + 1) * COARSE, LANES:]
            columns.append(jnp.concatenate([ur * cos - ui * sin, ur * sin + ui * cos], 0))
        result = by_columns(last[...], jnp.concatenate(columns, 1))
        for j in range(GROUP):
            extra = sign * edge_out[pl.ds(c0 + j, 1), :]
            out_ref[pl.ds(c0 + j, COARSE, stride=OWN), :] = (
                result[:, j * LANES:(j + 1) * LANES] + extra
            )

    for i in range(OWN // GROUP):
        some_channels(i)


def convolve(x, *before):
    return pl.pallas_call(
        convolve_kernel,
        in_specs=[pl.BlockSpec()] * 2
        + [pl.BlockSpec(memory_space=pltpu.VMEM)] * len(before),
        out_shape=jax.ShapeDtypeStruct((COARSE * OWN, LANES), jnp.float32),
        scratch_shapes=[
            pltpu.VMEM((OWN, LANES), jnp.float32),
            pltpu.VMEM((2 * COARSE, 3 * COARSE), jnp.bfloat16),
            pltpu.VMEM((6 * LANES, 2 * LANES), jnp.bfloat16),
            pltpu.VMEM((6 * LANES, 2 * LANES), jnp.bfloat16),
            pltpu.VMEM((COARSE, 6 * COARSE), jnp.bfloat16),
        ],
        compiler_params=pltpu.CompilerParams(vmem_limit_bytes=SMALL),
        cost_estimate=pl.CostEstimate(flops=4 << 30, bytes_accessed=4 << 20, transcendentals=0),
    )(x, jnp.asarray(tables()), *before)


def widen_rest_kernel(
    token_ref, w_ref, same_ref, cross_ref, sibling_ref, buffer, wide, arrived, left
):
    channels, quarter = buffer.shape[1:]
    chip, _, gather, reduce, opposite = place()
    half = channels // 2
    copies = []
    for n, column in enumerate((opposite, gather, reduce, chip)):
        at = pl.multiple_of(column * quarter, quarter)
        for h in range(2):
            rows = pl.ds(h * half, half)
            copies.append(
                pltpu.make_async_copy(
                    w_ref.at[rows, pl.ds(at, quarter)], buffer.at[n, rows], arrived.at[2 * n + h]
                )
            )
            copies[-1].start()
    targets = (
        ((same_ref.at[0], MAIN), (cross_ref.at[0], MAIN)),
        ((same_ref.at[1], MAIN), (sibling_ref.at[0], channels)),
        ((cross_ref.at[1], MAIN),),
        ((sibling_ref.at[1], channels),),
    )
    sends = []
    for n, outs in enumerate(targets):
        for h in range(2):
            copies[2 * n + h].wait()
            wide[n, h * half:(h + 1) * half] = buffer[n, h * half:(h + 1) * half].astype(jnp.float32)
            for ref, end in outs:
                rows = pl.ds(h * half, min(end, (h + 1) * half) - h * half)
                sends.append(
                    pltpu.make_async_copy(wide.at[n, rows], ref.at[rows], left.at[len(sends)])
                )
                sends[-1].start()
    for copy in sends:
        copy.wait()


def widen_rest(token, w_out):
    channels, width = w_out.shape
    quarter = width // CHIPS
    shape = lambda rows: jax.ShapeDtypeStruct((2, rows, quarter), jnp.float32)
    anywhere = pl.BlockSpec(memory_space=pl.ANY)
    return pl.pallas_call(
        widen_rest_kernel,
        in_specs=[pl.BlockSpec(memory_space=pltpu.VMEM), pl.BlockSpec(memory_space=pltpu.HBM)],
        out_specs=(anywhere,) * 3,
        out_shape=(shape(MAIN), shape(MAIN), shape(channels)),
        scratch_shapes=[
            pltpu.VMEM((4, channels, quarter), jnp.bfloat16),
            pltpu.VMEM((4, channels, quarter), jnp.float32),
            pltpu.SemaphoreType.DMA((8,)),
            pltpu.SemaphoreType.DMA((12,)),
        ],
        compiler_params=pltpu.CompilerParams(vmem_limit_bytes=BIG),
        cost_estimate=pl.CostEstimate(flops=0, bytes_accessed=15 << 20, transcendentals=0),
    )(token, w_out)


def after_kernel(*refs):
    pass


def after(xs, before):
    anywhere = pl.BlockSpec(memory_space=pl.ANY)
    return pl.pallas_call(
        after_kernel,
        in_specs=[anywhere] * len(xs) + [pl.BlockSpec(memory_space=pltpu.VMEM)] * len(before),
        out_specs=(anywhere,) * len(xs),
        out_shape=tuple(jax.ShapeDtypeStruct(x.shape, x.dtype) for x in xs),
        input_output_aliases={i: i for i in range(len(xs))},
        compiler_params=pltpu.CompilerParams(vmem_limit_bytes=SMALL),
        cost_estimate=pl.CostEstimate(flops=0, bytes_accessed=4096, transcendentals=0),
    )(*xs, *before)


def narrow_tail_kernel(*refs):
    ins, outs = refs[:4], refs[4:]
    side = lax.axis_index("seq") % 2
    for near_ref, far_ref, out_ref in zip(ins[:2], ins[2:], outs):
        for ref, start in ((near_ref, side * TAIL), (far_ref, (1 - side) * TAIL)):
            out_ref[:, pl.ds(pl.multiple_of(start, 16), TAIL), :] = ref[...].astype(jnp.bfloat16)


def narrow_tail(*parts):
    _, rows, quarter = parts[0].shape
    shape = jax.ShapeDtypeStruct((2, 2 * rows, quarter), jnp.bfloat16)
    return pl.pallas_call(
        narrow_tail_kernel,
        out_shape=(shape, shape),
        compiler_params=pltpu.CompilerParams(vmem_limit_bytes=SMALL),
        cost_estimate=pl.CostEstimate(flops=0, bytes_accessed=3 << 20, transcendentals=0),
    )(*parts)


def narrow_kernel(*refs):
    out_ref = refs[-1]
    start = 0
    for ref in refs[:-1]:
        out_ref[start:start + ref.shape[0], :] = ref[...].astype(jnp.bfloat16)
        start += ref.shape[0]


def narrow(*parts):
    quarter = parts[0].shape[2]
    block = lambda rows: pl.BlockSpec((None, rows, quarter), lambda i: (i, 0, 0))
    channels = sum(part.shape[1] for part in parts)
    return pl.pallas_call(
        narrow_kernel,
        grid=(2,),
        in_specs=[block(part.shape[1]) for part in parts],
        out_specs=block(channels),
        out_shape=jax.ShapeDtypeStruct((2, channels, quarter), jnp.bfloat16),
        compiler_params=pltpu.CompilerParams(vmem_limit_bytes=SMALL),
        cost_estimate=pl.CostEstimate(flops=0, bytes_accessed=12 << 20, transcendentals=0),
    )(*parts)


def gate_kernel(conv_ref, query_ref, kept_ref, given_ref):
    _, core, *_ = place()
    half = SUB // 2
    for e in range(SUB):
        i = e % half
        at = core * half + i if e < half else (1 - core) * half + i
        conv = conv_ref[:, pl.ds(pl.multiple_of(at * OWN, OWN), OWN), :]
        conv = conv.reshape(PEERS * OWN, LANES).T
        query = query_ref[pl.ds(pl.multiple_of(at * LANES, LANES), LANES), :]
        gated = query.astype(jnp.float32) * conv
        out_ref = kept_ref if e < half else given_ref
        out_ref[i * LANES:(i + 1) * LANES, :] = gated.astype(jnp.bfloat16).astype(jnp.float32)


def gate(conv, query):
    rows, channels = query.shape
    half = jax.ShapeDtypeStruct((rows // 2, channels), jnp.float32)
    return pl.pallas_call(
        gate_kernel,
        out_shape=(half, half),
        compiler_params=pltpu.CompilerParams(vmem_limit_bytes=SMALL),
        cost_estimate=pl.CostEstimate(flops=0, bytes_accessed=3 << 20, transcendentals=0),
    )(conv, query)


def own_kernel(where_ref, mine_ref, theirs_ref, w_ref, w_other_ref, out_ref):
    mine, theirs = mine_ref[...].astype(jnp.bfloat16), theirs_ref[...].astype(jnp.bfloat16)
    out_ref[...] = dot(mine, w_ref[...]) + dot(theirs, w_other_ref[...].astype(jnp.bfloat16))


def own_part(mine, theirs, w_out, w_other, where):
    rows, channels = mine.shape
    width = w_out.shape[1]
    quarter = width // CHIPS
    return pl.pallas_call(
        own_kernel,
        grid_spec=pltpu.PrefetchScalarGridSpec(
            num_scalar_prefetch=1,
            grid=(2,),
            in_specs=[
                pl.BlockSpec((rows, channels), lambda i, where: (0, 0)),
                pl.BlockSpec((rows, channels), lambda i, where: (0, 0)),
                pl.BlockSpec((channels, quarter), lambda i, where: (0, where[i])),
                pl.BlockSpec((None, channels, quarter), lambda i, where: (i, 0, 0)),
            ],
            out_specs=pl.BlockSpec((None, rows, quarter), lambda i, where: (i, 0, 0)),
        ),
        out_shape=jax.ShapeDtypeStruct((2, rows, quarter), jnp.float32),
        compiler_params=pltpu.CompilerParams(vmem_limit_bytes=SMALL),
        cost_estimate=pl.CostEstimate(flops=1 << 30, bytes_accessed=8 << 20, transcendentals=0),
    )(where, mine, theirs, w_out, w_other)


def add_kernel(which, acc_ref, mine_ref, theirs_ref, w_ref, same_ref, cross_ref):
    _, core, *_ = place()
    mine, theirs = mine_ref[...].astype(jnp.bfloat16), theirs_ref[...].astype(jnp.bfloat16)
    for parity, out_ref in ((core, same_ref), (1 - core, cross_ref)):
        at = pl.ds(pl.multiple_of(parity * BLOCK, BLOCK), BLOCK)
        first, second = w_ref[which, :BLOCK, at], w_ref[which, BLOCK:, at]
        out_ref[...] = acc_ref[which, :, at] + (dot(mine, first) + dot(theirs, second))


def add_partner(acc, mine, theirs, w, which):
    shape = jax.ShapeDtypeStruct((mine.shape[0], BLOCK), jnp.float32)
    in_vmem = pl.BlockSpec(memory_space=pltpu.VMEM)
    return pl.pallas_call(
        functools.partial(add_kernel, which),
        in_specs=[in_vmem] * 4,
        out_specs=(in_vmem, in_vmem),
        out_shape=(shape, shape),
        compiler_params=pltpu.CompilerParams(vmem_limit_bytes=SMALL),
        cost_estimate=pl.CostEstimate(flops=1 << 29, bytes_accessed=4 << 20, transcendentals=0),
    )(acc, mine, theirs, w)


def last_kernel(kept_ref, cross_ref, other_ref, same_ref, out_ref):
    rows = kept_ref.shape[0]
    _, core, *_ = place()
    for half, a_ref, b_ref in ((core, kept_ref, same_ref), (1 - core, other_ref, cross_ref)):
        at = pl.ds(pl.multiple_of(half * rows, rows), rows)
        out_ref[at, :] = (a_ref[...] + b_ref[...]).astype(out_ref.dtype)


def last_sum(kept, cross, other, same):
    rows, columns = kept.shape
    return pl.pallas_call(
        last_kernel,
        out_shape=jax.ShapeDtypeStruct((2 * rows, columns), jnp.bfloat16),
        compiler_params=pltpu.CompilerParams(vmem_limit_bytes=SMALL),
        cost_estimate=pl.CostEstimate(flops=1 << 19, bytes_accessed=4 << 20, transcendentals=0),
    )(kept, cross, other, same)


def send(x, route):
    one = lambda chip: chip ^ 1
    two = lambda chip: (chip - 1 if chip % 2 == 0 else chip + 1) % CHIPS
    pairs = []
    for chip in range(CHIPS):
        for core in range(2):
            gather = lambda c: (one, two)[c](chip)
            reduce = lambda c: (two, one)[c](chip)
            to_chip, to_core = route(chip, core, gather, reduce)
            pairs.append((2 * chip + core, 2 * to_chip + to_core))
    return lax.ppermute(x, "chan", pairs)


def shards(query, key_stream, value, long_filter, w_out):
    send_gather = lambda x: send(x, lambda chip, core, gather, reduce: (gather(core), core))
    send_cross = lambda x: send(x, lambda chip, core, gather, reduce: (gather(1 - core), 1 - core))
    send_core = lambda x: send(x, lambda chip, core, gather, reduce: (chip, 1 - core))
    sum_same = lambda x: send(x, lambda chip, core, gather, reduce: (reduce(core), core))
    sum_cross = lambda x: send(x, lambda chip, core, gather, reduce: (reduce(core), 1 - core))
    send_side = lambda x: lax.ppermute(x, "seq", [(i, i ^ 1) for i in range(PEERS)])
    chip, core, gather, reduce, opposite = place()

    sent, token, tail_same, tail_cross = prepare(key_stream, value, long_filter, w_out)
    near_same, near_cross = send_gather(tail_same), send_cross(tail_cross)
    arrived = [x[0, :8, :LANES] for x in (near_same, near_cross)]
    main_same, main_cross, sibling = widen_rest(token, w_out)
    main_same, main_cross = after((main_same, main_cross), arrived)
    main_same, main_cross = send_gather(main_same), send_cross(main_cross)
    far_same, far_cross = send_side(near_same), send_side(near_cross)
    tails_same, tails_cross = narrow_tail(near_same, near_cross, far_same, far_cross)
    arrived = [x[0, :16, :LANES] for x in (tails_same, tails_cross)]
    w_other = send_core(sibling)
    moved = lax.all_to_all(sent, "seq", split_axis=0, concat_axis=0, tiled=True)
    conv = convolve(
        moved.reshape(PEERS * 2 * SUB * OWN, LANES),
        *arrived,
    )
    home = lax.all_to_all(
        conv.reshape(PEERS, SUB * OWN, LANES), "seq", split_axis=0, concat_axis=0, tiled=True
    )
    mine, given = gate(home, query)
    far_mine, far_theirs = send_gather(mine), send_cross(given)
    theirs = send_core(given)
    acc = own_part(mine, theirs, w_out, w_other, jnp.stack([reduce, chip]))
    w_partner = narrow(main_same, tails_same, main_cross, tails_cross)
    away_same, away_cross = add_partner(acc, far_mine, far_theirs, w_partner, 0)
    from_cross = sum_cross(away_cross)
    from_same = sum_same(away_same)
    kept, other = add_partner(acc, far_mine, far_theirs, w_partner, 1)
    return last_sum(kept, from_cross, send_core(other), from_same)


def solution(mesh):
    in_specs = (
        P("seq", "chan"),
        P("seq", "chan"),
        P("seq", "chan"),
        P("seq", "chan"),
        P("chan", None),
    )
    out_specs = P("seq", "chan")
    return jax.shard_map(shards, mesh=mesh, in_specs=in_specs, out_specs=out_specs, check_vma=False)
```

time: 140 us -> 139 us (level)
  waiting for transfers between devices: 52.1 us -> 50.3 us
    ppermute x10 -> x11, waiting for transfers between devices: 18.6 us -> 15.8 us  [send(): return lax.ppermute(x, 'chan', pairs)]
    pallas_call x9 -> x6, Pallas kernels: 11.8 us -> 11.2 us  [the longest x1 6.14 us: widen_rest(): pl.pallas_call(widen_rest_kernel, in_specs=[pl.BlockSpec(memory_space=plt...]
    ppermute x10 -> x11, starting transfers between devices: 12.4 us -> 13 us  [send(): return lax.ppermute(x, 'chan', pairs)]
  transfers between devices with their start and end apart: 13 -> 14, of which waited for: 10 -> 8; matrix products, arithmetic and copies ran while one was open for 0% -> 0% of each run, Pallas kernels for 16% -> 16%
where the time goes in v5:
time: 139 us
  waiting for transfers between devices  50.3 us (36%)
  blocking collectives  33.7 us (24%)
  starting transfers between devices  26.8 us (19%)
  Pallas kernels  26.6 us (19%)
    all_to_all x1, blocking collectives, shards(): lax.all_to_all(conv.reshape(PEERS, SUB * OWN, LANES), 'seq', split_axis=0...  33.7 us
    ppermute x2, waiting for transfers between devices, shards(): lax.ppermute(x, 'seq', [(i, i ^ 1) for i in range(PEERS)])  18.5 us
    all_to_all x1, waiting for transfers between devices, shards(): moved = lax.all_to_all(sent, 'seq', split_axis=0, concat_axis=0, tiled=True)  15.9 us
    ppermute x11, waiting for transfers between devices, send(): return lax.ppermute(x, 'chan', pairs)  15.8 us
    ppermute x11, starting transfers between devices, send(): return lax.ppermute(x, 'chan', pairs)  13 us
    all_to_all x1, starting transfers between devices, shards(): moved = lax.all_to_all(sent, 'seq', split_axis=0, concat_axis=0, tiled=True)  11.8 us
    pallas_call x1, Pallas kernels, convolve(): pl.pallas_call(convolve_kernel, in_specs=[pl.BlockSpec()] * 2 + [pl.Block...  7.24 us
    pallas_call x1, Pallas kernels, widen_rest(): pl.pallas_call(widen_rest_kernel, in_specs=[pl.BlockSpec(memory_space=plt...  6.14 us
  transfers between devices with their start and end apart: 14, of which 8 were waited for; matrix products, arithmetic and copies ran while one was open for 0% of the time, Pallas kernels for 16%

profile of v5, /device:TPU:8, one launch (start us, length us, event | category | flops | bytes accessed | tf_op | source)
XLA Modules:
  0.0 138.6 jit_solution(3705617876818502480)
XLA Ops:
  0.0 3.4 %shard_map.64 = (f32[32,128,128]{2,1,0:T(8,128)}, f32[8,128]{1,0:T(8,128)}, f32[2,32,1024]{2,1,0:T(8,128)}, f32[2,32,1024]{2,1,0:T(8,128)}) custom-call(bf16[512,512]{1,0:T(8,128)(2,1)} %key_ref.1, bf16[512,512]{1,0:T(8,128)(2,1)} %value_ref.1, f32[512,512]{1,0:T(8,128)} %taps_ref.1, bf16[512,4096]{1,0:T(8,128)(2,1)} %w_ref.5), custom_call_target="tpu_custom_call" | custom-call | bytes 5242880 | tf_op jit(solution)/shard_map/pallas_call | solution.py:101
  3.4 11.8 %all-to-all-start = ((f32[32,128,128]{2,1,0:T(8,128)}), f32[32,128,128]{2,1,0:T(8,128)S(1)}, u32[]{:S(2)}, u32[]{:S(2)}) async-start(f32[32,128,128]{2,1,0:T(8,128)} %get-tuple-element.22), calls=%async_computation | async-start | bytes 4194304 | tf_op jit(solution)/shard_map/all_to_all | solution.py:475
  15.2 1.7 %collective-permute-start.1 = (f32[2,32,1024]{2,1,0:T(8,128)S(1)}, f32[2,32,1024]{2,1,0:T(8,128)S(1)}, u32[]{:S(2)}, u32[]{:S(2)}) collective-permute-start(f32[2,32,1024]{2,1,0:T(8,128)S(1)} %copy-done.4), channel_id=1, source_target_pairs={{0,7},{1,2},{2,5},{3,0},{4,3},{5,6},{6,1},{7,4},{8,15},{9,10},{10,... | collective-permute-start | bytes 786440 | tf_op jit(solution)/shard_map/ppermute | solution.py:453
  17.0 0.2 collective-permute-start
  17.2 6.1 %shard_map.68 = (f32[2,448,1024]{2,1,0:T(8,128)}, f32[2,448,1024]{2,1,0:T(8,128)}, f32[2,512,1024]{2,1,0:T(8,128)}) custom-call(f32[8,128]{1,0:T(8,128)} %get-tuple-element.29.token_ref, bf16[512,4096]{1,0:T(8,128)(2,1)} %w_ref.5), custom_call_target="tpu_custom_call" | custom-call | bytes 15728640 | tf_op jit(solution)/shard_map/pallas_call | solution.py:275
  23.3 1.6 %collective-permute-start.5 = (f32[2,512,1024]{2,1,0:T(8,128)}, f32[2,512,1024]{2,1,0:T(8,128)}, u32[]{:S(2)}, u32[]{:S(2)}) collective-permute-start(f32[2,512,1024]{2,1,0:T(8,128)} %get-tuple-element.30), channel_id=1, source_target_pairs={{0,1},{1,0},{2,3},{3,2},{4,5},{5,4},{6,7},{7,6},{8,9},{9,8},{10,11... | collective-permute-start | bytes 12582920 | tf_op jit(solution)/shard_map/ppermute | solution.py:453
  25.0 0.7 collective-permute-start.8
  25.7 2.2 %collective-permute-start.9 = (f32[2,448,1024]{2,1,0:T(8,128)}, f32[2,448,1024]{2,1,0:T(8,128)}, u32[]{:S(2)}, u32[]{:S(2)}) collective-permute-start(f32[2,448,1024]{2,1,0:T(8,128)} %get-tuple-element.34), channel_id=1, source_target_pairs={{0,7},{1,2},{2,5},{3,0},{4,3},{5,6},{6,1},{7,4},{8,15},{9,10},{10,... | collective-permute-start | bytes 11010056 | tf_op jit(solution)/shard_map/ppermute | solution.py:453
  27.9 0.2 collective-permute-start.2
  28.2 1.8 %collective-permute-start.3 = (f32[2,32,1024]{2,1,0:T(8,128)S(1)}, f32[2,32,1024]{2,1,0:T(8,128)S(1)}, u32[]{:S(2)}, u32[]{:S(2)}) collective-permute-start(f32[2,32,1024]{2,1,0:T(8,128)S(1)} %collective-permute-done.1.refs_1_), channel_id=1, source_target_pairs={{0,8},{8,0},{16,24},{24,16},{32,40},{40,32},{48,56},{56,48},{64,72... | collective-permute-start | bytes 786440 | tf_op jit(solution)/shard_map/ppermute | solution.py:462
  30.0 11.9 %collective-permute-done.2.refs_2_ = f32[2,32,1024]{2,1,0:T(8,128)S(1)} collective-permute-done((f32[2,32,1024]{2,1,0:T(8,128)S(1)}, f32[2,32,1024]{2,1,0:T(8,128)S(1)}, u32[]{:S(2)}, u32[]{:S(2)}) %collective-permute-start.2) | collective-permute-done | bytes 262176 | tf_op jit(solution)/shard_map/ppermute | solution.py:462
  41.8 6.6 %collective-permute-done.3.refs_3_ = f32[2,32,1024]{2,1,0:T(8,128)S(1)} collective-permute-done((f32[2,32,1024]{2,1,0:T(8,128)S(1)}, f32[2,32,1024]{2,1,0:T(8,128)S(1)}, u32[]{:S(2)}, u32[]{:S(2)}) %collective-permute-start.3) | collective-permute-done | bytes 262176 | tf_op jit(solution)/shard_map/ppermute | solution.py:462
  48.6 15.9 %all-to-all-done = f32[32,128,128]{2,1,0:T(8,128)S(1)} async-done(((f32[32,128,128]{2,1,0:T(8,128)}), f32[32,128,128]{2,1,0:T(8,128)S(1)}, u32[]{:S(2)}, u32[]{:S(2)}) %all-to-all-start) | async-done | bytes 2097184 | tf_op jit(solution)/shard_map/all_to_all | solution.py:475
  64.5 7.2 %shard_map.66 = f32[2048,128]{1,0:T(8,128)S(1)} custom-call(f32[4096,128]{1,0:T(8,128)S(1)} %bitcast.12, f32[392,256]{1,0:T(8,128)S(1)} %copy-done.2, bf16[16,128]{1,0:T(8,128)(2,1)S(1)} %get-tuple-element.40.refs_0_, bf16[16,128]{1,0:T(8,128)(2,1)S(1)} %get-tuple-element.39.refs_1_), custom_call_target="tpu_custom_call" | custom-call | flops 4294967296 | bytes 4194304 | tf_op jit(solution)/shard_map/pallas_call | solution.py:215
  71.7 33.7 %all_to_all.10.conv_ref = f32[32,64,128]{2,1,0:T(8,128)S(1)} all-to-all(f32[32,64,128]{2,1,0:T(8,128)S(1)} %bitcast.13), channel_id=1, replica_groups=mesh['seq'=32,'chan'=8] {'seq'}, dimensions={0} | all-to-all | bytes 2097152 | tf_op jit(solution)/shard_map/all_to_all | solution.py:480
  105.5 0.3 shard_map.67
  105.8 0.1 collective-permute-start.4
  105.9 1.6 %collective-permute-start.6 = (f32[256,512]{1,0:T(8,128)S(1)}, f32[256,512]{1,0:T(8,128)S(1)}, u32[]{:S(2)}, u32[]{:S(2)}) collective-permute-start(f32[256,512]{1,0:T(8,128)S(1)} %get-tuple-element.27.mine_ref), channel_id=1, source_target_pairs={{0,2},{1,7},{2,0},{3,5},{4,6},{5,3},{6,4},{7,1},{8,10},{9,15},{10,... | collective-permute-start | bytes 1572872 | tf_op jit(solution)/shard_map/ppermute | solution.py:453
  107.5 0.1 collective-permute-done.8.refs_0_
  107.6 1.3 collective-permute-start.7
  109.0 3.5 %shard_map.71.w_ref = bf16[2,1024,1024]{2,1,0:T(8,128)(2,1)S(1)} custom-call(f32[2,448,1024]{2,1,0:T(8,128)} %collective-permute-done.8.refs_0_, bf16[2,64,1024]{2,1,0:T(8,128)(2,1)S(1)} %get-tuple-element.25.refs_1_, f32[2,448,1024]{2,1,0:T(8,128)} %collective-permute-done.9.refs_2_, bf16[2,64,1024]{2,1,0:T(8,128)(2,1)S(1)} %get-tuple-element.26.refs_3_), custom_call_target="tpu_custom_call" | custom-call | bytes 12582912 | tf_op jit(solution)/shard_map/pallas_call | solution.py:339
  112.6 0.8 copy-done
  113.4 3.7 %shard_map.69.acc_ref = f32[2,256,1024]{2,1,0:T(8,128)S(1)} custom-call(s32[2]{0:T(128)S(1)} %pad_add_fusion.where_ref, f32[256,512]{1,0:T(8,128)S(1)} %get-tuple-element.27.mine_ref, f32[256,512]{1,0:T(8,128)S(1)} %collective-permute-done.4.theirs_ref, bf16[512,4096]{1,0:T(8,128)(2,1)S(1)} %copy-done, f32[2,512,1024]{2,1,0:T(8,128)} %collective-permute-done.5.w_other_ref), custom_call_target="tpu_custom_call" | custom-call | flops 1073741824 | bytes 8388608 | tf_op jit(solution)/shard_map/pallas_call | solution.py:384
  117.1 2.6 %collective-permute-done.6.mine_ref = f32[256,512]{1,0:T(8,128)S(1)} collective-permute-done((f32[256,512]{1,0:T(8,128)S(1)}, f32[256,512]{1,0:T(8,128)S(1)}, u32[]{:S(2)}, u32[]{:S(2)}) %collective-permute-start.6) | collective-permute-done | bytes 524320 | tf_op jit(solution)/shard_map/ppermute | solution.py:453
  119.7 1.1 collective-permute-done.7.theirs_ref
  120.8 0.7 shard_map.73
  121.5 2.9 %collective-permute-start.10 = (f32[256,512]{1,0:T(8,128)S(1)}, f32[256,512]{1,0:T(8,128)S(1)}, u32[]{:S(2)}, u32[]{:S(2)}) collective-permute-start(f32[256,512]{1,0:T(8,128)S(1)} %get-tuple-element.36), channel_id=1, source_target_pairs={{0,7},{1,2},{2,5},{3,0},{4,3},{5,6},{6,1},{7,4},{8,15},{9,10},{10,... | collective-permute-start | bytes 1572872 | tf_op jit(solution)/shard_map/ppermute | solution.py:453
  124.4 0.5 collective-permute-start.12
  124.9 0.7 shard_map.72
  125.7 5.4 %collective-permute-done.10.cross_ref = f32[256,512]{1,0:T(8,128)S(1)} collective-permute-done((f32[256,512]{1,0:T(8,128)S(1)}, f32[256,512]{1,0:T(8,128)S(1)}, u32[]{:S(2)}, u32[]{:S(2)}) %collective-permute-start.10) | collective-permute-done | bytes 524320 | tf_op jit(solution)/shard_map/ppermute | solution.py:453
  131.1 6.5 %collective-permute-done.12.same_ref = f32[256,512]{1,0:T(8,128)S(1)} collective-permute-done((f32[256,512]{1,0:T(8,128)S(1)}, f32[256,512]{1,0:T(8,128)S(1)}, u32[]{:S(2)}, u32[]{:S(2)}) %collective-permute-start.12) | collective-permute-done | bytes 524320 | tf_op jit(solution)/shard_map/ppermute | solution.py:453
  137.7 0.9 shard_map.74
  (22 shorter events, 0.3 us)
Async XLA Ops:
  3.4 11.9 %copy-start.4 = (f32[2,32,1024]{2,1,0:T(8,128)S(1)}, f32[2,32,1024]{2,1,0:T(8,128)}, u32[]{:S(2)}) copy-start(f32[2,32,1024]{2,1,0:T(8,128)} %get-tuple-element.24) | copy-start | bytes 786436
  3.4 13.6 %copy-start.3 = (f32[2,32,1024]{2,1,0:T(8,128)S(1)}, f32[2,32,1024]{2,1,0:T(8,128)}, u32[]{:S(2)}) copy-start(f32[2,32,1024]{2,1,0:T(8,128)} %get-tuple-element.23) | copy-start | bytes 786436
  3.4 61.1 %all-to-all-start = ((f32[32,128,128]{2,1,0:T(8,128)}), f32[32,128,128]{2,1,0:T(8,128)S(1)}, u32[]{:S(2)}, u32[]{:S(2)}) async-start(f32[32,128,128]{2,1,0:T(8,128)} %get-tuple-element.22), calls=%async_computation | async-start | bytes 4194304 | tf_op jit(solution)/shard_map/all_to_all | solution.py:475
  15.2 9.7 %collective-permute-start.1 = (f32[2,32,1024]{2,1,0:T(8,128)S(1)}, f32[2,32,1024]{2,1,0:T(8,128)S(1)}, u32[]{:S(2)}, u32[]{:S(2)}) collective-permute-start(f32[2,32,1024]{2,1,0:T(8,128)S(1)} %copy-done.4), channel_id=1, source_target_pairs={{0,7},{1,2},{2,5},{3,0},{4,3},{5,6},{6,1},{7,4},{8,15},{9,10},{10,... | collective-permute-start | bytes 786440 | tf_op jit(solution)/shard_map/ppermute | solution.py:453
  17.0 8.0 %collective-permute-start = (f32[2,32,1024]{2,1,0:T(8,128)S(1)}, f32[2,32,1024]{2,1,0:T(8,128)S(1)}, u32[]{:S(2)}, u32[]{:S(2)}) collective-permute-start(f32[2,32,1024]{2,1,0:T(8,128)S(1)} %copy-done.3), channel_id=1, source_target_pairs={{0,2},{1,7},{2,0},{3,5},{4,6},{5,3},{6,4},{7,1},{8,10},{9,15},{10,... | collective-permute-start | bytes 786440 | tf_op jit(solution)/shard_map/ppermute | solution.py:453
  23.3 89.2 %collective-permute-start.5 = (f32[2,512,1024]{2,1,0:T(8,128)}, f32[2,512,1024]{2,1,0:T(8,128)}, u32[]{:S(2)}, u32[]{:S(2)}) collective-permute-start(f32[2,512,1024]{2,1,0:T(8,128)} %get-tuple-element.30), channel_id=1, source_target_pairs={{0,1},{1,0},{2,3},{3,2},{4,5},{5,4},{6,7},{7,6},{8,9},{9,8},{10,11... | collective-permute-start | bytes 12582920 | tf_op jit(solution)/shard_map/ppermute | solution.py:453
  25.0 39.5 %copy-start.2 = (f32[392,256]{1,0:T(8,128)S(1)}, f32[392,256]{1,0:T(8,128)}, u32[]{:S(2)}) copy-start(f32[392,256]{1,0:T(8,128)} %constant.45.clone.table_ref) | copy-start | bytes 1204228
  25.0 82.6 %collective-permute-start.8 = (f32[2,448,1024]{2,1,0:T(8,128)}, f32[2,448,1024]{2,1,0:T(8,128)}, u32[]{:S(2)}, u32[]{:S(2)}) collective-permute-start(f32[2,448,1024]{2,1,0:T(8,128)} %get-tuple-element.33), channel_id=1, source_target_pairs={{0,2},{1,7},{2,0},{3,5},{4,6},{5,3},{6,4},{7,1},{8,10},{9,15},{10,... | collective-permute-start | bytes 11010056 | tf_op jit(solution)/shard_map/ppermute | solution.py:453
  25.7 83.3 %collective-permute-start.9 = (f32[2,448,1024]{2,1,0:T(8,128)}, f32[2,448,1024]{2,1,0:T(8,128)}, u32[]{:S(2)}, u32[]{:S(2)}) collective-permute-start(f32[2,448,1024]{2,1,0:T(8,128)} %get-tuple-element.34), channel_id=1, source_target_pairs={{0,7},{1,2},{2,5},{3,0},{4,3},{5,6},{6,1},{7,4},{8,15},{9,10},{10,... | collective-permute-start | bytes 11010056 | tf_op jit(solution)/shard_map/ppermute | solution.py:453
  27.9 13.9 %collective-permute-start.2 = (f32[2,32,1024]{2,1,0:T(8,128)S(1)}, f32[2,32,1024]{2,1,0:T(8,128)S(1)}, u32[]{:S(2)}, u32[]{:S(2)}) collective-permute-start(f32[2,32,1024]{2,1,0:T(8,128)S(1)} %collective-permute-done.refs_0_), channel_id=1, source_target_pairs={{0,8},{8,0},{16,24},{24,16},{32,40},{40,32},{48,56},{56,48},{64,72... | collective-permute-start | bytes 786440 | tf_op jit(solution)/shard_map/ppermute | solution.py:462
  28.2 20.3 %collective-permute-start.3 = (f32[2,32,1024]{2,1,0:T(8,128)S(1)}, f32[2,32,1024]{2,1,0:T(8,128)S(1)}, u32[]{:S(2)}, u32[]{:S(2)}) collective-permute-start(f32[2,32,1024]{2,1,0:T(8,128)S(1)} %collective-permute-done.1.refs_1_), channel_id=1, source_target_pairs={{0,8},{8,0},{16,24},{24,16},{32,40},{40,32},{48,56},{56,48},{64,72... | collective-permute-start | bytes 786440 | tf_op jit(solution)/shard_map/ppermute | solution.py:462
  64.5 41.0 %copy-start.1 = (bf16[512,512]{1,0:T(8,128)(2,1)S(1)}, bf16[512,512]{1,0:T(8,128)(2,1)}, u32[]{:S(2)}) copy-start(bf16[512,512]{1,0:T(8,128)(2,1)} %query_ref.1) | copy-start | bytes 1572868
  105.8 6.8 %collective-permute-start.4 = (f32[256,512]{1,0:T(8,128)S(1)}, f32[256,512]{1,0:T(8,128)S(1)}, u32[]{:S(2)}, u32[]{:S(2)}) collective-permute-start(f32[256,512]{1,0:T(8,128)S(1)} %get-tuple-element.28), channel_id=1, source_target_pairs={{0,1},{1,0},{2,3},{3,2},{4,5},{5,4},{6,7},{7,6},{8,9},{9,8},{10,11... | collective-permute-start | bytes 1572872 | tf_op jit(solution)/shard_map/ppermute | solution.py:453
  105.9 13.8 %collective-permute-start.6 = (f32[256,512]{1,0:T(8,128)S(1)}, f32[256,512]{1,0:T(8,128)S(1)}, u32[]{:S(2)}, u32[]{:S(2)}) collective-permute-start(f32[256,512]{1,0:T(8,128)S(1)} %get-tuple-element.27.mine_ref), channel_id=1, source_target_pairs={{0,2},{1,7},{2,0},{3,5},{4,6},{5,3},{6,4},{7,1},{8,10},{9,15},{10,... | collective-permute-start | bytes 1572872 | tf_op jit(solution)/shard_map/ppermute | solution.py:453
  107.6 13.2 %collective-permute-start.7 = (f32[256,512]{1,0:T(8,128)S(1)}, f32[256,512]{1,0:T(8,128)S(1)}, u32[]{:S(2)}, u32[]{:S(2)}) collective-permute-start(f32[256,512]{1,0:T(8,128)S(1)} %get-tuple-element.28), channel_id=1, source_target_pairs={{0,7},{1,2},{2,5},{3,0},{4,3},{5,6},{6,1},{7,4},{8,15},{9,10},{10,... | collective-permute-start | bytes 1572872 | tf_op jit(solution)/shard_map/ppermute | solution.py:453
  109.0 4.4 %copy-start = (bf16[512,4096]{1,0:T(8,128)(2,1)S(1)}, bf16[512,4096]{1,0:T(8,128)(2,1)}, u32[]{:S(2)}) copy-start(bf16[512,4096]{1,0:T(8,128)(2,1)} %w_ref.5) | copy-start | bytes 12582916
  121.5 9.6 %collective-permute-start.10 = (f32[256,512]{1,0:T(8,128)S(1)}, f32[256,512]{1,0:T(8,128)S(1)}, u32[]{:S(2)}, u32[]{:S(2)}) collective-permute-start(f32[256,512]{1,0:T(8,128)S(1)} %get-tuple-element.36), channel_id=1, source_target_pairs={{0,7},{1,2},{2,5},{3,0},{4,3},{5,6},{6,1},{7,4},{8,15},{9,10},{10,... | collective-permute-start | bytes 1572872 | tf_op jit(solution)/shard_map/ppermute | solution.py:453
  124.4 13.2 %collective-permute-start.12 = (f32[256,512]{1,0:T(8,128)S(1)}, f32[256,512]{1,0:T(8,128)S(1)}, u32[]{:S(2)}, u32[]{:S(2)}) collective-permute-start(f32[256,512]{1,0:T(8,128)S(1)} %get-tuple-element.38), channel_id=1, source_target_pairs={{0,6},{1,3},{2,4},{3,1},{4,2},{5,7},{6,0},{7,5},{8,14},{9,11},{10,... | collective-permute-start | bytes 1572872 | tf_op jit(solution)/shard_map/ppermute | solution.py:453
  125.6 12.1 %collective-permute-start.11 = (f32[256,512]{1,0:T(8,128)S(1)}, f32[256,512]{1,0:T(8,128)S(1)}, u32[]{:S(2)}, u32[]{:S(2)}) collective-permute-start(f32[256,512]{1,0:T(8,128)S(1)} %get-tuple-element.37), channel_id=1, source_target_pairs={{0,1},{1,0},{2,3},{3,2},{4,5},{5,4},{6,7},{7,6},{8,9},{9,8},{10,11... | collective-permute-start | bytes 1572872 | tf_op jit(solution)/shard_map/ppermute | solution.py:453

commit v6 on v5

--- a/solution.py
+++ b/solution.py
@@ -80,7 +80,7 @@
             at = (2 * e + s) * OWN
             out_ref[:, at:at + OWN, :] = stream[part, :].T.reshape(PEERS, OWN, LANES)
 
-    @pl.when(pl.program_id(0) == pl.num_programs(0) - 1)
+    @pl.when(pl.program_id(0) == 0)
     def _():
         for copy in copies:
             copy.wait()

time: 139 us -> 139 us (level)
  no operation moved by 1% of the time
where the time goes in v6:
time: 139 us
  waiting for transfers between devices  50.3 us (36%)
  blocking collectives  33.7 us (24%)
  Pallas kernels  27.1 us (19%)
  starting transfers between devices  26.8 us (19%)
    all_to_all x1, blocking collectives, shards(): lax.all_to_all(conv.reshape(PEERS, SUB * OWN, LANES), 'seq', split_axis=0...  33.7 us
    ppermute x2, waiting for transfers between devices, shards(): lax.ppermute(x, 'seq', [(i, i ^ 1) for i in range(PEERS)])  18.5 us
    all_to_all x1, waiting for transfers between devices, shards(): moved = lax.all_to_all(sent, 'seq', split_axis=0, concat_axis=0, tiled=True)  15.9 us
    ppermute x11, waiting for transfers between devices, send(): return lax.ppermute(x, 'chan', pairs)  15.8 us
    ppermute x11, starting transfers between devices, send(): return lax.ppermute(x, 'chan', pairs)  13 us
    all_to_all x1, starting transfers between devices, shards(): moved = lax.all_to_all(sent, 'seq', split_axis=0, concat_axis=0, tiled=True)  11.8 us
    pallas_call x1, Pallas kernels, convolve(): pl.pallas_call(convolve_kernel, in_specs=[pl.BlockSpec()] * 2 + [pl.Block...  7.24 us
    pallas_call x1, Pallas kernels, widen_rest(): pl.pallas_call(widen_rest_kernel, in_specs=[pl.BlockSpec(memory_space=plt...  6.14 us
  transfers between devices with their start and end apart: 14, of which 8 were waited for; matrix products, arithmetic and copies ran while one was open for 0% of the time, Pallas kernels for 16%

profile of v6, /device:TPU:8, one launch (start us, length us, event | category | flops | bytes accessed | tf_op | source)
XLA Modules:
  0.0 139.0 jit_solution(14477088259395573119)
XLA Ops:
  0.0 3.8 %shard_map.64 = (f32[32,128,128]{2,1,0:T(8,128)}, f32[8,128]{1,0:T(8,128)}, f32[2,32,1024]{2,1,0:T(8,128)}, f32[2,32,1024]{2,1,0:T(8,128)}) custom-call(bf16[512,512]{1,0:T(8,128)(2,1)} %key_ref.1, bf16[512,512]{1,0:T(8,128)(2,1)} %value_ref.1, f32[512,512]{1,0:T(8,128)} %taps_ref.1, bf16[512,4096]{1,0:T(8,128)(2,1)} %w_ref.5), custom_call_target="tpu_custom_call" | custom-call | bytes 5242880 | tf_op jit(solution)/shard_map/pallas_call | solution.py:101
  3.8 11.8 %all-to-all-start = ((f32[32,128,128]{2,1,0:T(8,128)}), f32[32,128,128]{2,1,0:T(8,128)S(1)}, u32[]{:S(2)}, u32[]{:S(2)}) async-start(f32[32,128,128]{2,1,0:T(8,128)} %get-tuple-element.22), calls=%async_computation | async-start | bytes 4194304 | tf_op jit(solution)/shard_map/all_to_all | solution.py:475
  15.7 1.7 %collective-permute-start.1 = (f32[2,32,1024]{2,1,0:T(8,128)S(1)}, f32[2,32,1024]{2,1,0:T(8,128)S(1)}, u32[]{:S(2)}, u32[]{:S(2)}) collective-permute-start(f32[2,32,1024]{2,1,0:T(8,128)S(1)} %copy-done.4), channel_id=1, source_target_pairs={{0,7},{1,2},{2,5},{3,0},{4,3},{5,6},{6,1},{7,4},{8,15},{9,10},{10,... | collective-permute-start | bytes 786440 | tf_op jit(solution)/shard_map/ppermute | solution.py:453
  17.4 0.2 collective-permute-start
  17.6 6.1 %shard_map.68 = (f32[2,448,1024]{2,1,0:T(8,128)}, f32[2,448,1024]{2,1,0:T(8,128)}, f32[2,512,1024]{2,1,0:T(8,128)}) custom-call(f32[8,128]{1,0:T(8,128)} %get-tuple-element.29.token_ref, bf16[512,4096]{1,0:T(8,128)(2,1)} %w_ref.5), custom_call_target="tpu_custom_call" | custom-call | bytes 15728640 | tf_op jit(solution)/shard_map/pallas_call | solution.py:275
  23.8 1.6 %collective-permute-start.5 = (f32[2,512,1024]{2,1,0:T(8,128)}, f32[2,512,1024]{2,1,0:T(8,128)}, u32[]{:S(2)}, u32[]{:S(2)}) collective-permute-start(f32[2,512,1024]{2,1,0:T(8,128)} %get-tuple-element.30), channel_id=1, source_target_pairs={{0,1},{1,0},{2,3},{3,2},{4,5},{5,4},{6,7},{7,6},{8,9},{9,8},{10,11... | collective-permute-start | bytes 12582920 | tf_op jit(solution)/shard_map/ppermute | solution.py:453
  25.4 0.7 collective-permute-start.8
  26.1 2.2 %collective-permute-start.9 = (f32[2,448,1024]{2,1,0:T(8,128)}, f32[2,448,1024]{2,1,0:T(8,128)}, u32[]{:S(2)}, u32[]{:S(2)}) collective-permute-start(f32[2,448,1024]{2,1,0:T(8,128)} %get-tuple-element.34), channel_id=1, source_target_pairs={{0,7},{1,2},{2,5},{3,0},{4,3},{5,6},{6,1},{7,4},{8,15},{9,10},{10,... | collective-permute-start | bytes 11010056 | tf_op jit(solution)/shard_map/ppermute | solution.py:453
  28.3 0.2 collective-permute-start.2
  28.6 1.8 %collective-permute-start.3 = (f32[2,32,1024]{2,1,0:T(8,128)S(1)}, f32[2,32,1024]{2,1,0:T(8,128)S(1)}, u32[]{:S(2)}, u32[]{:S(2)}) collective-permute-start(f32[2,32,1024]{2,1,0:T(8,128)S(1)} %collective-permute-done.1.refs_1_), channel_id=1, source_target_pairs={{0,8},{8,0},{16,24},{24,16},{32,40},{40,32},{48,56},{56,48},{64,72... | collective-permute-start | bytes 786440 | tf_op jit(solution)/shard_map/ppermute | solution.py:462
  30.4 11.9 %collective-permute-done.2.refs_2_ = f32[2,32,1024]{2,1,0:T(8,128)S(1)} collective-permute-done((f32[2,32,1024]{2,1,0:T(8,128)S(1)}, f32[2,32,1024]{2,1,0:T(8,128)S(1)}, u32[]{:S(2)}, u32[]{:S(2)}) %collective-permute-start.2) | collective-permute-done | bytes 262176 | tf_op jit(solution)/shard_map/ppermute | solution.py:462
  42.3 6.6 %collective-permute-done.3.refs_3_ = f32[2,32,1024]{2,1,0:T(8,128)S(1)} collective-permute-done((f32[2,32,1024]{2,1,0:T(8,128)S(1)}, f32[2,32,1024]{2,1,0:T(8,128)S(1)}, u32[]{:S(2)}, u32[]{:S(2)}) %collective-permute-start.3) | collective-permute-done | bytes 262176 | tf_op jit(solution)/shard_map/ppermute | solution.py:462
  49.0 15.9 %all-to-all-done = f32[32,128,128]{2,1,0:T(8,128)S(1)} async-done(((f32[32,128,128]{2,1,0:T(8,128)}), f32[32,128,128]{2,1,0:T(8,128)S(1)}, u32[]{:S(2)}, u32[]{:S(2)}) %all-to-all-start) | async-done | bytes 2097184 | tf_op jit(solution)/shard_map/all_to_all | solution.py:475
  64.9 7.2 %shard_map.66 = f32[2048,128]{1,0:T(8,128)S(1)} custom-call(f32[4096,128]{1,0:T(8,128)S(1)} %bitcast.12, f32[392,256]{1,0:T(8,128)S(1)} %copy-done.2, bf16[16,128]{1,0:T(8,128)(2,1)S(1)} %get-tuple-element.40.refs_0_, bf16[16,128]{1,0:T(8,128)(2,1)S(1)} %get-tuple-element.39.refs_1_), custom_call_target="tpu_custom_call" | custom-call | flops 4294967296 | bytes 4194304 | tf_op jit(solution)/shard_map/pallas_call | solution.py:215
  72.1 33.7 %all_to_all.10.conv_ref = f32[32,64,128]{2,1,0:T(8,128)S(1)} all-to-all(f32[32,64,128]{2,1,0:T(8,128)S(1)} %bitcast.13), channel_id=1, replica_groups=mesh['seq'=32,'chan'=8] {'seq'}, dimensions={0} | all-to-all | bytes 2097152 | tf_op jit(solution)/shard_map/all_to_all | solution.py:480
  105.9 0.3 shard_map.67
  106.2 0.1 collective-permute-start.4
  106.3 1.6 %collective-permute-start.6 = (f32[256,512]{1,0:T(8,128)S(1)}, f32[256,512]{1,0:T(8,128)S(1)}, u32[]{:S(2)}, u32[]{:S(2)}) collective-permute-start(f32[256,512]{1,0:T(8,128)S(1)} %get-tuple-element.27.mine_ref), channel_id=1, source_target_pairs={{0,2},{1,7},{2,0},{3,5},{4,6},{5,3},{6,4},{7,1},{8,10},{9,15},{10,... | collective-permute-start | bytes 1572872 | tf_op jit(solution)/shard_map/ppermute | solution.py:453
  107.9 0.1 collective-permute-done.8.refs_0_
  108.0 1.3 collective-permute-start.7
  109.5 3.5 %shard_map.71.w_ref = bf16[2,1024,1024]{2,1,0:T(8,128)(2,1)S(1)} custom-call(f32[2,448,1024]{2,1,0:T(8,128)} %collective-permute-done.8.refs_0_, bf16[2,64,1024]{2,1,0:T(8,128)(2,1)S(1)} %get-tuple-element.25.refs_1_, f32[2,448,1024]{2,1,0:T(8,128)} %collective-permute-done.9.refs_2_, bf16[2,64,1024]{2,1,0:T(8,128)(2,1)S(1)} %get-tuple-element.26.refs_3_), custom_call_target="tpu_custom_call" | custom-call | bytes 12582912 | tf_op jit(solution)/shard_map/pallas_call | solution.py:339
  113.0 0.8 copy-done
  113.8 3.7 %shard_map.69.acc_ref = f32[2,256,1024]{2,1,0:T(8,128)S(1)} custom-call(s32[2]{0:T(128)S(1)} %pad_add_fusion.where_ref, f32[256,512]{1,0:T(8,128)S(1)} %get-tuple-element.27.mine_ref, f32[256,512]{1,0:T(8,128)S(1)} %collective-permute-done.4.theirs_ref, bf16[512,4096]{1,0:T(8,128)(2,1)S(1)} %copy-done, f32[2,512,1024]{2,1,0:T(8,128)} %collective-permute-done.5.w_other_ref), custom_call_target="tpu_custom_call" | custom-call | flops 1073741824 | bytes 8388608 | tf_op jit(solution)/shard_map/pallas_call | solution.py:384
  117.5 2.6 %collective-permute-done.6.mine_ref = f32[256,512]{1,0:T(8,128)S(1)} collective-permute-done((f32[256,512]{1,0:T(8,128)S(1)}, f32[256,512]{1,0:T(8,128)S(1)}, u32[]{:S(2)}, u32[]{:S(2)}) %collective-permute-start.6) | collective-permute-done | bytes 524320 | tf_op jit(solution)/shard_map/ppermute | solution.py:453
  120.1 1.1 collective-permute-done.7.theirs_ref
  121.2 0.7 shard_map.73
  121.9 2.9 %collective-permute-start.10 = (f32[256,512]{1,0:T(8,128)S(1)}, f32[256,512]{1,0:T(8,128)S(1)}, u32[]{:S(2)}, u32[]{:S(2)}) collective-permute-start(f32[256,512]{1,0:T(8,128)S(1)} %get-tuple-element.36), channel_id=1, source_target_pairs={{0,7},{1,2},{2,5},{3,0},{4,3},{5,6},{6,1},{7,4},{8,15},{9,10},{10,... | collective-permute-start | bytes 1572872 | tf_op jit(solution)/shard_map/ppermute | solution.py:453
  124.8 0.5 collective-permute-start.12
  125.3 0.7 shard_map.72
  126.1 5.4 %collective-permute-done.10.cross_ref = f32[256,512]{1,0:T(8,128)S(1)} collective-permute-done((f32[256,512]{1,0:T(8,128)S(1)}, f32[256,512]{1,0:T(8,128)S(1)}, u32[]{:S(2)}, u32[]{:S(2)}) %collective-permute-start.10) | collective-permute-done | bytes 524320 | tf_op jit(solution)/shard_map/ppermute | solution.py:453
  131.5 6.6 %collective-permute-done.12.same_ref = f32[256,512]{1,0:T(8,128)S(1)} collective-permute-done((f32[256,512]{1,0:T(8,128)S(1)}, f32[256,512]{1,0:T(8,128)S(1)}, u32[]{:S(2)}, u32[]{:S(2)}) %collective-permute-start.12) | collective-permute-done | bytes 524320 | tf_op jit(solution)/shard_map/ppermute | solution.py:453
  138.1 0.9 shard_map.74
  (22 shorter events, 0.3 us)
Async XLA Ops:
  3.8 11.9 %copy-start.4 = (f32[2,32,1024]{2,1,0:T(8,128)S(1)}, f32[2,32,1024]{2,1,0:T(8,128)}, u32[]{:S(2)}) copy-start(f32[2,32,1024]{2,1,0:T(8,128)} %get-tuple-element.24) | copy-start | bytes 786436
  3.8 13.6 %copy-start.3 = (f32[2,32,1024]{2,1,0:T(8,128)S(1)}, f32[2,32,1024]{2,1,0:T(8,128)}, u32[]{:S(2)}) copy-start(f32[2,32,1024]{2,1,0:T(8,128)} %get-tuple-element.23) | copy-start | bytes 786436
  3.8 61.1 %all-to-all-start = ((f32[32,128,128]{2,1,0:T(8,128)}), f32[32,128,128]{2,1,0:T(8,128)S(1)}, u32[]{:S(2)}, u32[]{:S(2)}) async-start(f32[32,128,128]{2,1,0:T(8,128)} %get-tuple-element.22), calls=%async_computation | async-start | bytes 4194304 | tf_op jit(solution)/shard_map/all_to_all | solution.py:475
  15.7 9.7 %collective-permute-start.1 = (f32[2,32,1024]{2,1,0:T(8,128)S(1)}, f32[2,32,1024]{2,1,0:T(8,128)S(1)}, u32[]{:S(2)}, u32[]{:S(2)}) collective-permute-start(f32[2,32,1024]{2,1,0:T(8,128)S(1)} %copy-done.4), channel_id=1, source_target_pairs={{0,7},{1,2},{2,5},{3,0},{4,3},{5,6},{6,1},{7,4},{8,15},{9,10},{10,... | collective-permute-start | bytes 786440 | tf_op jit(solution)/shard_map/ppermute | solution.py:453
  17.4 8.0 %collective-permute-start = (f32[2,32,1024]{2,1,0:T(8,128)S(1)}, f32[2,32,1024]{2,1,0:T(8,128)S(1)}, u32[]{:S(2)}, u32[]{:S(2)}) collective-permute-start(f32[2,32,1024]{2,1,0:T(8,128)S(1)} %copy-done.3), channel_id=1, source_target_pairs={{0,2},{1,7},{2,0},{3,5},{4,6},{5,3},{6,4},{7,1},{8,10},{9,15},{10,... | collective-permute-start | bytes 786440 | tf_op jit(solution)/shard_map/ppermute | solution.py:453
  23.8 89.2 %collective-permute-start.5 = (f32[2,512,1024]{2,1,0:T(8,128)}, f32[2,512,1024]{2,1,0:T(8,128)}, u32[]{:S(2)}, u32[]{:S(2)}) collective-permute-start(f32[2,512,1024]{2,1,0:T(8,128)} %get-tuple-element.30), channel_id=1, source_target_pairs={{0,1},{1,0},{2,3},{3,2},{4,5},{5,4},{6,7},{7,6},{8,9},{9,8},{10,11... | collective-permute-start | bytes 12582920 | tf_op jit(solution)/shard_map/ppermute | solution.py:453
  25.4 39.5 %copy-start.2 = (f32[392,256]{1,0:T(8,128)S(1)}, f32[392,256]{1,0:T(8,128)}, u32[]{:S(2)}) copy-start(f32[392,256]{1,0:T(8,128)} %constant.45.clone.table_ref) | copy-start | bytes 1204228
  25.4 82.6 %collective-permute-start.8 = (f32[2,448,1024]{2,1,0:T(8,128)}, f32[2,448,1024]{2,1,0:T(8,128)}, u32[]{:S(2)}, u32[]{:S(2)}) collective-permute-start(f32[2,448,1024]{2,1,0:T(8,128)} %get-tuple-element.33), channel_id=1, source_target_pairs={{0,2},{1,7},{2,0},{3,5},{4,6},{5,3},{6,4},{7,1},{8,10},{9,15},{10,... | collective-permute-start | bytes 11010056 | tf_op jit(solution)/shard_map/ppermute | solution.py:453
  26.1 83.3 %collective-permute-start.9 = (f32[2,448,1024]{2,1,0:T(8,128)}, f32[2,448,1024]{2,1,0:T(8,128)}, u32[]{:S(2)}, u32[]{:S(2)}) collective-permute-start(f32[2,448,1024]{2,1,0:T(8,128)} %get-tuple-element.34), channel_id=1, source_target_pairs={{0,7},{1,2},{2,5},{3,0},{4,3},{5,6},{6,1},{7,4},{8,15},{9,10},{10,... | collective-permute-start | bytes 11010056 | tf_op jit(solution)/shard_map/ppermute | solution.py:453
  28.3 13.9 %collective-permute-start.2 = (f32[2,32,1024]{2,1,0:T(8,128)S(1)}, f32[2,32,1024]{2,1,0:T(8,128)S(1)}, u32[]{:S(2)}, u32[]{:S(2)}) collective-permute-start(f32[2,32,1024]{2,1,0:T(8,128)S(1)} %collective-permute-done.refs_0_), channel_id=1, source_target_pairs={{0,8},{8,0},{16,24},{24,16},{32,40},{40,32},{48,56},{56,48},{64,72... | collective-permute-start | bytes 786440 | tf_op jit(solution)/shard_map/ppermute | solution.py:462
  28.6 20.3 %collective-permute-start.3 = (f32[2,32,1024]{2,1,0:T(8,128)S(1)}, f32[2,32,1024]{2,1,0:T(8,128)S(1)}, u32[]{:S(2)}, u32[]{:S(2)}) collective-permute-start(f32[2,32,1024]{2,1,0:T(8,128)S(1)} %collective-permute-done.1.refs_1_), channel_id=1, source_target_pairs={{0,8},{8,0},{16,24},{24,16},{32,40},{40,32},{48,56},{56,48},{64,72... | collective-permute-start | bytes 786440 | tf_op jit(solution)/shard_map/ppermute | solution.py:462
  64.9 41.0 %copy-start.1 = (bf16[512,512]{1,0:T(8,128)(2,1)S(1)}, bf16[512,512]{1,0:T(8,128)(2,1)}, u32[]{:S(2)}) copy-start(bf16[512,512]{1,0:T(8,128)(2,1)} %query_ref.1) | copy-start | bytes 1572868
  106.2 6.8 %collective-permute-start.4 = (f32[256,512]{1,0:T(8,128)S(1)}, f32[256,512]{1,0:T(8,128)S(1)}, u32[]{:S(2)}, u32[]{:S(2)}) collective-permute-start(f32[256,512]{1,0:T(8,128)S(1)} %get-tuple-element.28), channel_id=1, source_target_pairs={{0,1},{1,0},{2,3},{3,2},{4,5},{5,4},{6,7},{7,6},{8,9},{9,8},{10,11... | collective-permute-start | bytes 1572872 | tf_op jit(solution)/shard_map/ppermute | solution.py:453
  106.3 13.8 %collective-permute-start.6 = (f32[256,512]{1,0:T(8,128)S(1)}, f32[256,512]{1,0:T(8,128)S(1)}, u32[]{:S(2)}, u32[]{:S(2)}) collective-permute-start(f32[256,512]{1,0:T(8,128)S(1)} %get-tuple-element.27.mine_ref), channel_id=1, source_target_pairs={{0,2},{1,7},{2,0},{3,5},{4,6},{5,3},{6,4},{7,1},{8,10},{9,15},{10,... | collective-permute-start | bytes 1572872 | tf_op jit(solution)/shard_map/ppermute | solution.py:453
  108.0 13.2 %collective-permute-start.7 = (f32[256,512]{1,0:T(8,128)S(1)}, f32[256,512]{1,0:T(8,128)S(1)}, u32[]{:S(2)}, u32[]{:S(2)}) collective-permute-start(f32[256,512]{1,0:T(8,128)S(1)} %get-tuple-element.28), channel_id=1, source_target_pairs={{0,7},{1,2},{2,5},{3,0},{4,3},{5,6},{6,1},{7,4},{8,15},{9,10},{10,... | collective-permute-start | bytes 1572872 | tf_op jit(solution)/shard_map/ppermute | solution.py:453
  109.5 4.4 %copy-start = (bf16[512,4096]{1,0:T(8,128)(2,1)S(1)}, bf16[512,4096]{1,0:T(8,128)(2,1)}, u32[]{:S(2)}) copy-start(bf16[512,4096]{1,0:T(8,128)(2,1)} %w_ref.5) | copy-start | bytes 12582916
  121.9 9.6 %collective-permute-start.10 = (f32[256,512]{1,0:T(8,128)S(1)}, f32[256,512]{1,0:T(8,128)S(1)}, u32[]{:S(2)}, u32[]{:S(2)}) collective-permute-start(f32[256,512]{1,0:T(8,128)S(1)} %get-tuple-element.36), channel_id=1, source_target_pairs={{0,7},{1,2},{2,5},{3,0},{4,3},{5,6},{6,1},{7,4},{8,15},{9,10},{10,... | collective-permute-start | bytes 1572872 | tf_op jit(solution)/shard_map/ppermute | solution.py:453
  124.8 13.3 %collective-permute-start.12 = (f32[256,512]{1,0:T(8,128)S(1)}, f32[256,512]{1,0:T(8,128)S(1)}, u32[]{:S(2)}, u32[]{:S(2)}) collective-permute-start(f32[256,512]{1,0:T(8,128)S(1)} %get-tuple-element.38), channel_id=1, source_target_pairs={{0,6},{1,3},{2,4},{3,1},{4,2},{5,7},{6,0},{7,5},{8,14},{9,11},{10,... | collective-permute-start | bytes 1572872 | tf_op jit(solution)/shard_map/ppermute | solution.py:453
  126.0 12.1 %collective-permute-start.11 = (f32[256,512]{1,0:T(8,128)S(1)}, f32[256,512]{1,0:T(8,128)S(1)}, u32[]{:S(2)}, u32[]{:S(2)}) collective-permute-start(f32[256,512]{1,0:T(8,128)S(1)} %get-tuple-element.37), channel_id=1, source_target_pairs={{0,1},{1,0},{2,3},{3,2},{4,5},{5,4},{6,7},{7,6},{8,9},{9,8},{10,11... | collective-permute-start | bytes 1572872 | tf_op jit(solution)/shard_map/ppermute | solution.py:453
